TPU v7x, 512 devices: a whole 4x8x8 slice. The times are simulated.
512 devices in a mesh: section: 16 (over z, core), tensor: 16 (over y_lo, x), dp: 2 (over y_hi).
Axes of the slice: x: 4, y: 8 (y_hi: 2, y_lo: 4; y = y_hi * 4 + y_lo), z: 8, core: 2. Of those that a mesh axis runs over, the one named last changes fastest.
Arguments:
- enc_hidden: bfloat16 [512, 2048], P(('dp', 'tensor'), 'section'), parts along dimension 0, may hold values from -70 to 70
- mlp_gain: float32 [2048], P('section'), may hold values from 0.25 to 1.75
- final_gain: float32 [2048], P('section'), may hold values from 0.25 to 1.75
- w_gate: bfloat16 [2048, 8192], P('section', 'tensor'), may hold values from -0.125 to 0.125
- w_up: bfloat16 [2048, 8192], P('section', 'tensor'), may hold values from -0.125 to 0.125
- w_down: bfloat16 [8192, 2048], P('tensor', 'section'), may hold values from -0.0625 to 0.0625
- key_weight: bfloat16 [16, 2048, 4096], P('section', None, 'tensor'), may hold values from -0.125 to 0.125
- value_weight: bfloat16 [16, 2048, 4096], P('section', None, 'tensor'), may hold values from -0.125 to 0.125
- queries: bfloat16 [16, 2048, 4096], P('section', 'dp', 'tensor'), parts along dimension 1, may hold values from -340 to 340
- context_grad: bfloat16 [16, 2048, 4096], P('section', 'dp', 'tensor'), parts along dimension 1, may hold values from -6 to 6
Outputs:
- query_grad: bfloat16 [16, 2048, 4096], P('section', 'dp', 'tensor'), parts along dimension 1
- hidden_grad: float32 [512, 2048], P(('dp', 'tensor'), 'section'), parts along dimension 0
- gate_weight_grad: bfloat16 [4096, 8192], P(('dp', 'section'), 'tensor'), parts along dimension 0
- up_weight_grad: bfloat16 [4096, 8192], P(('dp', 'section'), 'tensor'), parts along dimension 0
- down_weight_grad: bfloat16 [16384, 2048], P(('dp', 'tensor'), 'section'), parts along dimension 0
There are 2 independent parts, one for each index of `dp`. A program takes and returns all parts, laid end to end along the dimension named above; an argument that names none is the same for every part. Nothing has to cross between parts.
All inputs are finite; a program needn't handle non-finite values.
Results may differ from a plain program's by a relative error of at most 0.017.
Values may be sent and summed in bfloat16 or wider, within the bound.
No kernel may reach another device: no remote copies, remote signals or barrier semaphores. Data moves between devices by JAX's collectives and lax.ppermute only.
A program may use at most 64 MiB of HBM per device.

v0:
```python
import jax
import jax.numpy as jnp
from jax import lax
from jax.sharding import PartitionSpec as P

D = 2048
HEAD = 256


EPSILON = 1e-06


def sent_to_all(value, axis):
    copies = jnp.broadcast_to(value, (lax.axis_size(axis), *value.shape))
    return lax.all_to_all(copies, axis, split_axis=0, concat_axis=0, tiled=True)


def of_everyone(value, axis):
    everything = sent_to_all(value, axis)
    return jnp.sum(everything, axis=0)


def in_order(pieces, dim):
    dims = list(pieces.shape[1:])
    dims[dim] *= pieces.shape[0]
    return jnp.moveaxis(pieces, 0, dim).reshape(dims)


def collect(value, axis, dim):
    return in_order(sent_to_all(value, axis), dim)


def in_blocks(value, dim, size):
    before, after = (value.shape[:dim], value.shape[dim + 1 :])
    return jnp.moveaxis(value.reshape(*before, size, -1, *after), dim, 0)


def summed_on_arrival(value, axis, dim):
    pieces = in_blocks(value, dim, lax.axis_size(axis))
    arrived = lax.all_to_all(pieces, axis, split_axis=0, concat_axis=0, tiled=True)
    return arrived.sum(axis=0)


def side_by_side(arrays, axis, dim, along):
    ends, at = ([], 0)
    for a in arrays[:-1]:
        at += a.shape[along]
        ends.append(at)
    both = jnp.concatenate(arrays, axis=along)
    return tuple(jnp.split(lax.all_gather(both, axis, axis=dim, tiled=True), ends, axis=along))


def attend(query_block, grad_block, keys, values):
    scale_factor = HEAD ** (-0.5)
    tgt_rows = query_block.shape[0]
    src_rows = keys.shape[0]
    heads_here = query_block.shape[1] // HEAD
    query_heads = query_block.reshape(tgt_rows, heads_here, HEAD)
    key_heads = keys.reshape(src_rows, heads_here, HEAD)
    value_heads = values.reshape(src_rows, heads_here, HEAD)
    grad_heads = grad_block.reshape(tgt_rows, heads_here, HEAD)
    scores = (
        jnp.einsum("qhd,khd->hqk", query_heads, key_heads, preferred_element_type=jnp.float32)
        * scale_factor
    )
    probs = jax.nn.softmax(scores, axis=-1)
    probs_bf = probs.astype(jnp.bfloat16)
    context = jnp.einsum("hqk,khd->qhd", probs_bf, value_heads, preferred_element_type=jnp.float32)
    delta = jnp.sum(grad_heads.astype(jnp.float32) * context, axis=2)
    dprob = jnp.einsum("qhd,khd->hqk", grad_heads, value_heads, preferred_element_type=jnp.float32)
    dscore = (probs * (dprob - jnp.transpose(delta)[:, :, None]) * scale_factor).astype(
        jnp.bfloat16
    )
    query_grad = jnp.einsum(
        "hqk,khd->qhd", dscore, key_heads, preferred_element_type=jnp.float32
    ).astype(jnp.bfloat16)
    key_grad = jnp.einsum(
        "hqk,qhd->khd", dscore, query_heads, preferred_element_type=jnp.float32
    ).astype(jnp.bfloat16)
    value_grad = jnp.einsum(
        "hqk,qhd->khd", probs_bf, grad_heads, preferred_element_type=jnp.float32
    ).astype(jnp.bfloat16)
    width = heads_here * HEAD
    return (
        query_grad.reshape(tgt_rows, width),
        key_grad.reshape(src_rows, width),
        value_grad.reshape(src_rows, width),
    )


def on_device(
    enc_hidden,
    mlp_gain,
    final_gain,
    w_gate,
    w_up,
    w_down,
    key_weight,
    value_weight,
    queries,
    context_grad,
):
    rows_contract = (((0,), (0,)), ((), ()))
    cols_contract = (((1,), (1,)), ((), ()))
    hidden_wide = enc_hidden.astype(jnp.float32)
    square_in = of_everyone(jnp.sum(hidden_wide * hidden_wide, axis=1), "section")
    inv_in = lax.rsqrt(square_in / D + EPSILON)[:, None]
    normed = (hidden_wide * inv_in * mlp_gain[None, :]).astype(jnp.bfloat16)
    normed_all = collect(normed, "tensor", 0)
    picked = normed_all
    gate_part = jnp.dot(picked, w_gate, preferred_element_type=jnp.float32)
    up_part = jnp.dot(picked, w_up, preferred_element_type=jnp.float32)
    gate_up = summed_on_arrival(jnp.concatenate([gate_part, up_part], axis=1), "section", 0)
    hidden_width = w_gate.shape[1]
    gate_pre = gate_up[:, :hidden_width]
    up_pre = gate_up[:, hidden_width:]
    sigmoid_gate = jax.nn.sigmoid(gate_pre)
    activated = gate_pre * sigmoid_gate
    hidden_act = (activated * up_pre).astype(jnp.bfloat16)
    hidden_all = collect(hidden_act, "section", 0)
    picked = hidden_all
    mixed = summed_on_arrival(
        jnp.dot(picked, w_down, preferred_element_type=jnp.float32), "tensor", 0
    )
    outer = hidden_wide + mixed
    square_out = of_everyone(jnp.sum(outer * outer, axis=1), "section")
    inv_out = lax.rsqrt(square_out / D + EPSILON)[:, None]
    encoded = (outer * inv_out * final_gain[None, :]).astype(jnp.bfloat16)
    key_matrix = key_weight[0]
    value_matrix = value_weight[0]
    head_width = key_matrix.shape[1]
    encoded_feat = lax.all_gather(encoded, "section", axis=1, tiled=True)
    block_rows = collect(encoded_feat, "tensor", 0)
    key_part = jnp.dot(block_rows, key_matrix, preferred_element_type=jnp.float32)
    value_part = jnp.dot(block_rows, value_matrix, preferred_element_type=jnp.float32)
    joined = jnp.concatenate([key_part, value_part], axis=1)
    keys_wide = joined[:, :head_width]
    values_wide = joined[:, head_width:]
    keys = keys_wide.astype(jnp.bfloat16)
    values = values_wide.astype(jnp.bfloat16)
    query_grad, key_grad, value_grad = attend(queries[0], context_grad[0], keys, values)
    total = lax.dot_general(key_grad, key_matrix, cols_contract, preferred_element_type=jnp.float32)
    partial_rows = summed_on_arrival(
        total
        + lax.dot_general(
            value_grad, value_matrix, cols_contract, preferred_element_type=jnp.float32
        ),
        "tensor",
        0,
    )
    encoded_grad = summed_on_arrival(partial_rows, "section", 1)
    scaled_out = final_gain[None, :] * encoded_grad
    inner_out = of_everyone(jnp.sum(scaled_out * outer, axis=1), "section")
    outer_grad = (
        inv_out * scaled_out - outer * inv_out * inv_out * inv_out * (inner_out / D)[:, None]
    )
    outer_grad_bf = outer_grad.astype(jnp.bfloat16)
    outer_all = collect(outer_grad_bf, "tensor", 0)
    down_weight_grad = lax.dot_general(
        hidden_all, outer_all, rows_contract, preferred_element_type=jnp.float32
    ).astype(jnp.bfloat16)
    picked = outer_all
    act_grad = summed_on_arrival(
        lax.dot_general(picked, w_down, cols_contract, preferred_element_type=jnp.float32),
        "section",
        0,
    )
    up_grad = (act_grad * activated).astype(jnp.bfloat16)
    gate_grad = (act_grad * up_pre * sigmoid_gate * (1.0 + gate_pre * (1.0 - sigmoid_gate))).astype(
        jnp.bfloat16
    )
    gate_all, up_all = side_by_side((gate_grad, up_grad), "section", 0, 1)
    gate_weight_grad = lax.dot_general(
        normed_all, gate_all, rows_contract, preferred_element_type=jnp.float32
    ).astype(jnp.bfloat16)
    up_weight_grad = lax.dot_general(
        normed_all, up_all, rows_contract, preferred_element_type=jnp.float32
    ).astype(jnp.bfloat16)
    total = lax.dot_general(gate_all, w_gate, cols_contract, preferred_element_type=jnp.float32)
    normed_grad = summed_on_arrival(
        total + lax.dot_general(up_all, w_up, cols_contract, preferred_element_type=jnp.float32),
        "tensor",
        0,
    )
    scaled_in = mlp_gain[None, :] * normed_grad
    inner_in = of_everyone(jnp.sum(scaled_in * hidden_wide, axis=1), "section")
    hidden_grad = (
        outer_grad
        + inv_in * scaled_in
        - hidden_wide * inv_in * inv_in * inv_in * (inner_in / D)[:, None]
    )
    return (query_grad[None, :, :], hidden_grad, gate_weight_grad, up_weight_grad, down_weight_grad)


def solution(mesh):
    in_specs = (
        P(("dp", "tensor"), "section"),
        P("section"),
        P("section"),
        P("section", "tensor"),
        P("section", "tensor"),
        P("tensor", "section"),
        P("section", None, "tensor"),
        P("section", None, "tensor"),
        P("section", "dp", "tensor"),
        P("section", "dp", "tensor"),
    )
    out_specs = (
        P("section", "dp", "tensor"),
        P(("dp", "tensor"), "section"),
        P(("dp", "section"), "tensor"),
        P(("dp", "section"), "tensor"),
        P(("dp", "tensor"), "section"),
    )
    return jax.shard_map(
        on_device, mesh=mesh, in_specs=in_specs, out_specs=out_specs, check_vma=False
    )
```

profile of v0, /device:TPU:1, one launch (start us, length us, event | category | flops | bytes accessed | tf_op | source)
XLA Modules:
  0.0 323.9 jit_solution(14428593524110861365)
XLA Ops:
  0.6 0.9 fusion.37
  1.5 18.6 %all_to_all.74 = f32[16,1,16]{2,1,0:T(1,128)S(1)} all-to-all(f32[16,1,16]{2,1,0:T(1,128)S(1)} %broadcast_in_dim.16), channel_id=1, replica_groups=mesh['section'=16,'tensor'=16,'dp'=2] {'section'}, dimensions={0} | all-to-all | bytes 2048 | tf_op jit(solution)/shard_map/all_to_all | solution.py:15
  20.2 0.5 copy-done.19
  20.7 0.8 fusion.33
  21.5 14.2 %all_to_all.75 = bf16[16,16,128]{2,1,0:T(8,128)(2,1)S(1)} all-to-all(bf16[16,16,128]{2,1,0:T(8,128)(2,1)S(1)} %broadcast_in_dim.17), channel_id=1, replica_groups=mesh['section'=16,'tensor'=16,'dp'=2] {'tensor'}, dimensions={0} | all-to-all | bytes 131072 | tf_op jit(solution)/shard_map/all_to_all | solution.py:15
  35.7 1.1 fusion.45
  36.8 1.1 fusion.44
  38.1 33.2 %all_to_all.76 = f32[16,16,1024]{2,1,0:T(8,128)S(1)} all-to-all(f32[16,16,1024]{2,1,0:T(8,128)S(1)} %bitcast.86), channel_id=1, replica_groups=mesh['section'=16,'tensor'=16,'dp'=2] {'section'}, dimensions={0} | all-to-all | bytes 2097152 | tf_op jit(solution)/shard_map/all_to_all | solution.py:40
  71.4 14.4 %all_to_all.77 = bf16[16,16,512]{2,1,0:T(8,128)(2,1)S(1)} all-to-all(bf16[16,16,512]{2,1,0:T(8,128)(2,1)S(1)} %broadcast_in_dim.36), channel_id=1, replica_groups=mesh['section'=16,'tensor'=16,'dp'=2] {'section'}, dimensions={0} | all-to-all | bytes 524288 | tf_op jit(solution)/shard_map/all_to_all | solution.py:15
  85.8 0.7 copy-done.5
  86.6 0.2 fusion.28
  86.8 11.7 %all_to_all.78 = f32[16,16,128]{2,1,0:T(8,128)S(1)} all-to-all(f32[16,16,128]{2,1,0:T(8,128)S(1)} %fusion.28), channel_id=1, replica_groups=mesh['section'=16,'tensor'=16,'dp'=2] {'tensor'}, dimensions={0} | all-to-all | bytes 262144 | tf_op jit(solution)/shard_map/all_to_all | solution.py:40
  98.6 9.9 %all_to_all.79 = f32[16,1,16]{2,1,0:T(1,128)S(1)} all-to-all(f32[16,1,16]{2,1,0:T(1,128)S(1)} %broadcast_in_dim.37), channel_id=1, replica_groups=mesh['section'=16,'tensor'=16,'dp'=2] {'section'}, dimensions={0} | all-to-all | bytes 2048 | tf_op jit(solution)/shard_map/all_to_all | solution.py:15
  108.6 15.3 %all_gather.6 = bf16[16,2048]{1,0:T(8,128)(2,1)S(1)} all-gather(bf16[16,128]{1,0:T(8,128)(2,1)S(1)} %multiply_convert_fusion.3), channel_id=1, replica_groups=mesh['section'=16,'tensor'=16,'dp'=2] {'section'}, dimensions={1}, use_global_device_ids=true | all-gather | bytes 69632 | tf_op jit(solution)/shard_map/all_gather | solution.py:132
  124.0 1.1 broadcast_in_dim.38
  125.1 3.7 %all-to-all-start.6 = ((bf16[16,16,2048]{2,1,0:T(8,128)(2,1)}), bf16[16,16,2048]{2,1,0:T(8,128)(2,1)S(1)}, u32[]{:S(2)}, u32[]{:S(2)}) async-start(bf16[16,16,2048]{2,1,0:T(8,128)(2,1)} %broadcast_in_dim.38), calls=%async_computation.6 | async-start | bytes 2097152 | tf_op jit(solution)/shard_map/all_to_all | solution.py:15
  128.7 2.0 copy.27
  130.8 21.3 %all-to-all-done.6 = bf16[16,16,2048]{2,1,0:T(8,128)(2,1)S(1)} async-done(((bf16[16,16,2048]{2,1,0:T(8,128)(2,1)}), bf16[16,16,2048]{2,1,0:T(8,128)(2,1)S(1)}, u32[]{:S(2)}, u32[]{:S(2)}) %all-to-all-start.6) | async-done | bytes 1048608 | tf_op jit(solution)/shard_map/all_to_all | solution.py:15
  152.1 0.4 convolution_convert_fusion.5
  152.6 0.4 convolution_convert_fusion.6
  153.2 0.3 fusion.43
  153.7 0.4 fusion.4
  154.3 0.5 copy-done.3
  154.7 1.2 fusion.3
  155.9 3.5 %fusion.7 = f32[256,2048]{1,0:T(8,128)} fusion(bf16[256,1024]{1,0:T(8,128)(2,1)} %fusion.3, bf16[1,2048,256]{2,1,0:T(8,128)(2,1)S(1)} %copy-done, bf16[1,1024,256]{2,1,0:T(8,128)(2,1)} %param.18), kind=kOutput, calls=%fused_computation.20 | convolution fusion | flops 402718720 | bytes 4194304 | tf_op jit(solution)/shard_map/dot_general | solution.py:142
  159.4 4.0 %convolution_add_fusion = f32[256,2048]{1,0:T(8,128)} fusion(f32[256,2048]{1,0:T(8,128)} %fusion.7, bf16[1,2048,256]{2,1,0:T(8,128)(2,1)S(1)} %copy-done.1, bf16[1,1024,256]{2,1,0:T(8,128)(2,1)} %param.19, f32[1024]{0:T(1024)S(1)} %copy-done.13, f32[256,1024]{1,0:T(8,128)S(1)} %get-tuple-element.33, f32[1024]{0:T(1024)S(1)} %get-tuple-element.32), kind=kOutput, calls=%fused_computation | convolution fusion | flops 404029440 | bytes 6823936 | tf_op jit(solution)/shard_map/dot_general | solution.py:145
  163.4 54.4 %all_to_all.80 = f32[16,16,2048]{2,1,0:T(8,128)S(1)} all-to-all(f32[16,16,2048]{2,1,0:T(8,128)} %bitcast.85), channel_id=1, replica_groups=mesh['section'=16,'tensor'=16,'dp'=2] {'tensor'}, dimensions={0} | all-to-all | bytes 4194304 | tf_op jit(solution)/shard_map/all_to_all | solution.py:40
  218.0 15.9 %all_to_all.81 = f32[16,16,128]{2,1,0:T(8,128)S(1)} all-to-all(f32[16,16,128]{2,1,0:T(8,128)S(1)} %copy.28), channel_id=1, replica_groups=mesh['section'=16,'tensor'=16,'dp'=2] {'section'}, dimensions={0} | all-to-all | bytes 262144 | tf_op jit(solution)/shard_map/all_to_all | solution.py:40
  234.1 9.4 %all_to_all.82 = f32[16,1,16]{2,1,0:T(1,128)S(1)} all-to-all(f32[16,1,16]{2,1,0:T(1,128)S(1)} %broadcast_in_dim.39), channel_id=1, replica_groups=mesh['section'=16,'tensor'=16,'dp'=2] {'section'}, dimensions={0} | all-to-all | bytes 2048 | tf_op jit(solution)/shard_map/all_to_all | solution.py:15
  243.6 0.7 fusion.39
  244.3 11.2 %all_to_all.83 = bf16[16,16,128]{2,1,0:T(8,128)(2,1)S(1)} all-to-all(bf16[16,16,128]{2,1,0:T(8,128)(2,1)S(1)} %broadcast_in_dim.40), channel_id=1, replica_groups=mesh['section'=16,'tensor'=16,'dp'=2] {'tensor'}, dimensions={0} | all-to-all | bytes 131072 | tf_op jit(solution)/shard_map/all_to_all | solution.py:15
  255.5 1.9 fusion.26
  257.4 5.6 %all-to-all-start.11 = ((f32[16,16,512]{2,1,0:T(8,128)}), f32[16,16,512]{2,1,0:T(8,128)S(1)}, u32[]{:S(2)}, u32[]{:S(2)}) async-start(f32[16,16,512]{2,1,0:T(8,128)} %fusion.26), calls=%async_computation.11 | async-start | bytes 1048576 | tf_op jit(solution)/shard_map/all_to_all | solution.py:40
  263.0 0.3 fusion.5
  263.4 1.0 copy.31
  264.4 16.0 %all-to-all-done.11 = f32[16,16,512]{2,1,0:T(8,128)S(1)} async-done(((f32[16,16,512]{2,1,0:T(8,128)}), f32[16,16,512]{2,1,0:T(8,128)S(1)}, u32[]{:S(2)}, u32[]{:S(2)}) %all-to-all-start.11) | async-done | bytes 524320 | tf_op jit(solution)/shard_map/all_to_all | solution.py:40
  280.4 15.9 %all_gather.7 = bf16[256,1024]{1,0:T(8,128)(2,1)S(1)} all-gather(bf16[16,1024]{1,0:T(8,128)(2,1)S(1)} %pad_maximum_fusion.1), channel_id=1, replica_groups=mesh['section'=16,'tensor'=16,'dp'=2] {'section'}, dimensions={0}, use_global_device_ids=true | all-gather | bytes 557056 | tf_op jit(solution)/shard_map/all_gather | solution.py:50
  296.4 0.2 fusion.24
  296.6 0.9 convolution_add_fusion.1
  297.5 3.5 %all-to-all-start.12 = ((f32[16,16,128]{2,1,0:T(8,128)}), f32[16,16,128]{2,1,0:T(8,128)S(1)}, u32[]{:S(2)}, u32[]{:S(2)}) async-start(f32[16,16,128]{2,1,0:T(8,128)} %bitcast.19), calls=%async_computation.12 | async-start | bytes 262144 | tf_op jit(solution)/shard_map/all_to_all | solution.py:40
  301.0 0.9 fusion.6
  301.9 0.9 convolution_convert_fusion.4
  302.8 6.4 %all-to-all-done.12 = f32[16,16,128]{2,1,0:T(8,128)S(1)} async-done(((f32[16,16,128]{2,1,0:T(8,128)}), f32[16,16,128]{2,1,0:T(8,128)S(1)}, u32[]{:S(2)}, u32[]{:S(2)}) %all-to-all-start.12) | async-done | bytes 131104 | tf_op jit(solution)/shard_map/all_to_all | solution.py:40
  309.4 0.6 broadcast_in_dim.41
  310.0 6.2 %all-to-all-start.13 = ((f32[16,1,16]{2,1,0:T(1,128)}), f32[16,1,16]{2,1,0:T(1,128)S(1)}, u32[]{:S(2)}, u32[]{:S(2)}) async-start(f32[16,1,16]{2,1,0:T(1,128)} %broadcast_in_dim.41), calls=%async_computation.13 | async-start | bytes 16384 | tf_op jit(solution)/shard_map/all_to_all | solution.py:15
  316.2 0.9 convolution_convert_fusion.3
  317.1 6.1 %all-to-all-done.13 = f32[16,1,16]{2,1,0:T(1,128)S(1)} async-done(((f32[16,1,16]{2,1,0:T(1,128)}), f32[16,1,16]{2,1,0:T(1,128)S(1)}, u32[]{:S(2)}, u32[]{:S(2)}) %all-to-all-start.13) | async-done | bytes 1056 | tf_op jit(solution)/shard_map/all_to_all | solution.py:15
  323.2 0.7 fusion.36
  (70 shorter events, 1.7 us)
Async XLA Ops:
  0.6 151.9 %copy-start = (bf16[1,2048,256]{2,1,0:T(8,128)(2,1)S(1)}, bf16[1,2048,256]{2,1,0:T(8,128)(2,1)}, u32[]{:S(2)}) copy-start(bf16[1,2048,256]{2,1,0:T(8,128)(2,1)} %param.16) | copy-start | bytes 3145732
  20.2 0.5 copy-start.19
  38.0 48.5 %copy-start.9 = (bf16[512,128]{1,0:T(8,128)(2,1)S(1)}, bf16[512,128]{1,0:T(8,128)(2,1)}, u32[]{:S(2)}) copy-start(bf16[512,128]{1,0:T(8,128)(2,1)} %param.15) | copy-start | bytes 393220
  38.0 60.5 %copy-start.11 = (bf16[16,128]{1,0:T(8,128)(2,1)S(1)}, bf16[16,128]{1,0:T(8,128)(2,1)}, u32[]{:S(2)}) copy-start(bf16[16,128]{1,0:T(8,128)(2,1)} %param.10) | copy-start | bytes 12292
  38.1 70.5 %copy-start.14 = (f32[128]{0:T(128)S(1)}, f32[128]{0:T(128)}, u32[]{:S(2)}) copy-start(f32[128]{0:T(128)} %param.12) | copy-start | bytes 1540
  85.8 0.7 copy-start.5
  108.5 22.2 %copy-start.16 = (f32[16]{0:T(128)}, f32[16]{0:T(128)S(1)}, u32[]{:S(2)}) copy-start(f32[16]{0:T(128)S(1)} %add_rsqrt_fusion) | copy-start | bytes 196
  123.9 28.2 %copy-start.1 = (bf16[1,2048,256]{2,1,0:T(8,128)(2,1)S(1)}, bf16[1,2048,256]{2,1,0:T(8,128)(2,1)}, u32[]{:S(2)}) copy-start(bf16[1,2048,256]{2,1,0:T(8,128)(2,1)} %param.17) | copy-start | bytes 3145732
  125.1 27.1 %all-to-all-start.6 = ((bf16[16,16,2048]{2,1,0:T(8,128)(2,1)}), bf16[16,16,2048]{2,1,0:T(8,128)(2,1)S(1)}, u32[]{:S(2)}, u32[]{:S(2)}) async-start(bf16[16,16,2048]{2,1,0:T(8,128)(2,1)} %broadcast_in_dim.38), calls=%async_computation.6 | async-start | bytes 2097152 | tf_op jit(solution)/shard_map/all_to_all | solution.py:15
  152.1 1.0 copy-start.2
  152.6 1.1 copy-start.7
  153.7 0.6 copy-start.12
  153.7 1.0 copy-start.3
  155.9 3.5 %copy-start.13 = (f32[1024]{0:T(1024)S(1)}, f32[1024]{0:T(1024)}, u32[]{:S(2)}) copy-start(f32[1024]{0:T(1024)} %copy-done.12) | copy-start | bytes 12292
  217.8 16.2 %copy-start.15 = (f32[128]{0:T(128)S(1)}, f32[128]{0:T(128)}, u32[]{:S(2)}) copy-start(f32[128]{0:T(128)} %param.12) | copy-start | bytes 1540
  217.9 45.1 %copy-start.4 = (bf16[256,1024]{1,0:T(8,128)(2,1)S(1)}, bf16[256,1024]{1,0:T(8,128)(2,1)}, u32[]{:S(2)}) copy-start(bf16[256,1024]{1,0:T(8,128)(2,1)} %fusion.3) | copy-start | bytes 1572868
  257.4 38.9 %copy-start.10 = (bf16[128,512]{1,0:T(8,128)(2,1)S(1)}, bf16[128,512]{1,0:T(8,128)(2,1)}, u32[]{:S(2)}) copy-start(bf16[128,512]{1,0:T(8,128)(2,1)} %param.13) | copy-start | bytes 393220
  257.4 22.9 %all-to-all-start.11 = ((f32[16,16,512]{2,1,0:T(8,128)}), f32[16,16,512]{2,1,0:T(8,128)S(1)}, u32[]{:S(2)}, u32[]{:S(2)}) async-start(f32[16,16,512]{2,1,0:T(8,128)} %fusion.26), calls=%async_computation.11 | async-start | bytes 1048576 | tf_op jit(solution)/shard_map/all_to_all | solution.py:40
  263.0 33.6 %copy-start.8 = (bf16[128,512]{1,0:T(8,128)(2,1)S(1)}, bf16[128,512]{1,0:T(8,128)(2,1)}, u32[]{:S(2)}) copy-start(bf16[128,512]{1,0:T(8,128)(2,1)} %param.14) | copy-start | bytes 393220
  263.3 37.7 %copy-start.6 = (bf16[16,16,512]{2,1,0:T(8,128)(2,1)S(1)}, bf16[16,16,512]{2,1,0:T(8,128)(2,1)}, u32[]{:S(2)}) copy-start(bf16[16,16,512]{2,1,0:T(8,128)(2,1)} %copy-done.5) | copy-start | bytes 786436
  280.4 28.8 %copy-start.18 = (f32[128]{0:T(128)S(1)}, f32[128]{0:T(128)}, u32[]{:S(2)}) copy-start(f32[128]{0:T(128)} %param.11) | copy-start | bytes 1540
  296.4 26.8 %copy-start.17 = (f32[16]{0:T(128)S(1)}, f32[16]{0:T(128)}, u32[]{:S(2)}) copy-start(f32[16]{0:T(128)} %copy-done.16) | copy-start | bytes 196
  296.4 26.8 %copy-start.20 = (f32[16]{0:T(128)S(1)}, f32[16]{0:T(128)}, u32[]{:S(2)}) copy-start(f32[16]{0:T(128)} %copy-done.19) | copy-start | bytes 196
  297.5 11.7 %all-to-all-start.12 = ((f32[16,16,128]{2,1,0:T(8,128)}), f32[16,16,128]{2,1,0:T(8,128)S(1)}, u32[]{:S(2)}, u32[]{:S(2)}) async-start(f32[16,16,128]{2,1,0:T(8,128)} %bitcast.19), calls=%async_computation.12 | async-start | bytes 262144 | tf_op jit(solution)/shard_map/all_to_all | solution.py:40
  310.0 13.2 %all-to-all-start.13 = ((f32[16,1,16]{2,1,0:T(1,128)}), f32[16,1,16]{2,1,0:T(1,128)S(1)}, u32[]{:S(2)}, u32[]{:S(2)}) async-start(f32[16,1,16]{2,1,0:T(1,128)} %broadcast_in_dim.41), calls=%async_computation.13 | async-start | bytes 16384 | tf_op jit(solution)/shard_map/all_to_all | solution.py:15
where the time goes:
time: 325 us; the launch traced here: 324 us
  blocking collectives  224 us (69%)
  waiting for transfers between devices  49.8 us (15%)
  starting transfers between devices  19 us (6%)
  matrix products  18.7 us (6%)
  local copies, waits for them, and re-layouts  7 us (2%)
  other arithmetic  4.11 us (1%)
    all_to_all x4, blocking collectives, summed_on_arrival(): lax.all_to_all(pieces, axis, split_axis=0, concat_axis=0, tiled=True)  115 us
    all_to_all x6, blocking collectives, sent_to_all(): return lax.all_to_all(copies, axis, split_axis=0, concat_axis=0, tiled=True)  77.8 us
    all_to_all x2, waiting for transfers between devices, sent_to_all(): return lax.all_to_all(copies, axis, split_axis=0, concat_axis=0, tiled=True)  27.4 us
    all_to_all x2, waiting for transfers between devices, summed_on_arrival(): lax.all_to_all(pieces, axis, split_axis=0, concat_axis=0, tiled=True)  22.4 us
    all_gather x1, blocking collectives, side_by_side(): lax.all_gather(both, axis, axis=dim, tiled=True)  15.9 us
    all_gather x1, blocking collectives, on_device(): encoded_feat = lax.all_gather(encoded, 'section', axis=1, tiled=True)  15.3 us
    all_to_all x2, starting transfers between devices, sent_to_all(): return lax.all_to_all(copies, axis, split_axis=0, concat_axis=0, tiled=True)  9.87 us
    all_to_all x2, starting transfers between devices, summed_on_arrival(): lax.all_to_all(pieces, axis, split_axis=0, concat_axis=0, tiled=True)  9.09 us
  transfers between devices with their start and end apart: 4, of which 4 were waited for; matrix products, arithmetic and copies ran while one was open for 2% of the time, Pallas kernels for 0%

commit v1 on v0

v1 whole, which is shorter than its diff:
```python
import jax
import jax.numpy as jnp
from jax import lax
from jax.experimental import pallas as pl
from jax.experimental.pallas import tpu as pltpu
from jax.sharding import Mesh
from jax.sharding import PartitionSpec as P

D = 2048
HEAD = 256
LANES = 128
EPSILON = 1e-06
BF = jnp.bfloat16
F32 = jnp.float32

ROWS = (((0,), (0,)), ((), ()))
COLS = (((1,), (1,)), ((), ()))
SECTION = ("z", "core")


def exchange(pieces, axis):
    return lax.all_to_all(pieces, axis, split_axis=0, concat_axis=0, tiled=True)


def sent_to_all(value, axis):
    return exchange(jnp.broadcast_to(value, (lax.axis_size(axis), *value.shape)), axis)


def other_core(value):
    return lax.ppermute(value, "core", [(0, 1), (1, 0)])


def high_low(value):
    high = lax.reduce_precision(value, 8, 7)
    return high.astype(BF), (value - high).astype(BF)


def attend(core_ref, mine_ref, other_ref, wk_ref, wv_ref, recip_ref, q_ref, g_ref, qg_ref, keep_ref, send_ref):
    core = core_ref[0]
    pairs = mine_ref.shape[0]
    rows = mine_ref.shape[1]
    scale = HEAD ** (-0.5)
    keys_raw = jnp.zeros((rows, HEAD), F32)
    values_raw = jnp.zeros((rows, HEAD), F32)
    square = jnp.zeros((rows, 1), F32)
    for z in range(pairs):
        for block_ref, side in ((mine_ref, core), (other_ref, 1 - core)):
            block = block_ref[z]
            keys_raw += jnp.dot(block, wk_ref[z, side], preferred_element_type=F32)
            values_raw += jnp.dot(block, wv_ref[z, side], preferred_element_type=F32)
            wide = block.astype(F32) * recip_ref[z, side]
            square += jnp.sum(wide * wide, axis=1, keepdims=True)
    inv_out = lax.rsqrt(square / D + EPSILON)
    keys = (keys_raw * inv_out).astype(BF)
    values = (values_raw * inv_out).astype(BF)
    key_grad = jnp.zeros((rows, HEAD), F32)
    value_grad = jnp.zeros((rows, HEAD), F32)
    step = 256
    for at in range(0, q_ref.shape[0], step):
        query = q_ref[at : at + step, :]
        grad = g_ref[at : at + step, :]
        scores = lax.dot_general(keys, query, COLS, preferred_element_type=F32) * scale
        raised = jnp.exp(scores - jnp.max(scores, axis=0, keepdims=True))
        probs = raised / jnp.sum(raised, axis=0, keepdims=True)
        probs_bf = probs.astype(BF)
        dprob = lax.dot_general(values, grad, COLS, preferred_element_type=F32)
        delta = jnp.sum(probs_bf.astype(F32) * dprob, axis=0, keepdims=True)
        dscore = (probs * (dprob - delta) * scale).astype(BF)
        qg_ref[at : at + step, :] = lax.dot_general(
            dscore, keys, ROWS, preferred_element_type=F32
        ).astype(BF)
        key_grad += jnp.dot(dscore, query, preferred_element_type=F32)
        value_grad += jnp.dot(probs_bf, grad, preferred_element_type=F32)
    key_grad = key_grad.astype(BF)
    value_grad = value_grad.astype(BF)
    inner = jnp.sum(
        key_grad.astype(F32) * keys_raw + value_grad.astype(F32) * values_raw, axis=1, keepdims=True
    )
    along = inv_out * inv_out * inv_out * inner * (1.0 / D)
    for z in range(pairs):
        for block_ref, out_ref, side in ((mine_ref, keep_ref, core), (other_ref, send_ref, 1 - core)):
            total = lax.dot_general(key_grad, wk_ref[z, side], COLS, preferred_element_type=F32)
            total += lax.dot_general(value_grad, wv_ref[z, side], COLS, preferred_element_type=F32)
            recip = recip_ref[z, side]
            term = inv_out * total - block_ref[z].astype(F32) * (recip * recip) * along
            out_ref[z] = term.astype(out_ref.dtype)


def cross_attention(mine, other, key_matrix, value_matrix, gain_all, query, grad):
    pairs = mine.shape[0]
    blocks = (pairs, 2, LANES, HEAD)
    recip = (1.0 / gain_all).reshape(pairs, 2, 1, LANES)
    core = lax.axis_index("core").astype(jnp.int32).reshape(1)
    vmem = pl.BlockSpec(memory_space=pltpu.VMEM)
    return pl.pallas_call(
        attend,
        out_shape=(
            jax.ShapeDtypeStruct(query.shape, BF),
            jax.ShapeDtypeStruct(mine.shape, F32),
            jax.ShapeDtypeStruct(mine.shape, BF),
        ),
        in_specs=[pl.BlockSpec(memory_space=pltpu.SMEM)] + [vmem] * 7,
        out_specs=(vmem, vmem, vmem),
        compiler_params=pltpu.CompilerParams(vmem_limit_bytes=40 * 1024 * 1024),
        cost_estimate=pl.CostEstimate(
            flops=3_500_000_000, bytes_accessed=8_000_000, transcendentals=262144
        ),
    )(core, mine, other, key_matrix.reshape(blocks), value_matrix.reshape(blocks), recip, query, grad)


def on_device(
    enc_hidden,
    mlp_gain,
    final_gain,
    w_gate,
    w_up,
    w_down,
    key_weight,
    value_weight,
    queries,
    context_grad,
):
    block, feats = enc_hidden.shape
    width = w_gate.shape[1]
    hidden_all = sent_to_all(enc_hidden, "tensor").reshape(-1, feats)
    tokens = hidden_all.shape[0]
    hidden_all_wide = hidden_all.astype(F32)
    scaled_all = (hidden_all_wide * mlp_gain[None, :]).astype(BF)
    gate_part = jnp.dot(scaled_all, w_gate, preferred_element_type=F32).astype(BF)
    up_part = jnp.dot(scaled_all, w_up, preferred_element_type=F32).astype(BF)
    square = jnp.sum(hidden_all_wide * hidden_all_wide, axis=1).reshape(-1, 1, block)
    groups = square.shape[0]
    gain_1 = lax.reduce_precision(final_gain, 8, 7)
    gain_2 = lax.reduce_precision(final_gain - gain_1, 8, 7)
    gain_3 = final_gain - gain_1 - gain_2
    gains = jnp.stack([gain_1, gain_2, gain_3]).astype(BF)
    gains = jnp.broadcast_to(gains, (groups, 3, LANES))
    squares = jnp.concatenate(high_low(square), axis=1)
    squares = jnp.pad(squares, ((0, 0), (0, 0), (0, LANES - block)))
    extra = jnp.pad(jnp.concatenate([gains, squares], axis=1), ((0, 0), (0, block - 5), (0, 0)))
    pieces = jnp.concatenate(
        [gate_part.reshape(groups, block, width), up_part.reshape(groups, block, width), extra], axis=2
    )
    arrived = exchange(pieces, SECTION).astype(F32)
    gain_all = jnp.sum(arrived[:, :3, 2 * width :], axis=1).reshape(-1)
    square_in = jnp.sum(arrived[:, 3:5, 2 * width : 2 * width + block], axis=(0, 1))
    gate_up = jnp.sum(arrived[:, :, : 2 * width], axis=0)
    inv_in = lax.rsqrt(square_in / D + EPSILON)[:, None]
    gate_pre = gate_up[:, :width] * inv_in
    up_pre = gate_up[:, width:] * inv_in
    sigmoid_gate = jax.nn.sigmoid(gate_pre)
    activated = gate_pre * sigmoid_gate
    hidden_act = (activated * up_pre).astype(BF)
    act_all = sent_to_all(hidden_act, SECTION).reshape(tokens, width)
    mixed_part = jnp.dot(act_all, w_down, preferred_element_type=F32).astype(BF)
    mixed = exchange(mixed_part.reshape(groups, block, feats), "tensor").astype(F32).sum(axis=0)
    outer = enc_hidden.astype(F32) + mixed
    scaled_outer = (outer * final_gain[None, :]).astype(BF)
    mine = sent_to_all(scaled_outer, ("z", "tensor")).reshape(-1, tokens, feats)
    other = other_core(mine)
    query_grad, keep, send = cross_attention(
        mine, other, key_weight[0], value_weight[0], gain_all, queries[0], context_grad[0]
    )
    both = (keep + other_core(send).astype(F32)).astype(BF)
    both = exchange(both.reshape(-1, block, feats), ("z", "tensor")).astype(F32).sum(axis=0)
    outer_grad = both * final_gain[None, :]
    outer_all = sent_to_all(outer_grad.astype(BF), "tensor").reshape(tokens, feats)
    act_part = lax.dot_general(outer_all, w_down, COLS, preferred_element_type=F32).astype(BF)
    act_grad = exchange(act_part.reshape(groups, block, width), SECTION).astype(F32).sum(axis=0)
    down_weight_grad = lax.dot_general(
        act_all, outer_all, ROWS, preferred_element_type=F32
    ).astype(BF)
    up_grad = act_grad * activated
    gate_grad = act_grad * up_pre * sigmoid_gate * (1.0 + gate_pre * (1.0 - sigmoid_gate))
    inner = jnp.sum(gate_grad * gate_pre + up_grad * up_pre, axis=1, keepdims=True)
    inner = inner * inv_in * inv_in / D
    inner = jnp.pad(jnp.concatenate(high_low(inner), axis=1), ((0, 0), (0, LANES - 2)))
    grads = jnp.concatenate(
        [(gate_grad * inv_in).astype(BF), (up_grad * inv_in).astype(BF), inner], axis=1
    )
    grads = sent_to_all(grads, SECTION).reshape(tokens, 2 * width + LANES)
    gate_all = grads[:, :width]
    up_all = grads[:, width : 2 * width]
    inner_all = jnp.sum(grads[:, 2 * width : 2 * width + 2].astype(F32), axis=1, keepdims=True)
    normed_grad = lax.dot_general(gate_all, w_gate, COLS, preferred_element_type=F32)
    normed_grad += lax.dot_general(up_all, w_up, COLS, preferred_element_type=F32)
    part = (normed_grad * mlp_gain[None, :] - hidden_all_wide * inner_all).astype(BF)
    part = exchange(part.reshape(groups, block, feats), "tensor").astype(F32).sum(axis=0)
    gate_weight_grad = lax.dot_general(
        scaled_all, gate_all, ROWS, preferred_element_type=F32
    ).astype(BF)
    up_weight_grad = lax.dot_general(
        scaled_all, up_all, ROWS, preferred_element_type=F32
    ).astype(BF)
    hidden_grad = outer_grad + part
    return (query_grad[None], hidden_grad, gate_weight_grad, up_weight_grad, down_weight_grad)


def solution(mesh):
    names = list(mesh.axis_names)
    at = names.index("section")
    shape = list(mesh.devices.shape)
    names[at : at + 1] = SECTION
    shape[at : at + 1] = [shape[at] // 2, 2]
    fine = Mesh(mesh.devices.reshape(shape), tuple(names))
    in_specs = (
        P(("dp", "tensor"), SECTION),
        P(SECTION),
        P(SECTION),
        P(SECTION, "tensor"),
        P(SECTION, "tensor"),
        P("tensor", SECTION),
        P(SECTION, None, "tensor"),
        P(SECTION, None, "tensor"),
        P(SECTION, "dp", "tensor"),
        P(SECTION, "dp", "tensor"),
    )
    out_specs = (
        P(SECTION, "dp", "tensor"),
        P(("dp", "tensor"), SECTION),
        P(("dp", *SECTION), "tensor"),
        P(("dp", *SECTION), "tensor"),
        P(("dp", "tensor"), SECTION),
    )
    return jax.shard_map(
        on_device, mesh=fine, in_specs=in_specs, out_specs=out_specs, check_vma=False
    )
```

time: 325 us -> 209 us (0.64)
  blocking collectives: 224 us -> 133 us
  waiting for transfers between devices: 49.8 us -> 32.1 us
  matrix products: 18.7 us -> 6.39 us
  Pallas kernels: 0 us -> 5.88 us
  local copies, waits for them, and re-layouts: 7 us -> 3.62 us
    all_to_all x10 -> x7, blocking collectives: 193 us -> 133 us  [exchange(): return lax.all_to_all(pieces, axis, split_axis=0, concat_axis=0, tiled=True)]
    all_gather x2 -> x0, blocking collectives: 31.2 us -> none  [the longest x1 15.9 us: side_by_side(): lax.all_gather(both, axis, axis=dim, tiled=True)]
    all_to_all x4 -> x3, waiting for transfers between devices: 49.8 us -> 29.8 us  [exchange(): return lax.all_to_all(pieces, axis, split_axis=0, concat_axis=0, tiled=True)]
    dot_general x17 -> x9, matrix products: 18.7 us -> 6.39 us  [the longest x1 1.11 us: on_device(): up_part = jnp.dot(scaled_all, w_up, preferred_element_type=F32).astype(BF)]
    ppermute x0 -> x2, starting transfers between devices: none -> 6.11 us  [other_core(): return lax.ppermute(value, 'core', [(0, 1), (1, 0)])]
    pallas_call x0 -> x1, Pallas kernels: none -> 5.88 us  [cross_attention(): pl.pallas_call(attend, out_shape=(jax.ShapeDtypeStruct(query.shape, BF),...]
    all_to_all x4 -> x3, starting transfers between devices: 19 us -> 15 us  [exchange(): return lax.all_to_all(pieces, axis, split_axis=0, concat_axis=0, tiled=True)]
    unnamed x45 -> x29, local copies, waits for them, and re-layouts: 5.17 us -> 1.29 us
  transfers between devices with their start and end apart: 4 -> 5, of which waited for: 4 -> 5; matrix products, arithmetic and copies ran while one was open for 2% -> 2% of each run, Pallas kernels for 0% -> 0%
where the time goes in v1:
time: 209 us; the launch traced here: 208 us
  blocking collectives  133 us (64%)
  waiting for transfers between devices  32.1 us (15%)
  starting transfers between devices  21.1 us (10%)
  matrix products  6.39 us (3%)
  Pallas kernels  5.88 us (3%)
  other arithmetic  4.09 us (2%)
  local copies, waits for them, and re-layouts  3.62 us (2%)
    all_to_all x7, blocking collectives, exchange(): return lax.all_to_all(pieces, axis, split_axis=0, concat_axis=0, tiled=True)  133 us
    all_to_all x3, waiting for transfers between devices, exchange(): return lax.all_to_all(pieces, axis, split_axis=0, concat_axis=0, tiled=True)  29.8 us
    all_to_all x3, starting transfers between devices, exchange(): return lax.all_to_all(pieces, axis, split_axis=0, concat_axis=0, tiled=True)  15 us
    ppermute x2, starting transfers between devices, other_core(): return lax.ppermute(value, 'core', [(0, 1), (1, 0)])  6.11 us
    pallas_call x1, Pallas kernels, cross_attention(): pl.pallas_call(attend, out_shape=(jax.ShapeDtypeStruct(query.shape, BF),...  5.88 us
  transfers between devices with their start and end apart: 5, of which 5 were waited for; matrix products, arithmetic and copies ran while one was open for 2% of the time, Pallas kernels for 0%

profile of v1, /device:TPU:1, one launch (start us, length us, event | category | flops | bytes accessed | tf_op | source)
XLA Modules:
  0.0 207.7 jit_solution(636709210478072370)
XLA Ops:
  0.6 0.0 copy-start
  0.6 1.4 broadcast_in_dim.28
  2.0 8.0 %all-to-all-start = ((bf16[16,16,128]{2,1,0:T(8,128)(2,1)}), bf16[16,16,128]{2,1,0:T(8,128)(2,1)S(1)}, u32[]{:S(2)}, u32[]{:S(2)}) async-start(bf16[16,16,128]{2,1,0:T(8,128)(2,1)} %broadcast_in_dim.28), calls=%async_computation | async-start | bytes 131072 | tf_op jit(solution)/shard_map/all_to_all | solution.py:22
  10.0 0.7 fusion.19
  10.7 6.6 %all-to-all-done = bf16[16,16,128]{2,1,0:T(8,128)(2,1)S(1)} async-done(((bf16[16,16,128]{2,1,0:T(8,128)(2,1)}), bf16[16,16,128]{2,1,0:T(8,128)(2,1)S(1)}, u32[]{:S(2)}, u32[]{:S(2)}) %all-to-all-start) | async-done | bytes 65568 | tf_op jit(solution)/shard_map/all_to_all | solution.py:22
  17.3 0.1 fusion.11
  17.4 0.7 fusion.12
  18.1 1.1 convolution_convert_fusion.1
  19.2 1.1 convolution_convert_fusion.2
  20.4 31.2 %all_to_all.50 = bf16[16,16,1152]{2,1,0:T(8,128)(2,1)S(1)} all-to-all(bf16[16,16,1152]{2,1,0:T(8,128)(2,1)S(1)} %fusion.5), channel_id=1, replica_groups=mesh['z'=8,'core'=2,'tensor'=16,'dp'=2] {'z','core'}, dimensions={0} | all-to-all | bytes 1179648 | tf_op jit(solution)/shard_map/all_to_all | solution.py:22
  51.6 0.1 convert_element_type.138
  51.8 0.1 slice_reduce_fusion
  51.8 0.1 multiply_convert_fusion.2
  52.0 14.6 %all_to_all.51 = bf16[16,16,512]{2,1,0:T(8,128)(2,1)S(1)} all-to-all(bf16[16,16,512]{2,1,0:T(8,128)(2,1)S(1)} %broadcast_in_dim.30), channel_id=1, replica_groups=mesh['z'=8,'core'=2,'tensor'=16,'dp'=2] {'z','core'}, dimensions={0} | all-to-all | bytes 524288 | tf_op jit(solution)/shard_map/all_to_all | solution.py:22
  66.6 0.2 convolution_convert_fusion.5
  66.8 10.4 %all_to_all.52 = bf16[16,16,128]{2,1,0:T(8,128)(2,1)S(1)} all-to-all(bf16[16,16,128]{2,1,0:T(8,128)(2,1)S(1)} %bitcast.79), channel_id=1, replica_groups=mesh['z'=8,'core'=2,'tensor'=16,'dp'=2] {'tensor'}, dimensions={0} | all-to-all | bytes 131072 | tf_op jit(solution)/shard_map/all_to_all | solution.py:22
  77.3 0.1 broadcast_in_dim.31
  77.4 24.7 %all_to_all.53 = bf16[128,16,128]{2,1,0:T(8,128)(2,1)S(1)} all-to-all(bf16[128,16,128]{2,1,0:T(8,128)(2,1)S(1)} %broadcast_in_dim.31), channel_id=1, replica_groups=mesh['z'=8,'core'=2,'tensor'=16,'dp'=2] {'z','tensor'}, dimensions={0} | all-to-all | bytes 1048576 | tf_op jit(solution)/shard_map/all_to_all | solution.py:22
  102.1 3.8 %collective-permute-start = (bf16[8,256,128]{2,1,0:T(8,128)(2,1)S(1)}, bf16[8,256,128]{2,1,0:T(8,128)(2,1)}, u32[]{:S(2)}, u32[]{:S(2)}) collective-permute-start(bf16[8,256,128]{2,1,0:T(8,128)(2,1)S(1)} %bitcast.61), channel_id=1, source_target_pairs={{0,32},{32,0},{1,33},{33,1},{2,34},{34,2},{3,35},{35,3},{4,36},{36... | collective-permute-start | bytes 1572872 | tf_op jit(solution)/shard_map/ppermute | solution.py:30
  105.9 0.9 slice_reduce_fusion.1
  106.8 0.8 collective-permute-done.other_ref
  107.6 1.0 copy-done.4
  108.6 5.9 %shard_map.137 = (bf16[1024,256]{1,0:T(8,128)(2,1)}, f32[8,256,128]{2,1,0:T(8,128)S(1)}, bf16[8,256,128]{2,1,0:T(8,128)(2,1)S(1)}) custom-call(s32[1]{0:T(128)} %bitcast.core_ref, bf16[8,256,128]{2,1,0:T(8,128)(2,1)S(1)} %bitcast.62, bf16[8,256,128]{2,1,0:T(8,128)(2,1)} %collective-permute-done.other_ref, bf16[8,2,128,256]{3,2,1,0:T(8,128)(2,1)S(1)} %bitcast.64, ...), custom_call_target="tpu_custom_call" | custom-call | flops 3500000000 | bytes 8000000 | tf_op jit(solution)/shard_map/pallas_call | solution.py:95
  114.5 2.3 %collective-permute-start.1 = (bf16[8,256,128]{2,1,0:T(8,128)(2,1)S(1)}, bf16[8,256,128]{2,1,0:T(8,128)(2,1)S(1)}, u32[]{:S(2)}, u32[]{:S(2)}) collective-permute-start(bf16[8,256,128]{2,1,0:T(8,128)(2,1)S(1)} %get-tuple-element.10), channel_id=1, source_target_pairs={{0,32},{32,0},{1,33},{33,1},{2,34},{34,2},{3,35},{35,3},{4,36},{36... | collective-permute-start | bytes 1572872 | tf_op jit(solution)/shard_map/ppermute | solution.py:30
  116.8 1.5 collective-permute-done.1
  118.3 0.1 add_convert_fusion
  118.4 24.9 %all_to_all.54 = bf16[128,16,128]{2,1,0:T(8,128)(2,1)S(1)} all-to-all(bf16[128,16,128]{2,1,0:T(8,128)(2,1)S(1)} %bitcast.73), channel_id=1, replica_groups=mesh['z'=8,'core'=2,'tensor'=16,'dp'=2] {'z','tensor'}, dimensions={0} | all-to-all | bytes 1048576 | tf_op jit(solution)/shard_map/all_to_all | solution.py:22
  143.3 0.1 convert_reduce_fusion
  143.5 11.1 %all_to_all.55 = bf16[16,16,128]{2,1,0:T(8,128)(2,1)S(1)} all-to-all(bf16[16,16,128]{2,1,0:T(8,128)(2,1)S(1)} %broadcast_in_dim.33), channel_id=1, replica_groups=mesh['z'=8,'core'=2,'tensor'=16,'dp'=2] {'tensor'}, dimensions={0} | all-to-all | bytes 131072 | tf_op jit(solution)/shard_map/all_to_all | solution.py:22
  154.6 0.2 convolution_convert_fusion
  154.8 16.6 %all_to_all.56 = bf16[16,16,512]{2,1,0:T(8,128)(2,1)S(1)} all-to-all(bf16[16,16,512]{2,1,0:T(8,128)(2,1)S(1)} %bitcast.75), channel_id=1, replica_groups=mesh['z'=8,'core'=2,'tensor'=16,'dp'=2] {'z','core'}, dimensions={0} | all-to-all | bytes 524288 | tf_op jit(solution)/shard_map/all_to_all | solution.py:22
  171.4 0.1 multiply_convert_fusion.1
  171.5 0.2 add_reduce_fusion
  171.8 0.1 copy.25
  171.9 0.9 broadcast_in_dim.34
  172.7 3.5 %all-to-all-start.8 = ((bf16[16,16,1152]{2,1,0:T(8,128)(2,1)}), bf16[16,16,1152]{2,1,0:T(8,128)(2,1)S(1)}, u32[]{:S(2)}, u32[]{:S(2)}) async-start(bf16[16,16,1152]{2,1,0:T(8,128)(2,1)} %broadcast_in_dim.34), calls=%async_computation.8 | async-start | bytes 1179648 | tf_op jit(solution)/shard_map/all_to_all | solution.py:22
  176.2 0.0 copy-start.8
  176.3 0.9 fusion.1
  177.2 16.9 %all-to-all-done.8 = bf16[16,16,1152]{2,1,0:T(8,128)(2,1)S(1)} async-done(((bf16[16,16,1152]{2,1,0:T(8,128)(2,1)}), bf16[16,16,1152]{2,1,0:T(8,128)(2,1)S(1)}, u32[]{:S(2)}, u32[]{:S(2)}) %all-to-all-start.8) | async-done | bytes 589856 | tf_op jit(solution)/shard_map/all_to_all | solution.py:22
  194.1 0.9 convolution_convert_fusion.4
  195.0 0.2 fusion.9
  195.2 0.1 copy.23
  195.3 0.1 bitcast_multiply_fusion
  195.5 0.9 fusion.4
  196.3 3.5 %all-to-all-start.9 = ((bf16[16,16,128]{2,1,0:T(8,128)(2,1)}), bf16[16,16,128]{2,1,0:T(8,128)(2,1)S(1)}, u32[]{:S(2)}, u32[]{:S(2)}) async-start(bf16[16,16,128]{2,1,0:T(8,128)(2,1)} %bitcast.23), calls=%async_computation.9 | async-start | bytes 131072 | tf_op jit(solution)/shard_map/all_to_all | solution.py:22
  199.8 0.9 convolution_convert_fusion.3
  200.7 6.3 %all-to-all-done.9 = bf16[16,16,128]{2,1,0:T(8,128)(2,1)S(1)} async-done(((bf16[16,16,128]{2,1,0:T(8,128)(2,1)}), bf16[16,16,128]{2,1,0:T(8,128)(2,1)S(1)}, u32[]{:S(2)}, u32[]{:S(2)}) %all-to-all-start.9) | async-done | bytes 65568 | tf_op jit(solution)/shard_map/all_to_all | solution.py:22
  207.1 0.6 multiply_add_fusion
  (45 shorter events, 0.4 us)
Async XLA Ops:
  0.6 65.9 %copy-start = (bf16[512,128]{1,0:T(8,128)(2,1)S(1)}, bf16[512,128]{1,0:T(8,128)(2,1)}, u32[]{:S(2)}) copy-start(bf16[512,128]{1,0:T(8,128)(2,1)} %param.15) | copy-start | bytes 393220
  2.0 15.3 %all-to-all-start = ((bf16[16,16,128]{2,1,0:T(8,128)(2,1)}), bf16[16,16,128]{2,1,0:T(8,128)(2,1)S(1)}, u32[]{:S(2)}, u32[]{:S(2)}) async-start(bf16[16,16,128]{2,1,0:T(8,128)(2,1)} %broadcast_in_dim.28), calls=%async_computation | async-start | bytes 131072 | tf_op jit(solution)/shard_map/all_to_all | solution.py:22
  51.7 15.1 %copy-start.5 = (f32[16,16,1152]{2,1,0:T(8,128)}, f32[16,16,1152]{2,1,0:T(8,128)S(1)}, u32[]{:S(2)}) copy-start(f32[16,16,1152]{2,1,0:T(8,128)S(1)} %convert_element_type.138) | copy-start | bytes 3538948
  51.7 25.5 %copy-start.10 = (bf16[16,128]{1,0:T(8,128)(2,1)S(1)}, bf16[16,128]{1,0:T(8,128)(2,1)}, u32[]{:S(2)}) copy-start(bf16[16,128]{1,0:T(8,128)(2,1)} %param.10) | copy-start | bytes 12292
  51.7 25.5 %copy-start.11 = (f32[128]{0:T(128)S(1)}, f32[128]{0:T(128)}, u32[]{:S(2)}) copy-start(f32[128]{0:T(128)} %param.12) | copy-start | bytes 1540
  51.9 55.6 %copy-start.3 = (bf16[1,1024,256]{2,1,0:T(8,128)(2,1)S(1)}, bf16[1,1024,256]{2,1,0:T(8,128)(2,1)}, u32[]{:S(2)}) copy-start(bf16[1,1024,256]{2,1,0:T(8,128)(2,1)} %param.18) | copy-start | bytes 1572868
  66.6 10.7 %copy-start.6 = (bf16[16,16,512]{2,1,0:T(8,128)(2,1)}, bf16[16,16,512]{2,1,0:T(8,128)(2,1)S(1)}, u32[]{:S(2)}) copy-start(bf16[16,16,512]{2,1,0:T(8,128)(2,1)S(1)} %all_to_all.51) | copy-start | bytes 786436
  66.6 41.0 %copy-start.1 = (bf16[1,2048,256]{2,1,0:T(8,128)(2,1)S(1)}, bf16[1,2048,256]{2,1,0:T(8,128)(2,1)}, u32[]{:S(2)}) copy-start(bf16[1,2048,256]{2,1,0:T(8,128)(2,1)} %param.16) | copy-start | bytes 3145732
  66.6 41.0 %copy-start.2 = (bf16[1,2048,256]{2,1,0:T(8,128)(2,1)S(1)}, bf16[1,2048,256]{2,1,0:T(8,128)(2,1)}, u32[]{:S(2)}) copy-start(bf16[1,2048,256]{2,1,0:T(8,128)(2,1)} %param.17) | copy-start | bytes 3145732
  102.1 5.5 %collective-permute-start = (bf16[8,256,128]{2,1,0:T(8,128)(2,1)S(1)}, bf16[8,256,128]{2,1,0:T(8,128)(2,1)}, u32[]{:S(2)}, u32[]{:S(2)}) collective-permute-start(bf16[8,256,128]{2,1,0:T(8,128)(2,1)S(1)} %bitcast.61), channel_id=1, source_target_pairs={{0,32},{32,0},{1,33},{33,1},{2,34},{34,2},{3,35},{35,3},{4,36},{36... | collective-permute-start | bytes 1572872 | tf_op jit(solution)/shard_map/ppermute | solution.py:30
  107.6 1.0 copy-start.4
  114.5 3.8 %collective-permute-start.1 = (bf16[8,256,128]{2,1,0:T(8,128)(2,1)S(1)}, bf16[8,256,128]{2,1,0:T(8,128)(2,1)S(1)}, u32[]{:S(2)}, u32[]{:S(2)}) collective-permute-start(bf16[8,256,128]{2,1,0:T(8,128)(2,1)S(1)} %get-tuple-element.10), channel_id=1, source_target_pairs={{0,32},{32,0},{1,33},{33,1},{2,34},{34,2},{3,35},{35,3},{4,36},{36... | collective-permute-start | bytes 1572872 | tf_op jit(solution)/shard_map/ppermute | solution.py:30
  171.4 4.8 %copy-start.7 = (bf16[16,16,512]{2,1,0:T(8,128)(2,1)S(1)}, bf16[16,16,512]{2,1,0:T(8,128)(2,1)}, u32[]{:S(2)}) copy-start(bf16[16,16,512]{2,1,0:T(8,128)(2,1)} %copy-done.6) | copy-start | bytes 786436
  172.7 21.4 %all-to-all-start.8 = ((bf16[16,16,1152]{2,1,0:T(8,128)(2,1)}), bf16[16,16,1152]{2,1,0:T(8,128)(2,1)S(1)}, u32[]{:S(2)}, u32[]{:S(2)}) async-start(bf16[16,16,1152]{2,1,0:T(8,128)(2,1)} %broadcast_in_dim.34), calls=%async_computation.8 | async-start | bytes 1179648 | tf_op jit(solution)/shard_map/all_to_all | solution.py:22
  176.2 18.8 %copy-start.9 = (bf16[128,512]{1,0:T(8,128)(2,1)S(1)}, bf16[128,512]{1,0:T(8,128)(2,1)}, u32[]{:S(2)}) copy-start(bf16[128,512]{1,0:T(8,128)(2,1)} %param.13) | copy-start | bytes 393220
  176.2 19.2 %copy-start.8 = (bf16[128,512]{1,0:T(8,128)(2,1)S(1)}, bf16[128,512]{1,0:T(8,128)(2,1)}, u32[]{:S(2)}) copy-start(bf16[128,512]{1,0:T(8,128)(2,1)} %param.14) | copy-start | bytes 393220
  176.2 19.2 %copy-start.12 = (f32[128]{0:T(128)S(1)}, f32[128]{0:T(128)}, u32[]{:S(2)}) copy-start(f32[128]{0:T(128)} %param.11) | copy-start | bytes 1540
  196.3 10.7 %all-to-all-start.9 = ((bf16[16,16,128]{2,1,0:T(8,128)(2,1)}), bf16[16,16,128]{2,1,0:T(8,128)(2,1)S(1)}, u32[]{:S(2)}, u32[]{:S(2)}) async-start(bf16[16,16,128]{2,1,0:T(8,128)(2,1)} %bitcast.23), calls=%async_computation.9 | async-start | bytes 131072 | tf_op jit(solution)/shard_map/all_to_all | solution.py:22

commit v2 on v1

--- a/solution.py
+++ b/solution.py
@@ -77,18 +77,23 @@
         key_grad.astype(F32) * keys_raw + value_grad.astype(F32) * values_raw, axis=1, keepdims=True
     )
     along = inv_out * inv_out * inv_out * inner * (1.0 / D)
+    first = core == 0
     for z in range(pairs):
-        for block_ref, out_ref, side in ((mine_ref, keep_ref, core), (other_ref, send_ref, 1 - core)):
+        for side in range(2):
+            block = jnp.where(core == side, mine_ref[z], other_ref[z]).astype(F32)
             total = lax.dot_general(key_grad, wk_ref[z, side], COLS, preferred_element_type=F32)
             total += lax.dot_general(value_grad, wv_ref[z, side], COLS, preferred_element_type=F32)
             recip = recip_ref[z, side]
-            term = inv_out * total - block_ref[z].astype(F32) * (recip * recip) * along
-            out_ref[z] = term.astype(out_ref.dtype)
+            term = inv_out * total - block * (recip * recip) * along
+            term = term.reshape(pairs, 2, -1, LANES)
+            keep_ref[:, 2 * z + side] = jnp.where(first, term[:, 0], term[:, 1])
+            send_ref[:, 2 * z + side] = jnp.where(first, term[:, 1], term[:, 0]).astype(BF)
 
 
 def cross_attention(mine, other, key_matrix, value_matrix, gain_all, query, grad):
     pairs = mine.shape[0]
     blocks = (pairs, 2, LANES, HEAD)
+    split = (pairs, 2 * pairs, mine.shape[1] // (2 * pairs), LANES)
     recip = (1.0 / gain_all).reshape(pairs, 2, 1, LANES)
     core = lax.axis_index("core").astype(jnp.int32).reshape(1)
     vmem = pl.BlockSpec(memory_space=pltpu.VMEM)
@@ -96,8 +101,8 @@
         attend,
         out_shape=(
             jax.ShapeDtypeStruct(query.shape, BF),
-            jax.ShapeDtypeStruct(mine.shape, F32),
-            jax.ShapeDtypeStruct(mine.shape, BF),
+            jax.ShapeDtypeStruct(split, F32),
+            jax.ShapeDtypeStruct(split, BF),
         ),
         in_specs=[pl.BlockSpec(memory_space=pltpu.SMEM)] + [vmem] * 7,
         out_specs=(vmem, vmem, vmem),
@@ -122,6 +127,9 @@
 ):
     block, feats = enc_hidden.shape
     width = w_gate.shape[1]
+    gate_full = lax.all_gather(w_gate, SECTION, axis=0, tiled=True)
+    up_full = lax.all_gather(w_up, SECTION, axis=0, tiled=True)
+    down_full = lax.all_gather(w_down, SECTION, axis=0)
     hidden_all = sent_to_all(enc_hidden, "tensor").reshape(-1, feats)
     tokens = hidden_all.shape[0]
     hidden_all_wide = hidden_all.astype(F32)
@@ -130,20 +138,22 @@
     up_part = jnp.dot(scaled_all, w_up, preferred_element_type=F32).astype(BF)
     square = jnp.sum(hidden_all_wide * hidden_all_wide, axis=1).reshape(-1, 1, block)
     groups = square.shape[0]
-    gain_1 = lax.reduce_precision(final_gain, 8, 7)
-    gain_2 = lax.reduce_precision(final_gain - gain_1, 8, 7)
-    gain_3 = final_gain - gain_1 - gain_2
-    gains = jnp.stack([gain_1, gain_2, gain_3]).astype(BF)
-    gains = jnp.broadcast_to(gains, (groups, 3, LANES))
+    gains = jnp.stack([final_gain, mlp_gain])
+    gain_1 = lax.reduce_precision(gains, 8, 7)
+    gain_2 = lax.reduce_precision(gains - gain_1, 8, 7)
+    gain_3 = gains - gain_1 - gain_2
+    gains = jnp.concatenate([gain_1, gain_2, gain_3]).astype(BF)
+    gains = jnp.broadcast_to(gains, (groups, 6, LANES))
     squares = jnp.concatenate(high_low(square), axis=1)
     squares = jnp.pad(squares, ((0, 0), (0, 0), (0, LANES - block)))
-    extra = jnp.pad(jnp.concatenate([gains, squares], axis=1), ((0, 0), (0, block - 5), (0, 0)))
+    extra = jnp.pad(jnp.concatenate([gains, squares], axis=1), ((0, 0), (0, block - 8), (0, 0)))
     pieces = jnp.concatenate(
         [gate_part.reshape(groups, block, width), up_part.reshape(groups, block, width), extra], axis=2
     )
     arrived = exchange(pieces, SECTION).astype(F32)
-    gain_all = jnp.sum(arrived[:, :3, 2 * width :], axis=1).reshape(-1)
-    square_in = jnp.sum(arrived[:, 3:5, 2 * width : 2 * width + block], axis=(0, 1))
+    gain_all = arrived[:, 0:2, 2 * width :] + arrived[:, 2:4, 2 * width :]
+    gain_all = gain_all + arrived[:, 4:6, 2 * width :]
+    square_in = jnp.sum(arrived[:, 6:8, 2 * width : 2 * width + block], axis=(0, 1))
     gate_up = jnp.sum(arrived[:, :, : 2 * width], axis=0)
     inv_in = lax.rsqrt(square_in / D + EPSILON)[:, None]
     gate_pre = gate_up[:, :width] * inv_in
@@ -159,40 +169,46 @@
     mine = sent_to_all(scaled_outer, ("z", "tensor")).reshape(-1, tokens, feats)
     other = other_core(mine)
     query_grad, keep, send = cross_attention(
-        mine, other, key_weight[0], value_weight[0], gain_all, queries[0], context_grad[0]
+        mine, other, key_weight[0], value_weight[0], gain_all[:, 0], queries[0], context_grad[0]
     )
     both = (keep + other_core(send).astype(F32)).astype(BF)
     both = exchange(both.reshape(-1, block, feats), ("z", "tensor")).astype(F32).sum(axis=0)
-    outer_grad = both * final_gain[None, :]
-    outer_all = sent_to_all(outer_grad.astype(BF), "tensor").reshape(tokens, feats)
-    act_part = lax.dot_general(outer_all, w_down, COLS, preferred_element_type=F32).astype(BF)
-    act_grad = exchange(act_part.reshape(groups, block, width), SECTION).astype(F32).sum(axis=0)
+    gains_here = lax.dynamic_index_in_dim(gain_all, lax.axis_index("tensor"), 0, keepdims=False)
+    outer_grad = both * gains_here[:1]
+    outer_row = sent_to_all(outer_grad.astype(BF), "tensor")
+    act_grad = jnp.einsum("btf,bhf->th", outer_row, down_full, preferred_element_type=F32)
+    outer_all = exchange(outer_row, SECTION).reshape(tokens, feats)
     down_weight_grad = lax.dot_general(
         act_all, outer_all, ROWS, preferred_element_type=F32
     ).astype(BF)
     up_grad = act_grad * activated
     gate_grad = act_grad * up_pre * sigmoid_gate * (1.0 + gate_pre * (1.0 - sigmoid_gate))
-    inner = jnp.sum(gate_grad * gate_pre + up_grad * up_pre, axis=1, keepdims=True)
-    inner = inner * inv_in * inv_in / D
-    inner = jnp.pad(jnp.concatenate(high_low(inner), axis=1), ((0, 0), (0, LANES - 2)))
-    grads = jnp.concatenate(
-        [(gate_grad * inv_in).astype(BF), (up_grad * inv_in).astype(BF), inner], axis=1
-    )
-    grads = sent_to_all(grads, SECTION).reshape(tokens, 2 * width + LANES)
-    gate_all = grads[:, :width]
-    up_all = grads[:, width : 2 * width]
-    inner_all = jnp.sum(grads[:, 2 * width : 2 * width + 2].astype(F32), axis=1, keepdims=True)
-    normed_grad = lax.dot_general(gate_all, w_gate, COLS, preferred_element_type=F32)
-    normed_grad += lax.dot_general(up_all, w_up, COLS, preferred_element_type=F32)
-    part = (normed_grad * mlp_gain[None, :] - hidden_all_wide * inner_all).astype(BF)
-    part = exchange(part.reshape(groups, block, feats), "tensor").astype(F32).sum(axis=0)
+    inner = jnp.sum(gate_grad * gate_pre + up_grad * up_pre, axis=1)[None, :]
+    inner = inner * (inv_in * inv_in / D).reshape(1, -1)
+    inner = jnp.concatenate(high_low(inner), axis=0)
+    inner = jnp.pad(inner, ((0, 6), (0, LANES - block)))
+    gate_grad = (gate_grad * inv_in).astype(BF)
+    up_grad = (up_grad * inv_in).astype(BF)
+    normed_grad = lax.dot_general(gate_grad, gate_full, COLS, preferred_element_type=F32)
+    normed_grad += lax.dot_general(up_grad, up_full, COLS, preferred_element_type=F32)
+    part = jnp.swapaxes(normed_grad.astype(BF).reshape(block, groups, feats), 0, 1)
+    part = jnp.concatenate([part, jnp.broadcast_to(inner, (groups, *inner.shape))], axis=1)
+    part = exchange(part, "tensor").astype(F32).sum(axis=0)
+    along = part[block : block + 1] + part[block + 1 : block + 2]
+    final = jnp.concatenate(
+        [outer_grad + gains_here[1:] * part[:block], jnp.pad(along, ((0, 7), (0, 0)))], axis=0
+    )
+    swap = [(a * groups + b, b * groups + a) for a in range(groups) for b in range(groups)]
+    final = lax.ppermute(final, (*SECTION, "tensor"), swap)
+    hidden_grad = final[:block] - enc_hidden.astype(F32) * final[block, :block][:, None]
+    grads = sent_to_all(jnp.concatenate([gate_grad, up_grad], axis=1), SECTION)
+    grads = grads.reshape(tokens, 2 * width)
     gate_weight_grad = lax.dot_general(
-        scaled_all, gate_all, ROWS, preferred_element_type=F32
+        scaled_all, grads[:, :width], ROWS, preferred_element_type=F32
     ).astype(BF)
     up_weight_grad = lax.dot_general(
-        scaled_all, up_all, ROWS, preferred_element_type=F32
+        scaled_all, grads[:, width:], ROWS, preferred_element_type=F32
     ).astype(BF)
-    hidden_grad = outer_grad + part
     return (query_grad[None], hidden_grad, gate_weight_grad, up_weight_grad, down_weight_grad)
 
 

time: 209 us -> 236 us (1.13)
  blocking collectives: 133 us -> 60.5 us
  waiting for transfers between devices: 32.1 us -> 82.7 us
  starting transfers between devices: 21.1 us -> 48.7 us
  between operations: 1.03 us -> 14.1 us
  matrix products: 6.39 us -> 11.9 us
  local copies, waits for them, and re-layouts: 3.62 us -> 6.25 us
    all_to_all x7 -> x3, blocking collectives: 133 us -> 60.5 us  [exchange(): return lax.all_to_all(pieces, axis, split_axis=0, concat_axis=0, tiled=True)]
    all_to_all x3 -> x7, waiting for transfers between devices: 29.8 us -> 76.4 us  [exchange(): return lax.all_to_all(pieces, axis, split_axis=0, concat_axis=0, tiled=True)]
    all_to_all x3 -> x7, starting transfers between devices: 15 us -> 40.1 us  [exchange(): return lax.all_to_all(pieces, axis, split_axis=0, concat_axis=0, tiled=True)]
    dot_general x5, matrix products: 3.03 us -> 8.52 us  [the longest x1 2.29 us: on_device(): jnp.einsum('btf,bhf->th', outer_row, down_full, preferred_element_type=F32)]
  transfers between devices with their start and end apart: 5 -> 13, of which waited for: 5 -> 10; matrix products, arithmetic and copies ran while one was open for 2% -> 7% of each run, Pallas kernels for 0% -> 2%
where the time goes in v2:
time: 236 us; the launch traced here: 235 us
  waiting for transfers between devices  82.7 us (35%)
  blocking collectives  60.5 us (26%)
  starting transfers between devices  48.7 us (21%)
  between operations  14.1 us (6%)
  matrix products  11.9 us (5%)
  local copies, waits for them, and re-layouts  6.25 us (3%)
  other arithmetic  5.5 us (2%)
  Pallas kernels  5.24 us (2%)
    all_to_all x7, waiting for transfers between devices, exchange(): return lax.all_to_all(pieces, axis, split_axis=0, concat_axis=0, tiled=True)  76.4 us
    all_to_all x3, blocking collectives, exchange(): return lax.all_to_all(pieces, axis, split_axis=0, concat_axis=0, tiled=True)  60.5 us
    all_to_all x7, starting transfers between devices, exchange(): return lax.all_to_all(pieces, axis, split_axis=0, concat_axis=0, tiled=True)  40.1 us
    ppermute x2, starting transfers between devices, other_core(): return lax.ppermute(value, 'core', [(0, 1), (1, 0)])  6.15 us
    pallas_call x1, Pallas kernels, cross_attention(): pl.pallas_call(attend, out_shape=(jax.ShapeDtypeStruct(query.shape, BF),...  5.24 us
  transfers between devices with their start and end apart: 13, of which 10 were waited for; matrix products, arithmetic and copies ran while one was open for 7% of the time, Pallas kernels for 2%

profile of v2, /device:TPU:1, one launch (start us, length us, event | category | flops | bytes accessed | tf_op | source)
XLA Modules:
  0.0 234.9 jit_solution(5687652636327332435)
XLA Ops:
  7.2 0.7 all-gather.9.cloned.1.call-update
  7.9 1.3 broadcast_in_dim.30
  9.2 8.0 %all-to-all-start = ((bf16[16,16,128]{2,1,0:T(8,128)(2,1)}), bf16[16,16,128]{2,1,0:T(8,128)(2,1)S(1)}, u32[]{:S(2)}, u32[]{:S(2)}) async-start(bf16[16,16,128]{2,1,0:T(8,128)(2,1)} %broadcast_in_dim.30), calls=%async_computation | async-start | bytes 131072 | tf_op jit(solution)/shard_map/all_to_all | solution.py:22
  17.3 0.7 all-gather.5.cloned.1.call-update
  18.0 0.7 reduce-precision_convert_fusion.2
  18.7 5.8 %all-to-all-done = bf16[16,16,128]{2,1,0:T(8,128)(2,1)S(1)} async-done(((bf16[16,16,128]{2,1,0:T(8,128)(2,1)}), bf16[16,16,128]{2,1,0:T(8,128)(2,1)S(1)}, u32[]{:S(2)}, u32[]{:S(2)}) %all-to-all-start) | async-done | bytes 65568 | tf_op jit(solution)/shard_map/all_to_all | solution.py:22
  24.6 0.7 fusion.7
  25.3 1.1 convolution_convert_fusion.1
  26.4 1.1 convolution_convert_fusion
  27.6 35.3 %all_to_all.50 = bf16[16,16,1152]{2,1,0:T(8,128)(2,1)S(1)} all-to-all(bf16[16,16,1152]{2,1,0:T(8,128)(2,1)S(1)} %fusion.4), channel_id=1, replica_groups=mesh['z'=8,'core'=2,'tensor'=16,'dp'=2] {'z','core'}, dimensions={0} | all-to-all | bytes 1179648 | tf_op jit(solution)/shard_map/all_to_all | solution.py:22
  63.1 1.0 copy-done.4
  64.1 0.4 copy-done.11
  64.7 14.8 %all_to_all.51 = bf16[16,16,512]{2,1,0:T(8,128)(2,1)S(1)} all-to-all(bf16[16,16,512]{2,1,0:T(8,128)(2,1)S(1)} %broadcast_in_dim.33), channel_id=1, replica_groups=mesh['z'=8,'core'=2,'tensor'=16,'dp'=2] {'z','core'}, dimensions={0} | all-to-all | bytes 524288 | tf_op jit(solution)/shard_map/all_to_all | solution.py:22
  79.7 10.3 %all_to_all.52 = bf16[16,16,128]{2,1,0:T(8,128)(2,1)S(1)} all-to-all(bf16[16,16,128]{2,1,0:T(8,128)(2,1)S(1)} %bitcast.77), channel_id=1, replica_groups=mesh['z'=8,'core'=2,'tensor'=16,'dp'=2] {'tensor'}, dimensions={0} | all-to-all | bytes 131072 | tf_op jit(solution)/shard_map/all_to_all | solution.py:22
  90.1 0.9 broadcast_in_dim.34
  91.0 6.2 %all-to-all-start.4 = ((bf16[128,16,128]{2,1,0:T(8,128)(2,1)}), bf16[128,16,128]{2,1,0:T(8,128)(2,1)S(1)}, u32[]{:S(2)}, u32[]{:S(2)}) async-start(bf16[128,16,128]{2,1,0:T(8,128)(2,1)} %broadcast_in_dim.34), calls=%async_computation.4 | async-start | bytes 1048576 | tf_op jit(solution)/shard_map/all_to_all | solution.py:22
  97.2 0.7 all-gather.7.cloned.1.call-update
  97.9 18.4 %all-to-all-done.4 = bf16[128,16,128]{2,1,0:T(8,128)(2,1)S(1)} async-done(((bf16[128,16,128]{2,1,0:T(8,128)(2,1)}), bf16[128,16,128]{2,1,0:T(8,128)(2,1)S(1)}, u32[]{:S(2)}, u32[]{:S(2)}) %all-to-all-start.4) | async-done | bytes 524320 | tf_op jit(solution)/shard_map/all_to_all | solution.py:22
  116.3 3.9 %collective-permute-start = (bf16[8,256,128]{2,1,0:T(8,128)(2,1)S(1)}, bf16[8,256,128]{2,1,0:T(8,128)(2,1)}, u32[]{:S(2)}, u32[]{:S(2)}) collective-permute-start(bf16[8,256,128]{2,1,0:T(8,128)(2,1)S(1)} %bitcast.63), channel_id=1, source_target_pairs={{0,32},{32,0},{1,33},{33,1},{2,34},{34,2},{3,35},{35,3},{4,36},{36... | collective-permute-start | bytes 1572872 | tf_op jit(solution)/shard_map/ppermute | solution.py:30
  120.2 1.0 slice_add_fusion
  121.2 0.6 collective-permute-done.other_ref
  121.8 1.0 copy-done.3
  122.9 5.2 %shard_map.137 = (bf16[1024,256]{1,0:T(8,128)(2,1)}, f32[8,16,16,128]{3,2,1,0:T(8,128)S(1)}, bf16[8,16,16,128]{3,2,1,0:T(8,128)(2,1)S(1)}) custom-call(s32[1]{0:T(128)} %bitcast.core_ref, bf16[8,256,128]{2,1,0:T(8,128)(2,1)S(1)} %bitcast.64, bf16[8,256,128]{2,1,0:T(8,128)(2,1)} %collective-permute-done.other_ref, bf16[8,2,128,256]{3,2,1,0:T(8,128)(2,1)S(1)} %bitcast.66, ...), custom_call_target="tpu_custom_call" | custom-call | flops 3500000000 | bytes 8000000 | tf_op jit(solution)/shard_map/pallas_call | solution.py:100
  128.1 2.3 collective-permute-start.1
  130.4 1.5 collective-permute-done.1
  131.9 0.9 add_convert_fusion
  132.9 6.6 %all-to-all-start.5 = ((bf16[128,16,128]{2,1,0:T(8,128)(2,1)}), bf16[128,16,128]{2,1,0:T(8,128)(2,1)S(1)}, u32[]{:S(2)}, u32[]{:S(2)}) async-start(bf16[128,16,128]{2,1,0:T(8,128)(2,1)} %bitcast.16), calls=%async_computation.5 | async-start | bytes 1048576 | tf_op jit(solution)/shard_map/all_to_all | solution.py:22
  139.5 19.1 %all-to-all-done.5 = bf16[128,16,128]{2,1,0:T(8,128)(2,1)S(1)} async-done(((bf16[128,16,128]{2,1,0:T(8,128)(2,1)}), bf16[128,16,128]{2,1,0:T(8,128)(2,1)S(1)}, u32[]{:S(2)}, u32[]{:S(2)}) %all-to-all-start.5) | async-done | bytes 524320 | tf_op jit(solution)/shard_map/all_to_all | solution.py:22
  158.8 0.6 broadcast_in_dim.36
  159.4 5.6 %all-to-all-start.6 = ((bf16[16,16,128]{2,1,0:T(8,128)(2,1)}), bf16[16,16,128]{2,1,0:T(8,128)(2,1)}, u32[]{:S(2)}, u32[]{:S(2)}) async-start(bf16[16,16,128]{2,1,0:T(8,128)(2,1)} %broadcast_in_dim.36), calls=%async_computation.6 | async-start | bytes 131072 | tf_op jit(solution)/shard_map/all_to_all | solution.py:22
  165.0 7.3 %all-to-all-done.6 = bf16[16,16,128]{2,1,0:T(8,128)(2,1)} async-done(((bf16[16,16,128]{2,1,0:T(8,128)(2,1)}), bf16[16,16,128]{2,1,0:T(8,128)(2,1)}, u32[]{:S(2)}, u32[]{:S(2)}) %all-to-all-start.6) | async-done | bytes 65568 | tf_op jit(solution)/shard_map/all_to_all | solution.py:22
  172.3 2.3 multiply_convert_fusion.1
  174.6 2.2 fusion.24
  176.9 2.3 fusion.3
  179.4 0.7 pad_maximum_fusion
  180.1 3.5 %all-to-all-start.7 = ((bf16[16,24,128]{2,1,0:T(8,128)(2,1)}), bf16[16,24,128]{2,1,0:T(8,128)(2,1)S(1)}, u32[]{:S(2)}, u32[]{:S(2)}) async-start(bf16[16,24,128]{2,1,0:T(8,128)(2,1)} %pad_maximum_fusion), calls=%async_computation.7 | async-start | bytes 196608 | tf_op jit(solution)/shard_map/all_to_all | solution.py:22
  183.6 7.5 %all-to-all-done.7 = bf16[16,24,128]{2,1,0:T(8,128)(2,1)S(1)} async-done(((bf16[16,24,128]{2,1,0:T(8,128)(2,1)}), bf16[16,24,128]{2,1,0:T(8,128)(2,1)S(1)}, u32[]{:S(2)}, u32[]{:S(2)}) %all-to-all-start.7) | async-done | bytes 98336 | tf_op jit(solution)/shard_map/all_to_all | solution.py:22
  191.1 6.8 %all-to-all-start.9 = ((bf16[16,16,128]{2,1,0:T(8,128)(2,1)}), bf16[16,16,128]{2,1,0:T(8,128)(2,1)S(1)}, u32[]{:S(2)}, u32[]{:S(2)}) async-start(bf16[16,16,128]{2,1,0:T(8,128)(2,1)} %all-to-all-done.6), calls=%async_computation.9 | async-start | bytes 131072 | tf_op jit(solution)/shard_map/all_to_all | solution.py:22
  197.9 7.8 %all-to-all-done.9 = bf16[16,16,128]{2,1,0:T(8,128)(2,1)S(1)} async-done(((bf16[16,16,128]{2,1,0:T(8,128)(2,1)}), bf16[16,16,128]{2,1,0:T(8,128)(2,1)S(1)}, u32[]{:S(2)}, u32[]{:S(2)}) %all-to-all-start.9) | async-done | bytes 65568 | tf_op jit(solution)/shard_map/all_to_all | solution.py:22
  205.7 0.9 broadcast_in_dim.38
  206.6 3.5 %all-to-all-start.8 = ((bf16[16,16,1024]{2,1,0:T(8,128)(2,1)}), bf16[16,16,1024]{2,1,0:T(8,128)(2,1)S(1)}, u32[]{:S(2)}, u32[]{:S(2)}) async-start(bf16[16,16,1024]{2,1,0:T(8,128)(2,1)} %broadcast_in_dim.38), calls=%async_computation.8 | async-start | bytes 1048576 | tf_op jit(solution)/shard_map/all_to_all | solution.py:22
  210.1 2.3 collective-permute-start.2
  212.4 0.9 fusion.2
  213.3 2.1 collective-permute-done.2
  215.4 0.7 fusion.13
  216.1 10.6 %all-to-all-done.8 = bf16[16,16,1024]{2,1,0:T(8,128)(2,1)S(1)} async-done(((bf16[16,16,1024]{2,1,0:T(8,128)(2,1)}), bf16[16,16,1024]{2,1,0:T(8,128)(2,1)S(1)}, u32[]{:S(2)}, u32[]{:S(2)}) %all-to-all-start.8) | async-done | bytes 524320 | tf_op jit(solution)/shard_map/all_to_all | solution.py:22
  226.6 0.9 convolution_convert_fusion.2
  227.5 0.9 convolution_convert_fusion.3
  (62 shorter events, 1.4 us)
Async XLA Ops:
  7.2 157.8 %all-gather.9.cloned.1.call-start = ((), (), s32[]{:S(2)}) async-start(), calls=%async_computation.12 | async-start | bytes 2228224 | tf_op jit(solution)/shard_map/all_gather | solution.py:132
  9.2 15.3 %all-to-all-start = ((bf16[16,16,128]{2,1,0:T(8,128)(2,1)}), bf16[16,16,128]{2,1,0:T(8,128)(2,1)S(1)}, u32[]{:S(2)}, u32[]{:S(2)}) async-start(bf16[16,16,128]{2,1,0:T(8,128)(2,1)} %broadcast_in_dim.30), calls=%async_computation | async-start | bytes 131072 | tf_op jit(solution)/shard_map/all_to_all | solution.py:22
  17.2 157.4 %all-gather.5.cloned.1.call-start = ((), (), s32[]{:S(2)}) async-start(), calls=%async_computation.10 | async-start | bytes 2228224 | tf_op jit(solution)/shard_map/all_gather | solution.py:130
  63.0 16.5 %copy-start.5 = (bf16[512,128]{1,0:T(8,128)(2,1)S(1)}, bf16[512,128]{1,0:T(8,128)(2,1)}, u32[]{:S(2)}) copy-start(bf16[512,128]{1,0:T(8,128)(2,1)} %param.15) | copy-start | bytes 393220
  63.0 27.1 %copy-start.6 = (bf16[16,128]{1,0:T(8,128)(2,1)S(1)}, bf16[16,128]{1,0:T(8,128)(2,1)}, u32[]{:S(2)}) copy-start(bf16[16,128]{1,0:T(8,128)(2,1)} %param.10) | copy-start | bytes 12292
  63.0 27.1 %copy-start.10 = (f32[128]{0:T(128)S(1)}, f32[128]{0:T(128)}, u32[]{:S(2)}) copy-start(f32[128]{0:T(128)} %param.12) | copy-start | bytes 1540
  63.1 1.0 copy-start.4
  64.1 0.5 copy-start.11
  64.1 57.7 %copy-start = (bf16[1,2048,256]{2,1,0:T(8,128)(2,1)S(1)}, bf16[1,2048,256]{2,1,0:T(8,128)(2,1)}, u32[]{:S(2)}) copy-start(bf16[1,2048,256]{2,1,0:T(8,128)(2,1)} %param.16) | copy-start | bytes 3145732
  64.1 57.8 %copy-start.1 = (bf16[1,2048,256]{2,1,0:T(8,128)(2,1)S(1)}, bf16[1,2048,256]{2,1,0:T(8,128)(2,1)}, u32[]{:S(2)}) copy-start(bf16[1,2048,256]{2,1,0:T(8,128)(2,1)} %param.17) | copy-start | bytes 3145732
  64.1 57.8 %copy-start.2 = (bf16[1,1024,256]{2,1,0:T(8,128)(2,1)S(1)}, bf16[1,1024,256]{2,1,0:T(8,128)(2,1)}, u32[]{:S(2)}) copy-start(bf16[1,1024,256]{2,1,0:T(8,128)(2,1)} %param.18) | copy-start | bytes 1572868
  64.6 14.9 %copy-start.8 = (f32[16]{0:T(128)}, f32[16]{0:T(128)S(1)}, u32[]{:S(2)}) copy-start(f32[16]{0:T(128)S(1)} %add_rsqrt_fusion) | copy-start | bytes 196
  91.0 25.3 %all-to-all-start.4 = ((bf16[128,16,128]{2,1,0:T(8,128)(2,1)}), bf16[128,16,128]{2,1,0:T(8,128)(2,1)S(1)}, u32[]{:S(2)}, u32[]{:S(2)}) async-start(bf16[128,16,128]{2,1,0:T(8,128)(2,1)} %broadcast_in_dim.34), calls=%async_computation.4 | async-start | bytes 1048576 | tf_op jit(solution)/shard_map/all_to_all | solution.py:22
  97.2 79.7 %all-gather.7.cloned.1.call-start = ((), (), s32[]{:S(2)}) async-start(), calls=%async_computation.11 | async-start | bytes 2228224 | tf_op jit(solution)/shard_map/all_gather | solution.py:131
  116.3 5.5 %collective-permute-start = (bf16[8,256,128]{2,1,0:T(8,128)(2,1)S(1)}, bf16[8,256,128]{2,1,0:T(8,128)(2,1)}, u32[]{:S(2)}, u32[]{:S(2)}) collective-permute-start(bf16[8,256,128]{2,1,0:T(8,128)(2,1)S(1)} %bitcast.63), channel_id=1, source_target_pairs={{0,32},{32,0},{1,33},{33,1},{2,34},{34,2},{3,35},{35,3},{4,36},{36... | collective-permute-start | bytes 1572872 | tf_op jit(solution)/shard_map/ppermute | solution.py:30
  121.8 1.0 copy-start.3
  128.1 44.2 %copy-start.9 = (f32[16]{0:T(128)S(1)}, f32[16]{0:T(128)}, u32[]{:S(2)}) copy-start(f32[16]{0:T(128)} %copy-done.8) | copy-start | bytes 196
  128.1 3.8 %collective-permute-start.1 = (bf16[8,16,16,128]{3,2,1,0:T(8,128)(2,1)S(1)}, bf16[8,16,16,128]{3,2,1,0:T(8,128)(2,1)S(1)}, u32[]{:S(2)}, u32[]{:S(2)}) collective-permute-start(bf16[8,16,16,128]{3,2,1,0:T(8,128)(2,1)S(1)} %get-tuple-element.10), channel_id=1, source_target_pairs={{0,32},{32,0},{1,33},{33,1},{2,34},{34,2},{3,35},{35,3},{4,36},{36... | collective-permute-start | bytes 1572872 | tf_op jit(solution)/shard_map/ppermute | solution.py:30
  132.9 25.8 %all-to-all-start.5 = ((bf16[128,16,128]{2,1,0:T(8,128)(2,1)}), bf16[128,16,128]{2,1,0:T(8,128)(2,1)S(1)}, u32[]{:S(2)}, u32[]{:S(2)}) async-start(bf16[128,16,128]{2,1,0:T(8,128)(2,1)} %bitcast.16), calls=%async_computation.5 | async-start | bytes 1048576 | tf_op jit(solution)/shard_map/all_to_all | solution.py:22
  159.4 12.9 %all-to-all-start.6 = ((bf16[16,16,128]{2,1,0:T(8,128)(2,1)}), bf16[16,16,128]{2,1,0:T(8,128)(2,1)}, u32[]{:S(2)}, u32[]{:S(2)}) async-start(bf16[16,16,128]{2,1,0:T(8,128)(2,1)} %broadcast_in_dim.36), calls=%async_computation.6 | async-start | bytes 131072 | tf_op jit(solution)/shard_map/all_to_all | solution.py:22
  174.6 4.7 %copy-start.12 = (f32[16]{0:T(128)S(1)}, f32[16]{0:T(128)}, u32[]{:S(2)}) copy-start(f32[16]{0:T(128)} %copy-done.11) | copy-start | bytes 196
  179.4 36.0 %copy-start.7 = (bf16[16,128]{1,0:T(8,128)(2,1)S(1)}, bf16[16,128]{1,0:T(8,128)(2,1)}, u32[]{:S(2)}) copy-start(bf16[16,128]{1,0:T(8,128)(2,1)} %param.10) | copy-start | bytes 12292
  180.1 11.0 %all-to-all-start.7 = ((bf16[16,24,128]{2,1,0:T(8,128)(2,1)}), bf16[16,24,128]{2,1,0:T(8,128)(2,1)S(1)}, u32[]{:S(2)}, u32[]{:S(2)}) async-start(bf16[16,24,128]{2,1,0:T(8,128)(2,1)} %pad_maximum_fusion), calls=%async_computation.7 | async-start | bytes 196608 | tf_op jit(solution)/shard_map/all_to_all | solution.py:22
  191.1 14.6 %all-to-all-start.9 = ((bf16[16,16,128]{2,1,0:T(8,128)(2,1)}), bf16[16,16,128]{2,1,0:T(8,128)(2,1)S(1)}, u32[]{:S(2)}, u32[]{:S(2)}) async-start(bf16[16,16,128]{2,1,0:T(8,128)(2,1)} %all-to-all-done.6), calls=%async_computation.9 | async-start | bytes 131072 | tf_op jit(solution)/shard_map/all_to_all | solution.py:22
  206.6 20.1 %all-to-all-start.8 = ((bf16[16,16,1024]{2,1,0:T(8,128)(2,1)}), bf16[16,16,1024]{2,1,0:T(8,128)(2,1)S(1)}, u32[]{:S(2)}, u32[]{:S(2)}) async-start(bf16[16,16,1024]{2,1,0:T(8,128)(2,1)} %broadcast_in_dim.38), calls=%async_computation.8 | async-start | bytes 1048576 | tf_op jit(solution)/shard_map/all_to_all | solution.py:22
  210.1 5.3 %collective-permute-start.2 = (f32[24,128]{1,0:T(8,128)S(1)}, f32[24,128]{1,0:T(8,128)S(1)}, u32[]{:S(2)}, u32[]{:S(2)}) collective-permute-start(f32[24,128]{1,0:T(8,128)S(1)} %select_maximum_fusion), channel_id=1, source_target_pairs={{0,0},{2,32},{4,64},{6,96},{8,128},{10,160},{12,192},{14,224},{16,... | collective-permute-start | bytes 36872 | tf_op jit(solution)/shard_map/ppermute | solution.py:202
Sparse Core Ops, SparseCore 0:
  10.1 54.4 all-gather.8
  66.7 49.4 all-gather.4
  118.3 50.0 all-gather.6

commit v3 on v1

v3 whole, which is shorter than its diff:
```python
import jax
import jax.numpy as jnp
from jax import lax
from jax.experimental import pallas as pl
from jax.experimental.pallas import tpu as pltpu
from jax.sharding import Mesh
from jax.sharding import PartitionSpec as P

D = 2048
HEAD = 256
LANES = 128
EPSILON = 1e-06
BF = jnp.bfloat16
F32 = jnp.float32

ROWS = (((0,), (0,)), ((), ()))
COLS = (((1,), (1,)), ((), ()))
SECTION = ("z", "core")
WIDE = ("core", "tensor")


def exchange(pieces, axis):
    return lax.all_to_all(pieces, axis, split_axis=0, concat_axis=0, tiled=True)


def other_core(value):
    return lax.ppermute(value, "core", [(0, 1), (1, 0)])


def dot(left, right, dims=(((1,), (0,)), ((), ()))):
    return lax.dot_general(left, right, dims, preferred_element_type=F32)


def in_thirds(value):
    high = value.astype(BF).astype(F32)
    middle = (value - high).astype(BF).astype(F32)
    return high, middle, value - high - middle


def in_two_lanes(column):
    lane = lax.broadcasted_iota(jnp.int32, (column.shape[0], LANES), 1)
    high = column.astype(BF).astype(F32)
    return jnp.where(lane == 0, high, jnp.where(lane == 1, column - high, 0.0)).astype(BF)


def from_two_lanes(tile):
    lane = lax.broadcasted_iota(jnp.int32, tile.shape, 1)
    return jnp.sum(jnp.where(lane < 2, tile, 0.0), axis=1, keepdims=True)


def half_of(core, half):
    return pl.ds(pl.multiple_of(core * half, half), half)


def start(core_ref, x_ref, mlp_ref, final_ref, gate_ref, up_ref, down_ref, copies_ref, sent_ref):
    half = gate_ref.shape[1] // 2
    feats = gate_ref.shape[0]
    quarter = half // 4
    there = half_of(1 - core_ref[0], half)
    for i in range(copies_ref.shape[0]):
        copies_ref[i] = x_ref[...]
    sent_ref[:feats, :half] = gate_ref[:, there]
    sent_ref[:feats, half:] = up_ref[:, there]
    for i in range(4):
        at = pl.ds(pl.multiple_of((1 - core_ref[0]) * half + i * quarter, quarter), quarter)
        sent_ref[feats : feats + quarter, i * LANES : (i + 1) * LANES] = down_ref[at, :]
    row = lax.broadcasted_iota(jnp.int32, (16, LANES), 0)
    thirds = zip(in_thirds(mlp_ref[...]), in_thirds(final_ref[...]))
    for i, (mlp, final) in enumerate(thirds):
        tile = jnp.where(row == 0, mlp, jnp.where(row == 1, final, 0.0))
        sent_ref[feats + quarter :, i * LANES : (i + 1) * LANES] = tile.astype(BF)
    sent_ref[feats + quarter :, 3 * LANES :] = jnp.zeros((16, LANES), BF)


def got_gains(got_ref, rows):
    tile = got_ref[rows : rows + 16, :].astype(F32)
    tile = tile[:, :LANES] + tile[:, LANES : 2 * LANES] + tile[:, 2 * LANES : 3 * LANES]
    return tile[0:1], tile[1:2]


def gate_up(core_ref, x_ref, mlp_ref, gate_ref, up_ref, got_ref, pieces_ref, scaled_ref):
    core = core_ref[0]
    half = gate_ref.shape[1] // 2
    feats = gate_ref.shape[0]
    here = half_of(core, half)
    x_here = x_ref[core].astype(F32)
    x_there = x_ref[1 - core].astype(F32)
    scaled = (x_here * mlp_ref[...]).astype(BF)
    scaled_ref[...] = scaled
    mlp_there, _ = got_gains(got_ref, feats + half // 4)
    scaled_there = (x_there * mlp_there).astype(BF)
    gate = dot(scaled, gate_ref[:, here]) + dot(scaled_there, got_ref[:feats, :half])
    up = dot(scaled, up_ref[:, here]) + dot(scaled_there, got_ref[:feats, half:])
    square = jnp.sum(x_here * x_here + x_there * x_there, axis=1, keepdims=True)
    shape = pieces_ref.shape[:2]
    pieces_ref[:, :, :half] = gate.astype(BF).reshape(*shape, half)
    pieces_ref[:, :, half : 2 * half] = up.astype(BF).reshape(*shape, half)
    pieces_ref[:, :, 2 * half :] = in_two_lanes(square).reshape(*shape, LANES)


def activate(core_ref, arrived_ref, final_ref, got_ref, copies_ref, gate_f_ref, up_f_ref, inner_f_ref):
    core = core_ref[0]
    pieces, share, half = copies_ref.shape
    share = share - 16
    total = arrived_ref[0].astype(F32)
    for i in range(1, pieces):
        total += arrived_ref[i].astype(F32)
    inv = lax.rsqrt(from_two_lanes(total[:, 2 * half :]) * (1.0 / D) + EPSILON)
    gate_pre = total[:, :half] * inv
    up_pre = total[:, half : 2 * half] * inv
    sigmoid_gate = jax.nn.sigmoid(gate_pre)
    activated = gate_pre * sigmoid_gate
    hidden_act = (activated * up_pre).astype(BF)
    gate_factor = up_pre * sigmoid_gate * (1.0 + gate_pre * (1.0 - sigmoid_gate))
    gate_f_ref[...] = gate_factor * inv
    up_f_ref[...] = activated * inv
    inner_f_ref[...] = (gate_factor * gate_pre + activated * up_pre) * (inv * inv * (1.0 / D))
    _, final_there = got_gains(got_ref, got_ref.shape[0] - 16)
    final_here = final_ref[...]
    first = core == 0
    low = in_thirds(jnp.where(first, final_here, final_there))
    high = in_thirds(jnp.where(first, final_there, final_here))
    row = lax.broadcasted_iota(jnp.int32, (16, LANES), 0)
    tiles = []
    for parts in (low, high):
        tile = jnp.where(row == 0, parts[0], jnp.where(row == 1, parts[1], 0.0))
        tiles.append(jnp.where(row == 2, parts[2], tile).astype(BF))
    gains = jnp.concatenate(tiles, axis=1)
    for i in range(pieces):
        copies_ref[i, :share] = hidden_act
        copies_ref[i, share:] = gains


def down_half(got_ref, feats, half):
    quarter = half // 4
    rows = got_ref[feats : feats + quarter, :]
    return jnp.concatenate([rows[:, i * LANES : (i + 1) * LANES] for i in range(4)], axis=0)


def mix(core_ref, act_ref, down_ref, got_ref, pieces_ref, recip_ref):
    core = core_ref[0]
    pieces, share, half = act_ref.shape
    share = share - 16
    feats = down_ref.shape[1]
    act = act_ref[:, :share].reshape(pieces * share, half)
    shape = pieces_ref.shape[1:]
    here = dot(act, down_ref[half_of(core, half), :])
    pieces_ref[core] = here.astype(BF).reshape(shape)
    there = dot(act, down_half(got_ref, feats, half))
    pieces_ref[1 - core] = there.astype(BF).reshape(shape)
    for z in range(pieces):
        tile = act_ref[z, share:].astype(F32)
        recip = 1.0 / (tile[0:1] + tile[1:2] + tile[2:3])
        recip_ref[z, 0] = recip[:, :LANES]
        recip_ref[z, 1] = recip[:, LANES:]


def finish_outer(arrived_ref, x_ref, final_ref, copies_ref):
    total = x_ref[...].astype(F32)
    for i in range(arrived_ref.shape[0]):
        total += arrived_ref[i].astype(F32)
    scaled = (total * final_ref[...]).astype(BF)
    for i in range(copies_ref.shape[0]):
        copies_ref[i] = scaled


def attend(core_ref, mine_ref, other_ref, wk_ref, wv_ref, recip_ref, q_ref, g_ref, qg_ref, keep_ref, send_ref):
    core = core_ref[0]
    pairs = mine_ref.shape[0]
    rows = mine_ref.shape[1]
    scale = HEAD ** (-0.5)
    keys_raw = jnp.zeros((rows, HEAD), F32)
    values_raw = jnp.zeros((rows, HEAD), F32)
    square = jnp.zeros((rows, 1), F32)
    for z in range(pairs):
        for block_ref, side in ((mine_ref, core), (other_ref, 1 - core)):
            block = block_ref[z]
            keys_raw += dot(block, wk_ref[z, side])
            values_raw += dot(block, wv_ref[z, side])
            wide = block.astype(F32) * recip_ref[z, side]
            square += jnp.sum(wide * wide, axis=1, keepdims=True)
    inv_out = lax.rsqrt(square / D + EPSILON)
    keys = (keys_raw * inv_out).astype(BF)
    values = (values_raw * inv_out).astype(BF)
    key_grad = jnp.zeros((rows, HEAD), F32)
    value_grad = jnp.zeros((rows, HEAD), F32)
    step = 256
    for at in range(0, q_ref.shape[0], step):
        query = q_ref[at : at + step, :]
        grad = g_ref[at : at + step, :]
        scores = dot(keys, query, COLS) * scale
        raised = jnp.exp(scores - jnp.max(scores, axis=0, keepdims=True))
        probs = raised / jnp.sum(raised, axis=0, keepdims=True)
        probs_bf = probs.astype(BF)
        dprob = dot(values, grad, COLS)
        delta = jnp.sum(probs_bf.astype(F32) * dprob, axis=0, keepdims=True)
        dscore = (probs * (dprob - delta) * scale).astype(BF)
        qg_ref[at : at + step, :] = dot(dscore, keys, ROWS).astype(BF)
        key_grad += dot(dscore, query)
        value_grad += dot(probs_bf, grad)
    key_grad = key_grad.astype(BF)
    value_grad = value_grad.astype(BF)
    inner = jnp.sum(
        key_grad.astype(F32) * keys_raw + value_grad.astype(F32) * values_raw, axis=1, keepdims=True
    )
    along = inv_out * inv_out * inv_out * inner * (1.0 / D)
    for z in range(pairs):
        for block_ref, out_ref, side in ((mine_ref, keep_ref, core), (other_ref, send_ref, 1 - core)):
            total = dot(key_grad, wk_ref[z, side], COLS) + dot(value_grad, wv_ref[z, side], COLS)
            recip = recip_ref[z, side]
            term = inv_out * total - block_ref[z].astype(F32) * (recip * recip) * along
            out_ref[z] = term.astype(out_ref.dtype)


def outer_gradient(arrived_ref, final_ref, grad_ref, copies_ref):
    totals = [arrived_ref[i].astype(F32) for i in range(8)]
    for i in range(8, arrived_ref.shape[0]):
        totals[i % 8] += arrived_ref[i].astype(F32)
    total = sum(totals[1:], totals[0]) * final_ref[...]
    grad_ref[...] = total
    rounded = total.astype(BF)
    for i in range(copies_ref.shape[0]):
        copies_ref[i] = rounded


def through_down(core_ref, outer_ref, down_ref, got_ref, pieces_ref):
    core = core_ref[0]
    feats = down_ref.shape[1]
    half = down_ref.shape[0] // 2
    part = dot(outer_ref[core], down_ref[half_of(core, half), :], COLS)
    part += dot(outer_ref[1 - core], down_half(got_ref, feats, half), COLS)
    pieces_ref[...] = part.astype(BF).reshape(pieces_ref.shape)


def gate_up_gradient(arrived_ref, gate_f_ref, up_f_ref, inner_f_ref, copies_ref):
    half = gate_f_ref.shape[1]
    total = arrived_ref[0].astype(F32)
    for i in range(1, arrived_ref.shape[0]):
        total += arrived_ref[i].astype(F32)
    gate = (total * gate_f_ref[...]).astype(BF)
    up = (total * up_f_ref[...]).astype(BF)
    inner = in_two_lanes(jnp.sum(total * inner_f_ref[...], axis=1, keepdims=True))
    for i in range(copies_ref.shape[0]):
        copies_ref[i, :, :half] = gate
        copies_ref[i, :, half : 2 * half] = up
        copies_ref[i, :, 2 * half :] = inner


def through_gate_up(core_ref, grads_ref, x_ref, mlp_ref, gate_ref, up_ref, got_ref, pieces_ref):
    core = core_ref[0]
    half = gate_ref.shape[1] // 2
    feats = gate_ref.shape[0]
    here = half_of(core, half)
    tokens = x_ref.shape[1]
    shape = pieces_ref.shape[1:]
    gate = grads_ref[:, :, :half].reshape(tokens, half)
    up = grads_ref[:, :, half : 2 * half].reshape(tokens, half)
    inner = from_two_lanes(grads_ref[:, :, 2 * half :].astype(F32).reshape(tokens, LANES))
    part = dot(gate, gate_ref[:, here], COLS) + dot(up, up_ref[:, here], COLS)
    part = part * mlp_ref[...] - x_ref[core].astype(F32) * inner
    pieces_ref[core] = part.astype(BF).reshape(shape)
    mlp_there, _ = got_gains(got_ref, feats + half // 4)
    part = dot(gate, got_ref[:feats, :half], COLS) + dot(up, got_ref[:feats, half:], COLS)
    part = part * mlp_there - x_ref[1 - core].astype(F32) * inner
    pieces_ref[1 - core] = part.astype(BF).reshape(shape)


def gate_up_weights(core_ref, scaled_ref, here_ref, there_ref, gate_ref, up_ref):
    core = core_ref[0]
    half = gate_ref.shape[1] // 2
    tokens = scaled_ref.shape[0]
    scaled = scaled_ref[...]
    for grads_ref, place in ((here_ref, core), (there_ref, 1 - core)):
        at = half_of(place, half)
        gate_ref[:, at] = dot(scaled, grads_ref[:, :, :half].reshape(tokens, half), ROWS).astype(BF)
        up = grads_ref[:, :, half : 2 * half].reshape(tokens, half)
        up_ref[:, at] = dot(scaled, up, ROWS).astype(BF)


def down_weights(core_ref, outer_ref, here_ref, there_ref, down_ref):
    core = core_ref[0]
    half = down_ref.shape[0] // 2
    tokens = outer_ref.shape[1]
    share = here_ref.shape[1] - 16
    outer = outer_ref[core]
    for act_ref, place in ((here_ref, core), (there_ref, 1 - core)):
        act = act_ref[:, :share].reshape(tokens, half)
        down_ref[half_of(place, half), :] = dot(act, outer, ROWS).astype(BF)


def call(body, outs, *args, flops=0):
    vmem = pl.BlockSpec(memory_space=pltpu.VMEM)
    in_specs = [vmem] * len(args)
    if args[0].dtype == jnp.int32:
        in_specs[0] = pl.BlockSpec(memory_space=pltpu.SMEM)
    shapes = tuple(jax.ShapeDtypeStruct(shape, dtype) for shape, dtype in outs)
    moved = sum(a.size * a.dtype.itemsize for a in (*args, *shapes))
    results = pl.pallas_call(
        body,
        out_shape=shapes,
        in_specs=in_specs,
        out_specs=(vmem,) * len(shapes),
        compiler_params=pltpu.CompilerParams(vmem_limit_bytes=40 * 1024 * 1024),
        cost_estimate=pl.CostEstimate(flops=flops, bytes_accessed=moved, transcendentals=0),
    )(*args)
    return results


def on_device(
    enc_hidden,
    mlp_gain,
    final_gain,
    w_gate,
    w_up,
    w_down,
    key_weight,
    value_weight,
    queries,
    context_grad,
):
    block, feats = enc_hidden.shape
    half = w_gate.shape[1] // 2
    core = lax.axis_index("core").astype(jnp.int32).reshape(1)
    chips = lax.axis_size("z")
    blocks = lax.axis_size("tensor")
    tokens = block * blocks
    share = tokens // chips
    mlp_gain = mlp_gain.reshape(1, feats)
    final_gain = final_gain.reshape(1, feats)

    copies, sent = call(
        start,
        [((2 * blocks, block, feats), BF), ((feats + half // 4 + 16, 2 * half), BF)],
        core, enc_hidden, mlp_gain, final_gain, w_gate, w_up, w_down,
    )
    hidden = exchange(copies, WIDE).reshape(2, tokens, feats)
    got = other_core(sent)
    pieces, scaled = call(
        gate_up,
        [((chips, share, 2 * half + LANES), BF), ((tokens, feats), BF)],
        core, hidden, mlp_gain, w_gate, w_up, got,
    )
    arrived = exchange(pieces, "z")
    copies, gate_f, up_f, inner_f = call(
        activate,
        [((chips, share + 16, half), BF)] + [((share, half), F32)] * 3,
        core, arrived, final_gain, got,
    )
    act = exchange(copies, "z")
    act_there = other_core(act)
    pieces, recip = call(
        mix,
        [((2, blocks, block, feats), BF), ((chips, 2, 1, LANES), F32)],
        core, act, w_down, got,
    )
    arrived = exchange(pieces.reshape(-1, block, feats), WIDE)
    (copies,) = call(
        finish_outer, [((chips * blocks, block, feats), BF)], arrived, enc_hidden, final_gain
    )
    mine = exchange(copies, ("z", "tensor")).reshape(chips, tokens, feats)
    other = other_core(mine)
    by_block = (chips, 2, LANES, HEAD)
    query_grad, keep, send = call(
        attend,
        [(queries.shape[1:], BF), (mine.shape, F32), (mine.shape, BF)],
        core, mine, other, key_weight.reshape(by_block), value_weight.reshape(by_block), recip,
        queries[0], context_grad[0],
        flops=3_500_000_000,
    )
    both = (keep + other_core(send).astype(F32)).astype(BF)
    arrived = exchange(both.reshape(-1, block, feats), ("z", "tensor"))
    outer_grad, copies = call(
        outer_gradient,
        [((block, feats), F32), ((2 * blocks, block, feats), BF)],
        arrived, final_gain,
    )
    outer = exchange(copies, WIDE).reshape(2, tokens, feats)
    (pieces,) = call(through_down, [((chips, share, half), BF)], core, outer, w_down, got)
    arrived = exchange(pieces, "z")
    (down_weight_grad,) = call(down_weights, [(w_down.shape, BF)], core, outer, act, act_there)
    (copies,) = call(
        gate_up_gradient, [((chips, share, 2 * half + LANES), BF)], arrived, gate_f, up_f, inner_f
    )
    grads = exchange(copies, "z")
    grads_there = other_core(grads)
    (pieces,) = call(
        through_gate_up,
        [((2, blocks, block, feats), BF)],
        core, grads, hidden, mlp_gain, w_gate, w_up, got,
    )
    arrived = exchange(pieces.reshape(-1, block, feats), WIDE)
    gate_weight_grad, up_weight_grad = call(
        gate_up_weights,
        [(w_gate.shape, BF), (w_up.shape, BF)],
        core, scaled, grads, grads_there,
    )
    hidden_grad = outer_grad + arrived.astype(F32).sum(axis=0)
    return (query_grad[None], hidden_grad, gate_weight_grad, up_weight_grad, down_weight_grad)


def solution(mesh):
    names = list(mesh.axis_names)
    at = names.index("section")
    shape = list(mesh.devices.shape)
    names[at : at + 1] = SECTION
    shape[at : at + 1] = [shape[at] // 2, 2]
    fine = Mesh(mesh.devices.reshape(shape), tuple(names))
    in_specs = (
        P(("dp", "tensor"), SECTION),
        P(SECTION),
        P(SECTION),
        P(SECTION, "tensor"),
        P(SECTION, "tensor"),
        P("tensor", SECTION),
        P(SECTION, None, "tensor"),
        P(SECTION, None, "tensor"),
        P(SECTION, "dp", "tensor"),
        P(SECTION, "dp", "tensor"),
    )
    out_specs = (
        P(SECTION, "dp", "tensor"),
        P(("dp", "tensor"), SECTION),
        P(("dp", *SECTION), "tensor"),
        P(("dp", *SECTION), "tensor"),
        P(("dp", "tensor"), SECTION),
    )
    return jax.shard_map(
        on_device, mesh=fine, in_specs=in_specs, out_specs=out_specs, check_vma=False
    )
```

time: 209 us -> 192 us (0.919)
  waiting for transfers between devices: 32.1 us -> 12.2 us
  starting transfers between devices: 21.1 us -> 31.9 us
  matrix products: 6.39 us -> 0 us
  Pallas kernels: 5.88 us -> 9.47 us
  other arithmetic: 4.09 us -> 0.74 us
    all_to_all x3 -> x2, waiting for transfers between devices: 29.8 us -> 6.86 us  [exchange(): return lax.all_to_all(pieces, axis, split_axis=0, concat_axis=0, tiled=True)]
    ppermute x2 -> x5, starting transfers between devices: 6.11 us -> 12.7 us  [other_core(): return lax.ppermute(value, 'core', [(0, 1), (1, 0)])]
    dot_general x9 -> x0, matrix products: 6.39 us -> none  [the longest x1 1.11 us: on_device(): up_part = jnp.dot(scaled_all, w_up, preferred_element_type=F32).astype(BF)]
    all_to_all x3 -> x2, starting transfers between devices: 15 us -> 19.3 us  [exchange(): return lax.all_to_all(pieces, axis, split_axis=0, concat_axis=0, tiled=True)]
    pallas_call x1 -> x12, Pallas kernels: 5.88 us -> 9.47 us  [call(): pl.pallas_call(body, out_shape=shapes, in_specs=in_specs, out_specs=(vmem...]
    ppermute x2 -> x5, waiting for transfers between devices: 2.28 us -> 5.37 us  [other_core(): return lax.ppermute(value, 'core', [(0, 1), (1, 0)])]
    broadcast_in_dim x6 -> x0, local copies, waits for them, and re-layouts: 2.33 us -> none  [the longest x5 2.32 us: sent_to_all(): jnp.broadcast_to(value, (lax.axis_size(axis), *value.shape))]
    unnamed x29 -> x26, local copies, waits for them, and re-layouts: 1.29 us -> 3.41 us
  transfers between devices with their start and end apart: 5 -> 7, of which waited for: 5 -> 6; matrix products, arithmetic and copies ran while one was open for 2% -> 0% of each run, Pallas kernels for 0% -> 0%
where the time goes in v3:
time: 192 us; the launch traced here: 191 us
  blocking collectives  132 us (69%)
  starting transfers between devices  31.9 us (17%)
  waiting for transfers between devices  12.2 us (6%)
  Pallas kernels  9.47 us (5%)
  local copies, waits for them, and re-layouts  3.41 us (2%)
    all_to_all x8, blocking collectives, exchange(): return lax.all_to_all(pieces, axis, split_axis=0, concat_axis=0, tiled=True)  132 us
    all_to_all x2, starting transfers between devices, exchange(): return lax.all_to_all(pieces, axis, split_axis=0, concat_axis=0, tiled=True)  19.3 us
    ppermute x5, starting transfers between devices, other_core(): return lax.ppermute(value, 'core', [(0, 1), (1, 0)])  12.7 us
    pallas_call x12, Pallas kernels, call(): pl.pallas_call(body, out_shape=shapes, in_specs=in_specs, out_specs=(vmem...  9.47 us
    all_to_all x2, waiting for transfers between devices, exchange(): return lax.all_to_all(pieces, axis, split_axis=0, concat_axis=0, tiled=True)  6.86 us
    ppermute x5, waiting for transfers between devices, other_core(): return lax.ppermute(value, 'core', [(0, 1), (1, 0)])  5.37 us
  transfers between devices with their start and end apart: 7, of which 6 were waited for; matrix products, arithmetic and copies ran while one was open for 0% of the time, Pallas kernels for 0%

profile of v3, /device:TPU:1, one launch (start us, length us, event | category | flops | bytes accessed | tf_op | source)
XLA Modules:
  0.0 190.9 jit_solution(13865264680707135163)
XLA Ops:
  0.6 0.0 copy-start.6
  0.7 0.7 copy-done.6
  1.3 0.0 copy-done.8
  1.3 0.9 copy-done
  2.2 0.9 copy-done.2
  3.1 0.9 copy-done.4
  4.0 0.7 shard_map.137
  4.7 10.6 %all-to-all-start = ((bf16[32,16,128]{2,1,0:T(8,128)(2,1)}), bf16[32,16,128]{2,1,0:T(8,128)(2,1)S(1)}, u32[]{:S(2)}, u32[]{:S(2)}) async-start(bf16[32,16,128]{2,1,0:T(8,128)(2,1)} %get-tuple-element.22), calls=%async_computation | async-start | bytes 262144 | tf_op jit(solution)/shard_map/all_to_all | solution.py:23
  15.4 2.2 %collective-permute-start = (bf16[208,512]{1,0:T(8,128)(2,1)S(1)}, bf16[208,512]{1,0:T(8,128)(2,1)S(1)}, u32[]{:S(2)}, u32[]{:S(2)}) collective-permute-start(bf16[208,512]{1,0:T(8,128)(2,1)S(1)} %get-tuple-element.23), channel_id=1, source_target_pairs={{0,32},{32,0},{1,33},{33,1},{2,34},{34,2},{3,35},{35,3},{4,36},{36... | collective-permute-start | bytes 638984 | tf_op jit(solution)/shard_map/ppermute | solution.py:27
  17.5 1.2 collective-permute-done.got_ref
  18.7 4.9 %all-to-all-done = bf16[32,16,128]{2,1,0:T(8,128)(2,1)S(1)} async-done(((bf16[32,16,128]{2,1,0:T(8,128)(2,1)}), bf16[32,16,128]{2,1,0:T(8,128)(2,1)S(1)}, u32[]{:S(2)}, u32[]{:S(2)}) %all-to-all-start) | async-done | bytes 131104 | tf_op jit(solution)/shard_map/all_to_all | solution.py:23
  23.7 0.0 copy-done.3
  23.7 0.3 shard_map.138
  24.0 19.5 %all_to_all.50.arrived_ref = bf16[8,32,640]{2,1,0:T(8,128)(2,1)S(1)} all-to-all(bf16[8,32,640]{2,1,0:T(8,128)(2,1)S(1)} %get-tuple-element.24), channel_id=1, replica_groups=mesh['z'=8,'core'=2,'tensor'=16,'dp'=2] {'z'}, dimensions={0} | all-to-all | bytes 655360 | tf_op jit(solution)/shard_map/all_to_all | solution.py:23
  43.5 0.1 shard_map.139
  43.6 0.0 copy-start.5
  43.7 0.0 copy-start.11
  43.7 12.1 %all_to_all.51.act_ref.here_ref = bf16[8,48,256]{2,1,0:T(8,128)(2,1)S(1)} all-to-all(bf16[8,48,256]{2,1,0:T(8,128)(2,1)S(1)} %get-tuple-element.25), channel_id=1, replica_groups=mesh['z'=8,'core'=2,'tensor'=16,'dp'=2] {'z'}, dimensions={0} | all-to-all | bytes 393216 | tf_op jit(solution)/shard_map/all_to_all | solution.py:23
  55.8 0.2 shard_map.140
  56.0 0.0 copy-start.9
  56.1 15.3 %all_to_all.52.arrived_ref = bf16[32,16,128]{2,1,0:T(8,128)(2,1)S(1)} all-to-all(bf16[32,16,128]{2,1,0:T(8,128)(2,1)S(1)} %bitcast.20), channel_id=1, replica_groups=mesh['z'=8,'core'=2,'tensor'=16,'dp'=2] {'core','tensor'}, dimensions={0} | all-to-all | bytes 262144 | tf_op jit(solution)/shard_map/all_to_all | solution.py:23
  71.4 0.1 shard_map.141
  71.5 24.6 %all_to_all.53 = bf16[128,16,128]{2,1,0:T(8,128)(2,1)S(1)} all-to-all(bf16[128,16,128]{2,1,0:T(8,128)(2,1)S(1)} %shard_map.141), channel_id=1, replica_groups=mesh['z'=8,'core'=2,'tensor'=16,'dp'=2] {'z','tensor'}, dimensions={0} | all-to-all | bytes 1048576 | tf_op jit(solution)/shard_map/all_to_all | solution.py:23
  96.1 3.9 %collective-permute-start.1 = (bf16[8,256,128]{2,1,0:T(8,128)(2,1)S(1)}, bf16[8,256,128]{2,1,0:T(8,128)(2,1)S(1)}, u32[]{:S(2)}, u32[]{:S(2)}) collective-permute-start(bf16[8,256,128]{2,1,0:T(8,128)(2,1)S(1)} %bitcast.18), channel_id=1, source_target_pairs={{0,32},{32,0},{1,33},{33,1},{2,34},{34,2},{3,35},{35,3},{4,36},{36... | collective-permute-start | bytes 1572872 | tf_op jit(solution)/shard_map/ppermute | solution.py:27
  100.0 1.5 collective-permute-done.1.other_ref
  101.5 0.0 copy-done.12
  101.5 0.0 copy-done.10
  101.5 4.8 %shard_map.142 = (bf16[1024,256]{1,0:T(8,128)(2,1)}, f32[8,256,128]{2,1,0:T(8,128)S(1)}, bf16[8,256,128]{2,1,0:T(8,128)(2,1)S(1)}) custom-call(s32[1]{0:T(128)} %bitcast.core_ref, bf16[8,256,128]{2,1,0:T(8,128)(2,1)S(1)} %bitcast.19, bf16[8,256,128]{2,1,0:T(8,128)(2,1)S(1)} %collective-permute-done.1.other_ref, bf16[8,2,128,256]{3,2,1,0:T(8,128)(2,1)S(1)} %bitcast.28, ...), custom_call_target="tpu_custom_call" | custom-call | flops 3500000000 | bytes 6299652 | tf_op jit(solution)/shard_map/pallas_call | solution.py:298
  106.3 2.3 %collective-permute-start.2 = (bf16[8,256,128]{2,1,0:T(8,128)(2,1)S(1)}, bf16[8,256,128]{2,1,0:T(8,128)(2,1)S(1)}, u32[]{:S(2)}, u32[]{:S(2)}) collective-permute-start(bf16[8,256,128]{2,1,0:T(8,128)(2,1)S(1)} %get-tuple-element.30), channel_id=1, source_target_pairs={{0,32},{32,0},{1,33},{33,1},{2,34},{34,2},{3,35},{35,3},{4,36},{36... | collective-permute-start | bytes 1572872 | tf_op jit(solution)/shard_map/ppermute | solution.py:27
  108.6 1.5 collective-permute-done.2
  110.1 0.1 add_convert_fusion
  110.2 24.9 %all_to_all.54.arrived_ref = bf16[128,16,128]{2,1,0:T(8,128)(2,1)S(1)} all-to-all(bf16[128,16,128]{2,1,0:T(8,128)(2,1)S(1)} %bitcast.32), channel_id=1, replica_groups=mesh['z'=8,'core'=2,'tensor'=16,'dp'=2] {'z','tensor'}, dimensions={0} | all-to-all | bytes 1048576 | tf_op jit(solution)/shard_map/all_to_all | solution.py:23
  135.1 0.1 shard_map.143
  135.2 13.4 %all_to_all.55 = bf16[32,16,128]{2,1,0:T(8,128)(2,1)S(1)} all-to-all(bf16[32,16,128]{2,1,0:T(8,128)(2,1)S(1)} %get-tuple-element.32), channel_id=1, replica_groups=mesh['z'=8,'core'=2,'tensor'=16,'dp'=2] {'core','tensor'}, dimensions={0} | all-to-all | bytes 262144 | tf_op jit(solution)/shard_map/all_to_all | solution.py:23
  148.6 0.2 shard_map.144
  148.8 10.1 %all_to_all.56.arrived_ref = bf16[8,32,256]{2,1,0:T(8,128)(2,1)S(1)} all-to-all(bf16[8,32,256]{2,1,0:T(8,128)(2,1)S(1)} %shard_map.144), channel_id=1, replica_groups=mesh['z'=8,'core'=2,'tensor'=16,'dp'=2] {'z'}, dimensions={0} | all-to-all | bytes 262144 | tf_op jit(solution)/shard_map/all_to_all | solution.py:23
  159.0 0.1 shard_map.145
  159.1 12.2 %all_to_all.57.grads_ref.here_ref = bf16[8,32,640]{2,1,0:T(8,128)(2,1)S(1)} all-to-all(bf16[8,32,640]{2,1,0:T(8,128)(2,1)S(1)} %shard_map.145), channel_id=1, replica_groups=mesh['z'=8,'core'=2,'tensor'=16,'dp'=2] {'z'}, dimensions={0} | all-to-all | bytes 655360 | tf_op jit(solution)/shard_map/all_to_all | solution.py:23
  171.3 1.0 shard_map.146
  172.3 8.6 %all-to-all-start.9 = ((bf16[32,16,128]{2,1,0:T(8,128)(2,1)}), bf16[32,16,128]{2,1,0:T(8,128)(2,1)S(1)}, u32[]{:S(2)}, u32[]{:S(2)}) async-start(bf16[32,16,128]{2,1,0:T(8,128)(2,1)} %bitcast.13), calls=%async_computation.9 | async-start | bytes 262144 | tf_op jit(solution)/shard_map/all_to_all | solution.py:23
  180.9 2.1 %collective-permute-start.3 = (bf16[8,32,640]{2,1,0:T(8,128)(2,1)S(1)}, bf16[8,32,640]{2,1,0:T(8,128)(2,1)S(1)}, u32[]{:S(2)}, u32[]{:S(2)}) collective-permute-start(bf16[8,32,640]{2,1,0:T(8,128)(2,1)S(1)} %all_to_all.57.grads_ref.here_ref), channel_id=1, source_target_pairs={{0,32},{32,0},{1,33},{33,1},{2,34},{34,2},{3,35},{35,3},{4,36},{36... | collective-permute-start | bytes 983048 | tf_op jit(solution)/shard_map/ppermute | solution.py:27
  183.1 2.2 %collective-permute-start.4 = (bf16[8,48,256]{2,1,0:T(8,128)(2,1)S(1)}, bf16[8,48,256]{2,1,0:T(8,128)(2,1)S(1)}, u32[]{:S(2)}, u32[]{:S(2)}) collective-permute-start(bf16[8,48,256]{2,1,0:T(8,128)(2,1)S(1)} %all_to_all.51.act_ref.here_ref), channel_id=1, source_target_pairs={{0,32},{32,0},{1,33},{33,1},{2,34},{34,2},{3,35},{35,3},{4,36},{36... | collective-permute-start | bytes 589832 | tf_op jit(solution)/shard_map/ppermute | solution.py:27
  185.3 1.1 collective-permute-done.4.there_ref
  186.4 0.9 shard_map.148
  187.3 1.9 %all-to-all-done.9 = bf16[32,16,128]{2,1,0:T(8,128)(2,1)S(1)} async-done(((bf16[32,16,128]{2,1,0:T(8,128)(2,1)}), bf16[32,16,128]{2,1,0:T(8,128)(2,1)S(1)}, u32[]{:S(2)}, u32[]{:S(2)}) %all-to-all-start.9) | async-done | bytes 131104 | tf_op jit(solution)/shard_map/all_to_all | solution.py:23
  189.3 0.6 add.7
  189.9 0.0 collective-permute-done.3.there_ref
  189.9 1.0 shard_map.147
  (15 shorter events, 0.1 us)
Async XLA Ops:
  0.6 0.7 copy-start.6
  0.6 0.7 copy-start.7
  0.7 0.7 copy-start.8
  1.3 0.9 copy-start
  2.2 0.9 copy-start.2
  3.1 0.9 copy-start.4
  4.7 18.9 %copy-start.1 = (bf16[128,512]{1,0:T(8,128)(2,1)S(1)}, bf16[128,512]{1,0:T(8,128)(2,1)}, u32[]{:S(2)}) copy-start(bf16[128,512]{1,0:T(8,128)(2,1)} %gate_ref.5) | copy-start | bytes 393220
  4.7 18.9 %copy-start.3 = (bf16[128,512]{1,0:T(8,128)(2,1)S(1)}, bf16[128,512]{1,0:T(8,128)(2,1)}, u32[]{:S(2)}) copy-start(bf16[128,512]{1,0:T(8,128)(2,1)} %up_ref.5) | copy-start | bytes 393220
  4.7 18.9 %all-to-all-start = ((bf16[32,16,128]{2,1,0:T(8,128)(2,1)}), bf16[32,16,128]{2,1,0:T(8,128)(2,1)S(1)}, u32[]{:S(2)}, u32[]{:S(2)}) async-start(bf16[32,16,128]{2,1,0:T(8,128)(2,1)} %get-tuple-element.22), calls=%async_computation | async-start | bytes 262144 | tf_op jit(solution)/shard_map/all_to_all | solution.py:23
  15.4 3.4 %collective-permute-start = (bf16[208,512]{1,0:T(8,128)(2,1)S(1)}, bf16[208,512]{1,0:T(8,128)(2,1)S(1)}, u32[]{:S(2)}, u32[]{:S(2)}) collective-permute-start(bf16[208,512]{1,0:T(8,128)(2,1)S(1)} %get-tuple-element.23), channel_id=1, source_target_pairs={{0,32},{32,0},{1,33},{33,1},{2,34},{34,2},{3,35},{35,3},{4,36},{36... | collective-permute-start | bytes 638984 | tf_op jit(solution)/shard_map/ppermute | solution.py:27
  43.5 58.0 %copy-start.12 = (bf16[1,1024,256]{2,1,0:T(8,128)(2,1)S(1)}, bf16[1,1024,256]{2,1,0:T(8,128)(2,1)}, u32[]{:S(2)}) copy-start(bf16[1,1024,256]{2,1,0:T(8,128)(2,1)} %param.19) | copy-start | bytes 1572868
  43.6 12.2 %copy-start.5 = (bf16[512,128]{1,0:T(8,128)(2,1)S(1)}, bf16[512,128]{1,0:T(8,128)(2,1)}, u32[]{:S(2)}) copy-start(bf16[512,128]{1,0:T(8,128)(2,1)} %down_ref.5) | copy-start | bytes 393220
  43.7 57.8 %copy-start.11 = (bf16[1,1024,256]{2,1,0:T(8,128)(2,1)S(1)}, bf16[1,1024,256]{2,1,0:T(8,128)(2,1)}, u32[]{:S(2)}) copy-start(bf16[1,1024,256]{2,1,0:T(8,128)(2,1)} %param.18) | copy-start | bytes 1572868
  55.8 45.7 %copy-start.10 = (bf16[1,2048,256]{2,1,0:T(8,128)(2,1)S(1)}, bf16[1,2048,256]{2,1,0:T(8,128)(2,1)}, u32[]{:S(2)}) copy-start(bf16[1,2048,256]{2,1,0:T(8,128)(2,1)} %param.17) | copy-start | bytes 3145732
  56.0 45.5 %copy-start.9 = (bf16[1,2048,256]{2,1,0:T(8,128)(2,1)S(1)}, bf16[1,2048,256]{2,1,0:T(8,128)(2,1)}, u32[]{:S(2)}) copy-start(bf16[1,2048,256]{2,1,0:T(8,128)(2,1)} %param.16) | copy-start | bytes 3145732
  96.1 5.4 %collective-permute-start.1 = (bf16[8,256,128]{2,1,0:T(8,128)(2,1)S(1)}, bf16[8,256,128]{2,1,0:T(8,128)(2,1)S(1)}, u32[]{:S(2)}, u32[]{:S(2)}) collective-permute-start(bf16[8,256,128]{2,1,0:T(8,128)(2,1)S(1)} %bitcast.18), channel_id=1, source_target_pairs={{0,32},{32,0},{1,33},{33,1},{2,34},{34,2},{3,35},{35,3},{4,36},{36... | collective-permute-start | bytes 1572872 | tf_op jit(solution)/shard_map/ppermute | solution.py:27
  106.3 3.8 %collective-permute-start.2 = (bf16[8,256,128]{2,1,0:T(8,128)(2,1)S(1)}, bf16[8,256,128]{2,1,0:T(8,128)(2,1)S(1)}, u32[]{:S(2)}, u32[]{:S(2)}) collective-permute-start(bf16[8,256,128]{2,1,0:T(8,128)(2,1)S(1)} %get-tuple-element.30), channel_id=1, source_target_pairs={{0,32},{32,0},{1,33},{33,1},{2,34},{34,2},{3,35},{35,3},{4,36},{36... | collective-permute-start | bytes 1572872 | tf_op jit(solution)/shard_map/ppermute | solution.py:27
  172.3 17.0 %all-to-all-start.9 = ((bf16[32,16,128]{2,1,0:T(8,128)(2,1)}), bf16[32,16,128]{2,1,0:T(8,128)(2,1)S(1)}, u32[]{:S(2)}, u32[]{:S(2)}) async-start(bf16[32,16,128]{2,1,0:T(8,128)(2,1)} %bitcast.13), calls=%async_computation.9 | async-start | bytes 262144 | tf_op jit(solution)/shard_map/all_to_all | solution.py:23
  180.9 9.0 %collective-permute-start.3 = (bf16[8,32,640]{2,1,0:T(8,128)(2,1)S(1)}, bf16[8,32,640]{2,1,0:T(8,128)(2,1)S(1)}, u32[]{:S(2)}, u32[]{:S(2)}) collective-permute-start(bf16[8,32,640]{2,1,0:T(8,128)(2,1)S(1)} %all_to_all.57.grads_ref.here_ref), channel_id=1, source_target_pairs={{0,32},{32,0},{1,33},{33,1},{2,34},{34,2},{3,35},{35,3},{4,36},{36... | collective-permute-start | bytes 983048 | tf_op jit(solution)/shard_map/ppermute | solution.py:27
  183.1 3.3 %collective-permute-start.4 = (bf16[8,48,256]{2,1,0:T(8,128)(2,1)S(1)}, bf16[8,48,256]{2,1,0:T(8,128)(2,1)S(1)}, u32[]{:S(2)}, u32[]{:S(2)}) collective-permute-start(bf16[8,48,256]{2,1,0:T(8,128)(2,1)S(1)} %all_to_all.51.act_ref.here_ref), channel_id=1, source_target_pairs={{0,32},{32,0},{1,33},{33,1},{2,34},{34,2},{3,35},{35,3},{4,36},{36... | collective-permute-start | bytes 589832 | tf_op jit(solution)/shard_map/ppermute | solution.py:27

commit v4 on v3

v4 whole, which is shorter than its diff:
```python
import jax
import jax.numpy as jnp
from jax import lax
from jax.experimental import pallas as pl
from jax.experimental.pallas import tpu as pltpu
from jax.sharding import Mesh
from jax.sharding import PartitionSpec as P

D = 2048
HEAD = 256
LANES = 128
EPSILON = 1e-06
BF = jnp.bfloat16
F32 = jnp.float32

ROWS = (((0,), (0,)), ((), ()))
COLS = (((1,), (1,)), ((), ()))
SECTION = ("z", "core")
WIDE = ("core", "tensor")


def exchange(pieces, axis):
    return lax.all_to_all(pieces, axis, split_axis=0, concat_axis=0, tiled=True)


def other_core(value):
    return lax.ppermute(value, "core", [(0, 1), (1, 0)])


def dot(left, right, dims=(((1,), (0,)), ((), ()))):
    return lax.dot_general(left, right, dims, preferred_element_type=F32)


def in_thirds(value):
    high = value.astype(BF).astype(F32)
    middle = (value - high).astype(BF).astype(F32)
    return high, middle, value - high - middle


def diagonal(count, shift):
    row = lax.broadcasted_iota(jnp.int32, (count, LANES), 0)
    return row + shift == lax.broadcasted_iota(jnp.int32, (count, LANES), 1)


def as_column(line, count, shift=0):
    return jnp.sum(jnp.where(diagonal(count, shift), line, 0.0), axis=1, keepdims=True)


def in_blocks(value):
    width = value.shape[1]
    return jnp.concatenate([value[:, i : i + LANES] for i in range(0, width, LANES)], axis=0)


def half_of(core, half):
    return pl.ds(pl.multiple_of(core * half, half), half)


def spread(x_ref, copies_ref):
    for i in range(copies_ref.shape[0]):
        copies_ref[i] = x_ref[...]


def by_row(rows, count):
    row = lax.broadcasted_iota(jnp.int32, (count, LANES), 0)
    tile = jnp.zeros((count, LANES), F32)
    for i, value in enumerate(rows):
        tile = jnp.where(row == i, value, tile)
    return tile


def start(place_ref, mlp_ref, final_ref, gate_ref, up_ref, down_ref, sent_ref):
    half = gate_ref.shape[1] // 2
    feats = gate_ref.shape[0]
    quarter = half // 4
    away = 1 - lax.rem(place_ref[0], 2)
    there = half_of(away, half)
    sent_ref[:feats, :half] = gate_ref[:, there]
    sent_ref[:feats, half:] = up_ref[:, there]
    for i in range(4):
        at = pl.ds(pl.multiple_of(away * half + i * quarter, quarter), quarter)
        sent_ref[feats : feats + quarter, i * LANES : (i + 1) * LANES] = down_ref[at, :]
    for i, parts in enumerate(zip(in_thirds(mlp_ref[...]), in_thirds(final_ref[...]))):
        sent_ref[feats + quarter :, i * LANES : (i + 1) * LANES] = by_row(parts, 16).astype(BF)
    sent_ref[feats + quarter :, 3 * LANES :] = jnp.zeros((16, LANES), BF)


def got_gains(got_ref, rows):
    tile = got_ref[rows : rows + 16, :].astype(F32)
    tile = tile[:, :LANES] + tile[:, LANES : 2 * LANES] + tile[:, 2 * LANES : 3 * LANES]
    return tile[0:1], tile[1:2]


def gate_up(place_ref, x_ref, mlp_ref, final_ref, gate_ref, up_ref, got_ref, pieces_ref, scaled_ref):
    core = lax.rem(place_ref[0], 2)
    half = gate_ref.shape[1] // 2
    feats = gate_ref.shape[0]
    here = half_of(core, half)
    x_here = x_ref[core].astype(F32)
    x_there = x_ref[1 - core].astype(F32)
    scaled = (x_here * mlp_ref[...]).astype(BF)
    scaled_ref[...] = scaled
    mlp_there, final_there = got_gains(got_ref, feats + half // 4)
    scaled_there = (x_there * mlp_there).astype(BF)
    gate = dot(scaled, gate_ref[:, here]) + dot(scaled_there, got_ref[:feats, :half])
    up = dot(scaled, up_ref[:, here]) + dot(scaled_there, got_ref[:feats, half:])
    pieces = pieces_ref.shape[0]
    tokens = scaled.shape[0]
    share = tokens // pieces
    for at, value in ((0, gate), (half, up)):
        for lanes in range(0, half, LANES):
            rows = (at + lanes) // LANES * share
            part = value[:, lanes : lanes + LANES].astype(BF).reshape(pieces, share, LANES)
            pieces_ref[:, rows : rows + share, :] = part
    squares = x_here * x_here + x_there * x_there
    line = lax.dot_general(
        jnp.ones((8, LANES), F32),
        squares,
        COLS,
        precision=lax.Precision.HIGHEST,
        preferred_element_type=F32,
    )[0:1]
    high = line.astype(BF).astype(F32)
    first = core == 0
    final_here = final_ref[...]
    gains = in_thirds(jnp.where(first, final_here, final_there))
    gains += in_thirds(jnp.where(first, final_there, final_here))
    base = by_row(gains, 16)
    row = lax.broadcasted_iota(jnp.int32, (16, LANES), 0)
    for at in range(0, tokens, LANES):
        lanes = slice(at, at + LANES)
        tile = jnp.where(row == 6, high[:, lanes], base)
        tile = jnp.where(row == 7, (line - high)[:, lanes], tile).astype(BF)
        for i in range(at // share, (at + LANES) // share):
            pieces_ref[i, 2 * half // LANES * share :, :] = tile


def activate(place_ref, arrived_ref, copies_ref, gate_f_ref, up_f_ref, inner_f_ref, recip_ref):
    pieces, share, half = copies_ref.shape
    rows = 2 * half // LANES * share
    total = arrived_ref[0, :rows].astype(F32)
    for i in range(1, pieces):
        total += arrived_ref[i, :rows].astype(F32)
    line = jnp.zeros((1, LANES), F32)
    for i in range(pieces):
        tile = arrived_ref[i, rows:].astype(F32)
        recip_ref[i, 0] = 1.0 / (tile[0:1] + tile[1:2] + tile[2:3])
        recip_ref[i, 1] = 1.0 / (tile[3:4] + tile[4:5] + tile[5:6])
        line += tile[6:7] + tile[7:8]
    shift = lax.rem(lax.div(place_ref[0], 2), LANES // share) * share
    inv = lax.rsqrt(as_column(line, share, shift) * (1.0 / D) + EPSILON)
    parts = [total[i * share : (i + 1) * share] for i in range(2 * half // LANES)]
    gate_pre = jnp.concatenate(parts[: half // LANES], axis=1) * inv
    up_pre = jnp.concatenate(parts[half // LANES :], axis=1) * inv
    sigmoid_gate = jax.nn.sigmoid(gate_pre)
    activated = gate_pre * sigmoid_gate
    hidden_act = (activated * up_pre).astype(BF)
    gate_factor = up_pre * sigmoid_gate * (1.0 + gate_pre * (1.0 - sigmoid_gate))
    gate_f_ref[...] = gate_factor * inv
    up_f_ref[...] = activated * inv
    inner_f_ref[...] = (gate_factor * gate_pre + activated * up_pre) * (inv * inv * (1.0 / D))
    for i in range(pieces):
        copies_ref[i] = hidden_act


def down_half(got_ref, feats, half):
    quarter = half // 4
    rows = got_ref[feats : feats + quarter, :]
    return jnp.concatenate([rows[:, i * LANES : (i + 1) * LANES] for i in range(4)], axis=0)


def mix(place_ref, act_ref, down_ref, got_ref, pieces_ref):
    core = lax.rem(place_ref[0], 2)
    pieces, share, half = act_ref.shape
    feats = down_ref.shape[1]
    act = act_ref[...].reshape(pieces * share, half)
    shape = pieces_ref.shape[1:]
    here = dot(act, down_ref[half_of(core, half), :])
    pieces_ref[core] = here.astype(BF).reshape(shape)
    there = dot(act, down_half(got_ref, feats, half))
    pieces_ref[1 - core] = there.astype(BF).reshape(shape)


def finish_outer(arrived_ref, x_ref, final_ref, copies_ref):
    total = x_ref[...].astype(F32)
    for i in range(arrived_ref.shape[0]):
        total += arrived_ref[i].astype(F32)
    scaled = (total * final_ref[...]).astype(BF)
    for i in range(copies_ref.shape[0]):
        copies_ref[i] = scaled


def attend(place_ref, mine_ref, other_ref, wk_ref, wv_ref, recip_ref, q_ref, g_ref, qg_ref, keep_ref, send_ref):
    core = lax.rem(place_ref[0], 2)
    pairs = mine_ref.shape[0]
    rows = mine_ref.shape[1]
    scale = HEAD ** (-0.5)
    keys_raw = jnp.zeros((rows, HEAD), F32)
    values_raw = jnp.zeros((rows, HEAD), F32)
    square = jnp.zeros((rows, LANES), F32)

    def both_sides(ref, z):
        return jnp.concatenate([ref[z, core], ref[z, 1 - core]], axis=0)

    for z in range(pairs):
        block = jnp.concatenate([mine_ref[z], other_ref[z]], axis=1)
        keys_raw += dot(block, both_sides(wk_ref, z))
        values_raw += dot(block, both_sides(wv_ref, z))
        for block_ref, side in ((mine_ref, core), (other_ref, 1 - core)):
            wide = block_ref[z].astype(F32) * recip_ref[z, side]
            square += wide * wide
    inv_out = lax.rsqrt(jnp.sum(square, axis=1, keepdims=True) / D + EPSILON)
    keys = (keys_raw * inv_out).astype(BF)
    values = (values_raw * inv_out).astype(BF)
    key_grad = jnp.zeros((rows, HEAD), F32)
    value_grad = jnp.zeros((rows, HEAD), F32)
    step = 256
    for at in range(0, q_ref.shape[0], step):
        query = q_ref[at : at + step, :]
        grad = g_ref[at : at + step, :]
        scores = dot(keys, query, COLS) * scale
        raised = jnp.exp(scores - jnp.max(scores, axis=0, keepdims=True))
        probs = raised / jnp.sum(raised, axis=0, keepdims=True)
        probs_bf = probs.astype(BF)
        dprob = dot(values, grad, COLS)
        delta = jnp.sum(probs_bf.astype(F32) * dprob, axis=0, keepdims=True)
        dscore = (probs * (dprob - delta) * scale).astype(BF)
        qg_ref[at : at + step, :] = dot(dscore, keys, ROWS).astype(BF)
        key_grad += dot(dscore, query)
        value_grad += dot(probs_bf, grad)
    key_grad = key_grad.astype(BF)
    value_grad = value_grad.astype(BF)
    inner = jnp.sum(
        key_grad.astype(F32) * keys_raw + value_grad.astype(F32) * values_raw, axis=1, keepdims=True
    )
    along = inv_out * inv_out * inv_out * inner * (1.0 / D)
    for z in range(pairs):
        total = dot(key_grad, both_sides(wk_ref, z), COLS)
        total += dot(value_grad, both_sides(wv_ref, z), COLS)
        total *= inv_out
        sides = ((mine_ref, keep_ref, core), (other_ref, send_ref, 1 - core))
        for i, (block_ref, out_ref, side) in enumerate(sides):
            recip = recip_ref[z, side]
            term = block_ref[z].astype(F32) * (recip * recip) * along
            out_ref[z] = (total[:, i * LANES : (i + 1) * LANES] - term).astype(out_ref.dtype)


def outer_gradient(arrived_ref, final_ref, grad_ref, copies_ref):
    totals = [arrived_ref[i].astype(F32) for i in range(8)]
    for i in range(8, arrived_ref.shape[0]):
        totals[i % 8] += arrived_ref[i].astype(F32)
    total = sum(totals[1:], totals[0]) * final_ref[...]
    grad_ref[...] = total
    rounded = total.astype(BF)
    for i in range(copies_ref.shape[0]):
        copies_ref[i] = rounded


def through_down(place_ref, outer_ref, down_ref, got_ref, pieces_ref):
    core = lax.rem(place_ref[0], 2)
    feats = down_ref.shape[1]
    half = down_ref.shape[0] // 2
    part = dot(outer_ref[core], down_ref[half_of(core, half), :], COLS)
    part += dot(outer_ref[1 - core], down_half(got_ref, feats, half), COLS)
    pieces_ref[...] = part.astype(BF).reshape(pieces_ref.shape)


def gate_up_gradient(arrived_ref, gate_f_ref, up_f_ref, inner_f_ref, copies_ref):
    half = gate_f_ref.shape[1]
    total = arrived_ref[0].astype(F32)
    for i in range(1, arrived_ref.shape[0]):
        total += arrived_ref[i].astype(F32)
    gate = in_blocks((total * gate_f_ref[...]).astype(BF))
    up = in_blocks((total * up_f_ref[...]).astype(BF))
    inner = jnp.sum(total * inner_f_ref[...], axis=1, keepdims=True)
    line = jnp.sum(jnp.where(diagonal(inner.shape[0], 0), inner, 0.0), axis=0, keepdims=True)
    high = line.astype(BF).astype(F32)
    tile = by_row((high, line - high), 16).astype(BF)
    rows = gate.shape[0]
    for i in range(copies_ref.shape[0]):
        copies_ref[i, :rows] = gate
        copies_ref[i, rows : 2 * rows] = up
        copies_ref[i, 2 * rows :] = tile


def columns_of(grads_ref, at, half):
    share = (grads_ref.shape[1] - 16) * LANES // (2 * half)
    blocks = range(at // LANES, (at + half) // LANES)
    tokens = grads_ref.shape[0] * share
    parts = [grads_ref[:, i * share : (i + 1) * share].reshape(tokens, LANES) for i in blocks]
    return jnp.concatenate(parts, axis=1)


def through_gate_up(place_ref, grads_ref, x_ref, mlp_ref, gate_ref, up_ref, got_ref, pieces_ref):
    core = lax.rem(place_ref[0], 2)
    half = gate_ref.shape[1] // 2
    feats = gate_ref.shape[0]
    here = half_of(core, half)
    tokens = x_ref.shape[1]
    shape = pieces_ref.shape[1:]
    gate = columns_of(grads_ref, 0, half)
    up = columns_of(grads_ref, half, half)
    share = tokens // grads_ref.shape[0]
    lines = [grads_ref[i, grads_ref.shape[1] - 16 :].astype(F32) for i in range(grads_ref.shape[0])]
    inner = jnp.concatenate([as_column(v[0:1] + v[1:2], share) for v in lines], axis=0)
    part = dot(gate, gate_ref[:, here], COLS) + dot(up, up_ref[:, here], COLS)
    part = part * mlp_ref[...] - x_ref[core].astype(F32) * inner
    pieces_ref[core] = part.astype(BF).reshape(shape)
    mlp_there, _ = got_gains(got_ref, feats + half // 4)
    part = dot(gate, got_ref[:feats, :half], COLS) + dot(up, got_ref[:feats, half:], COLS)
    part = part * mlp_there - x_ref[1 - core].astype(F32) * inner
    pieces_ref[1 - core] = part.astype(BF).reshape(shape)


def gate_up_weights(place_ref, scaled_ref, here_ref, there_ref, gate_ref, up_ref):
    core = lax.rem(place_ref[0], 2)
    half = gate_ref.shape[1] // 2
    scaled = scaled_ref[...]
    for grads_ref, place in ((here_ref, core), (there_ref, 1 - core)):
        at = half_of(place, half)
        gate_ref[:, at] = dot(scaled, columns_of(grads_ref, 0, half), ROWS).astype(BF)
        up_ref[:, at] = dot(scaled, columns_of(grads_ref, half, half), ROWS).astype(BF)


def down_weights(place_ref, outer_ref, here_ref, there_ref, down_ref):
    core = lax.rem(place_ref[0], 2)
    half = down_ref.shape[0] // 2
    tokens = outer_ref.shape[1]
    outer = outer_ref[core]
    for act_ref, place in ((here_ref, core), (there_ref, 1 - core)):
        act = act_ref[...].reshape(tokens, half)
        down_ref[half_of(place, half), :] = dot(act, outer, ROWS).astype(BF)


def call(body, outs, *args, flops=0):
    vmem = pl.BlockSpec(memory_space=pltpu.VMEM)
    in_specs = [vmem] * len(args)
    if args[0].dtype == jnp.int32:
        in_specs[0] = pl.BlockSpec(memory_space=pltpu.SMEM)
    shapes = tuple(jax.ShapeDtypeStruct(shape, dtype) for shape, dtype in outs)
    moved = sum(a.size * a.dtype.itemsize for a in (*args, *shapes))
    results = pl.pallas_call(
        body,
        out_shape=shapes,
        in_specs=in_specs,
        out_specs=(vmem,) * len(shapes),
        compiler_params=pltpu.CompilerParams(vmem_limit_bytes=40 * 1024 * 1024),
        cost_estimate=pl.CostEstimate(flops=flops, bytes_accessed=moved, transcendentals=0),
    )(*args)
    return results


def on_device(
    enc_hidden,
    mlp_gain,
    final_gain,
    w_gate,
    w_up,
    w_down,
    key_weight,
    value_weight,
    queries,
    context_grad,
):
    block, feats = enc_hidden.shape
    half = w_gate.shape[1] // 2
    place = (2 * lax.axis_index("z") + lax.axis_index("core")).astype(jnp.int32).reshape(1)
    chips = lax.axis_size("z")
    blocks = lax.axis_size("tensor")
    tokens = block * blocks
    share = tokens // chips
    mlp_gain = mlp_gain.reshape(1, feats)
    final_gain = final_gain.reshape(1, feats)

    piece = share * 2 * half // LANES + 16

    (copies,) = call(spread, [((2 * blocks, block, feats), BF)], enc_hidden)
    hidden = exchange(copies, WIDE).reshape(2, tokens, feats)
    (sent,) = call(
        start,
        [((feats + half // 4 + 16, 2 * half), BF)],
        place, mlp_gain, final_gain, w_gate, w_up, w_down,
    )
    got = other_core(sent)
    pieces, scaled = call(
        gate_up,
        [((chips, piece, LANES), BF), ((tokens, feats), BF)],
        place, hidden, mlp_gain, final_gain, w_gate, w_up, got,
    )
    arrived = exchange(pieces, "z")
    copies, gate_f, up_f, inner_f, recip = call(
        activate,
        [((chips, share, half), BF)]
        + [((share, half), F32)] * 3
        + [((chips, 2, 1, LANES), F32)],
        place, arrived,
    )
    act = exchange(copies, "z")
    act_there = other_core(act)
    (pieces,) = call(
        mix, [((2, blocks, block, feats), BF)], place, act, w_down, got
    )
    arrived = exchange(pieces.reshape(-1, block, feats), WIDE)
    (copies,) = call(
        finish_outer, [((chips * blocks, block, feats), BF)], arrived, enc_hidden, final_gain
    )
    mine = exchange(copies, ("z", "tensor")).reshape(chips, tokens, feats)
    other = other_core(mine)
    by_block = (chips, 2, LANES, HEAD)
    query_grad, keep, send = call(
        attend,
        [(queries.shape[1:], BF), (mine.shape, F32), (mine.shape, BF)],
        place, mine, other, key_weight.reshape(by_block), value_weight.reshape(by_block), recip,
        queries[0], context_grad[0],
        flops=3_500_000_000,
    )
    both = (keep + other_core(send).astype(F32)).astype(BF)
    arrived = exchange(both.reshape(-1, block, feats), ("z", "tensor"))
    outer_grad, copies = call(
        outer_gradient,
        [((block, feats), F32), ((2 * blocks, block, feats), BF)],
        arrived, final_gain,
    )
    outer = exchange(copies, WIDE).reshape(2, tokens, feats)
    (pieces,) = call(through_down, [((chips, share, half), BF)], place, outer, w_down, got)
    arrived = exchange(pieces, "z")
    (down_weight_grad,) = call(down_weights, [(w_down.shape, BF)], place, outer, act, act_there)
    (copies,) = call(
        gate_up_gradient, [((chips, piece, LANES), BF)], arrived, gate_f, up_f, inner_f
    )
    grads = exchange(copies, "z")
    grads_there = other_core(grads)
    (pieces,) = call(
        through_gate_up,
        [((2, blocks, block, feats), BF)],
        place, grads, hidden, mlp_gain, w_gate, w_up, got,
    )
    arrived = exchange(pieces.reshape(-1, block, feats), WIDE)
    gate_weight_grad, up_weight_grad = call(
        gate_up_weights,
        [(w_gate.shape, BF), (w_up.shape, BF)],
        place, scaled, grads, grads_there,
    )
    outer_grad, gate_weight_grad, up_weight_grad = lax.optimization_barrier(
        (outer_grad, gate_weight_grad, up_weight_grad)
    )
    hidden_grad = outer_grad + arrived.astype(F32).sum(axis=0)
    return (query_grad[None], hidden_grad, gate_weight_grad, up_weight_grad, down_weight_grad)


def solution(mesh):
    names = list(mesh.axis_names)
    at = names.index("section")
    shape = list(mesh.devices.shape)
    names[at : at + 1] = SECTION
    shape[at : at + 1] = [shape[at] // 2, 2]
    fine = Mesh(mesh.devices.reshape(shape), tuple(names))
    in_specs = (
        P(("dp", "tensor"), SECTION),
        P(SECTION),
        P(SECTION),
        P(SECTION, "tensor"),
        P(SECTION, "tensor"),
        P("tensor", SECTION),
        P(SECTION, None, "tensor"),
        P(SECTION, None, "tensor"),
        P(SECTION, "dp", "tensor"),
        P(SECTION, "dp", "tensor"),
    )
    out_specs = (
        P(SECTION, "dp", "tensor"),
        P(("dp", "tensor"), SECTION),
        P(("dp", *SECTION), "tensor"),
        P(("dp", *SECTION), "tensor"),
        P(("dp", "tensor"), SECTION),
    )
    return jax.shard_map(
        on_device, mesh=fine, in_specs=in_specs, out_specs=out_specs, check_vma=False
    )
```

time: 192 us -> 185 us (0.964)
  local copies, waits for them, and re-layouts: 3.41 us -> 1.35 us
    unnamed x26 -> x22, local copies, waits for them, and re-layouts: 3.41 us -> 1.35 us
    pallas_call x12 -> x13, Pallas kernels: 9.47 us -> 8.06 us  [call(): pl.pallas_call(body, out_shape=shapes, in_specs=in_specs, out_specs=(vmem...]
  transfers between devices with their start and end apart: 7 -> 7, of which waited for: 6 -> 6; matrix products, arithmetic and copies ran while one was open for 0% -> 0% of each run, Pallas kernels for 0% -> 1%
where the time goes in v4:
time: 185 us
  blocking collectives  131 us (71%)
  starting transfers between devices  31.4 us (17%)
  waiting for transfers between devices  11.5 us (6%)
  Pallas kernels  8.06 us (4%)
    all_to_all x8, blocking collectives, exchange(): return lax.all_to_all(pieces, axis, split_axis=0, concat_axis=0, tiled=True)  131 us
    all_to_all x2, starting transfers between devices, exchange(): return lax.all_to_all(pieces, axis, split_axis=0, concat_axis=0, tiled=True)  18.7 us
    ppermute x5, starting transfers between devices, other_core(): return lax.ppermute(value, 'core', [(0, 1), (1, 0)])  12.7 us
    pallas_call x13, Pallas kernels, call(): pl.pallas_call(body, out_shape=shapes, in_specs=in_specs, out_specs=(vmem...  8.06 us
    all_to_all x2, waiting for transfers between devices, exchange(): return lax.all_to_all(pieces, axis, split_axis=0, concat_axis=0, tiled=True)  6.25 us
    ppermute x5, waiting for transfers between devices, other_core(): return lax.ppermute(value, 'core', [(0, 1), (1, 0)])  5.27 us
  transfers between devices with their start and end apart: 7, of which 6 were waited for; matrix products, arithmetic and copies ran while one was open for 0% of the time, Pallas kernels for 1%

profile of v4, /device:TPU:1, one launch (start us, length us, event | category | flops | bytes accessed | tf_op | source)
XLA Modules:
  0.0 184.7 jit_solution(13757318792627889044)
XLA Ops:
  0.6 0.0 copy-start.3
  0.6 0.7 copy-done.3
  1.3 0.7 shard_map.137
  2.0 10.6 %all-to-all-start = ((bf16[32,16,128]{2,1,0:T(8,128)(2,1)}), bf16[32,16,128]{2,1,0:T(8,128)(2,1)S(1)}, u32[]{:S(2)}, u32[]{:S(2)}) async-start(bf16[32,16,128]{2,1,0:T(8,128)(2,1)} %shard_map.137), calls=%async_computation | async-start | bytes 262144 | tf_op jit(solution)/shard_map/all_to_all | solution.py:23
  12.6 0.0 copy-start.5
  12.6 0.0 copy-start.6
  12.7 0.6 copy-done.5
  13.3 0.0 copy-done.6
  13.3 2.2 %collective-permute-start = (bf16[208,512]{1,0:T(8,128)(2,1)S(1)}, bf16[208,512]{1,0:T(8,128)(2,1)S(1)}, u32[]{:S(2)}, u32[]{:S(2)}) collective-permute-start(bf16[208,512]{1,0:T(8,128)(2,1)S(1)} %shard_map.138), channel_id=1, source_target_pairs={{0,32},{32,0},{1,33},{33,1},{2,34},{34,2},{3,35},{35,3},{4,36},{36... | collective-permute-start | bytes 638984 | tf_op jit(solution)/shard_map/ppermute | solution.py:27
  15.5 1.2 collective-permute-done.got_ref
  16.7 4.2 %all-to-all-done = bf16[32,16,128]{2,1,0:T(8,128)(2,1)S(1)} async-done(((bf16[32,16,128]{2,1,0:T(8,128)(2,1)}), bf16[32,16,128]{2,1,0:T(8,128)(2,1)S(1)}, u32[]{:S(2)}, u32[]{:S(2)}) %all-to-all-start) | async-done | bytes 131104 | tf_op jit(solution)/shard_map/all_to_all | solution.py:23
  20.9 0.4 shard_map.139
  21.3 0.0 copy-start.10
  21.3 19.1 %all_to_all.50.arrived_ref = bf16[8,144,128]{2,1,0:T(8,128)(2,1)S(1)} all-to-all(bf16[8,144,128]{2,1,0:T(8,128)(2,1)S(1)} %get-tuple-element.22), channel_id=1, replica_groups=mesh['z'=8,'core'=2,'tensor'=16,'dp'=2] {'z'}, dimensions={0} | all-to-all | bytes 589824 | tf_op jit(solution)/shard_map/all_to_all | solution.py:23
  40.4 0.1 shard_map.140
  40.5 0.0 copy-start.8
  40.5 11.4 %all_to_all.51.act_ref.here_ref = bf16[8,32,256]{2,1,0:T(8,128)(2,1)S(1)} all-to-all(bf16[8,32,256]{2,1,0:T(8,128)(2,1)S(1)} %get-tuple-element.23), channel_id=1, replica_groups=mesh['z'=8,'core'=2,'tensor'=16,'dp'=2] {'z'}, dimensions={0} | all-to-all | bytes 262144 | tf_op jit(solution)/shard_map/all_to_all | solution.py:23
  51.9 0.2 shard_map.141
  52.2 0.0 copy-start.4
  52.2 0.0 copy-start.7
  52.2 15.1 %all_to_all.52.arrived_ref = bf16[32,16,128]{2,1,0:T(8,128)(2,1)S(1)} all-to-all(bf16[32,16,128]{2,1,0:T(8,128)(2,1)S(1)} %bitcast.20), channel_id=1, replica_groups=mesh['z'=8,'core'=2,'tensor'=16,'dp'=2] {'core','tensor'}, dimensions={0} | all-to-all | bytes 262144 | tf_op jit(solution)/shard_map/all_to_all | solution.py:23
  67.2 0.0 copy-done.4
  67.2 0.1 shard_map.142
  67.3 0.0 copy-start.9
  67.3 24.7 %all_to_all.53 = bf16[128,16,128]{2,1,0:T(8,128)(2,1)S(1)} all-to-all(bf16[128,16,128]{2,1,0:T(8,128)(2,1)S(1)} %shard_map.142), channel_id=1, replica_groups=mesh['z'=8,'core'=2,'tensor'=16,'dp'=2] {'z','tensor'}, dimensions={0} | all-to-all | bytes 1048576 | tf_op jit(solution)/shard_map/all_to_all | solution.py:23
  92.1 3.9 %collective-permute-start.1 = (bf16[8,256,128]{2,1,0:T(8,128)(2,1)S(1)}, bf16[8,256,128]{2,1,0:T(8,128)(2,1)S(1)}, u32[]{:S(2)}, u32[]{:S(2)}) collective-permute-start(bf16[8,256,128]{2,1,0:T(8,128)(2,1)S(1)} %bitcast.18), channel_id=1, source_target_pairs={{0,32},{32,0},{1,33},{33,1},{2,34},{34,2},{3,35},{35,3},{4,36},{36... | collective-permute-start | bytes 1572872 | tf_op jit(solution)/shard_map/ppermute | solution.py:27
  96.0 1.5 collective-permute-done.1.other_ref
  97.5 3.3 %shard_map.143 = (bf16[1024,256]{1,0:T(8,128)(2,1)}, f32[8,256,128]{2,1,0:T(8,128)S(1)}, bf16[8,256,128]{2,1,0:T(8,128)(2,1)S(1)}) custom-call(s32[1]{0:T(128)} %bitcast.place_ref, bf16[8,256,128]{2,1,0:T(8,128)(2,1)S(1)} %bitcast.19, bf16[8,256,128]{2,1,0:T(8,128)(2,1)S(1)} %collective-permute-done.1.other_ref, bf16[8,2,128,256]{3,2,1,0:T(8,128)(2,1)S(1)} %bitcast.28, ...), custom_call_target="tpu_custom_call" | custom-call | flops 3500000000 | bytes 6299652 | tf_op jit(solution)/shard_map/pallas_call | solution.py:341
  100.8 2.3 %collective-permute-start.2 = (bf16[8,256,128]{2,1,0:T(8,128)(2,1)S(1)}, bf16[8,256,128]{2,1,0:T(8,128)(2,1)S(1)}, u32[]{:S(2)}, u32[]{:S(2)}) collective-permute-start(bf16[8,256,128]{2,1,0:T(8,128)(2,1)S(1)} %get-tuple-element.27), channel_id=1, source_target_pairs={{0,32},{32,0},{1,33},{33,1},{2,34},{34,2},{3,35},{35,3},{4,36},{36... | collective-permute-start | bytes 1572872 | tf_op jit(solution)/shard_map/ppermute | solution.py:27
  103.1 1.5 collective-permute-done.2
  104.6 0.1 add_convert_fusion
  104.7 24.9 %all_to_all.54.arrived_ref = bf16[128,16,128]{2,1,0:T(8,128)(2,1)S(1)} all-to-all(bf16[128,16,128]{2,1,0:T(8,128)(2,1)S(1)} %bitcast.32), channel_id=1, replica_groups=mesh['z'=8,'core'=2,'tensor'=16,'dp'=2] {'z','tensor'}, dimensions={0} | all-to-all | bytes 1048576 | tf_op jit(solution)/shard_map/all_to_all | solution.py:23
  129.6 0.1 shard_map.144
  129.7 13.4 %all_to_all.55 = bf16[32,16,128]{2,1,0:T(8,128)(2,1)S(1)} all-to-all(bf16[32,16,128]{2,1,0:T(8,128)(2,1)S(1)} %get-tuple-element.30), channel_id=1, replica_groups=mesh['z'=8,'core'=2,'tensor'=16,'dp'=2] {'core','tensor'}, dimensions={0} | all-to-all | bytes 262144 | tf_op jit(solution)/shard_map/all_to_all | solution.py:23
  143.1 0.2 shard_map.145
  143.3 10.1 %all_to_all.56.arrived_ref = bf16[8,32,256]{2,1,0:T(8,128)(2,1)S(1)} all-to-all(bf16[8,32,256]{2,1,0:T(8,128)(2,1)S(1)} %shard_map.145), channel_id=1, replica_groups=mesh['z'=8,'core'=2,'tensor'=16,'dp'=2] {'z'}, dimensions={0} | all-to-all | bytes 262144 | tf_op jit(solution)/shard_map/all_to_all | solution.py:23
  153.5 0.1 shard_map.146
  153.6 12.1 %all_to_all.57.here_ref.grads_ref = bf16[8,144,128]{2,1,0:T(8,128)(2,1)S(1)} all-to-all(bf16[8,144,128]{2,1,0:T(8,128)(2,1)S(1)} %shard_map.146), channel_id=1, replica_groups=mesh['z'=8,'core'=2,'tensor'=16,'dp'=2] {'z'}, dimensions={0} | all-to-all | bytes 589824 | tf_op jit(solution)/shard_map/all_to_all | solution.py:23
  165.6 1.0 shard_map.148
  166.6 8.1 %all-to-all-start.9 = ((bf16[32,16,128]{2,1,0:T(8,128)(2,1)}), bf16[32,16,128]{2,1,0:T(8,128)(2,1)S(1)}, u32[]{:S(2)}, u32[]{:S(2)}) async-start(bf16[32,16,128]{2,1,0:T(8,128)(2,1)} %bitcast.13), calls=%async_computation.9 | async-start | bytes 262144 | tf_op jit(solution)/shard_map/all_to_all | solution.py:23
  174.8 2.1 %collective-permute-start.3 = (bf16[8,144,128]{2,1,0:T(8,128)(2,1)S(1)}, bf16[8,144,128]{2,1,0:T(8,128)(2,1)S(1)}, u32[]{:S(2)}, u32[]{:S(2)}) collective-permute-start(bf16[8,144,128]{2,1,0:T(8,128)(2,1)S(1)} %all_to_all.57.here_ref.grads_ref), channel_id=1, source_target_pairs={{0,32},{32,0},{1,33},{33,1},{2,34},{34,2},{3,35},{35,3},{4,36},{36... | collective-permute-start | bytes 884744 | tf_op jit(solution)/shard_map/ppermute | solution.py:27
  176.9 2.2 %collective-permute-start.4 = (bf16[8,32,256]{2,1,0:T(8,128)(2,1)S(1)}, bf16[8,32,256]{2,1,0:T(8,128)(2,1)S(1)}, u32[]{:S(2)}, u32[]{:S(2)}) collective-permute-start(bf16[8,32,256]{2,1,0:T(8,128)(2,1)S(1)} %all_to_all.51.act_ref.here_ref), channel_id=1, source_target_pairs={{0,32},{32,0},{1,33},{33,1},{2,34},{34,2},{3,35},{35,3},{4,36},{36... | collective-permute-start | bytes 393224 | tf_op jit(solution)/shard_map/ppermute | solution.py:27
  179.1 1.0 collective-permute-done.4.there_ref
  180.1 0.9 shard_map.149
  181.1 2.0 %all-to-all-done.9 = bf16[32,16,128]{2,1,0:T(8,128)(2,1)S(1)} async-done(((bf16[32,16,128]{2,1,0:T(8,128)(2,1)}), bf16[32,16,128]{2,1,0:T(8,128)(2,1)S(1)}, u32[]{:S(2)}, u32[]{:S(2)}) %all-to-all-start.9) | async-done | bytes 131104 | tf_op jit(solution)/shard_map/all_to_all | solution.py:23
  183.1 0.0 collective-permute-done.3.there_ref
  183.1 1.0 shard_map.147
  184.1 0.6 add.11
  (12 shorter events, 0.1 us)
Async XLA Ops:
  0.6 0.7 copy-start.3
  1.3 11.3 %copy-start.2 = (bf16[512,128]{1,0:T(8,128)(2,1)S(1)}, bf16[512,128]{1,0:T(8,128)(2,1)}, u32[]{:S(2)}) copy-start(bf16[512,128]{1,0:T(8,128)(2,1)} %down_ref.5) | copy-start | bytes 393220
  2.0 10.7 %copy-start = (bf16[128,512]{1,0:T(8,128)(2,1)S(1)}, bf16[128,512]{1,0:T(8,128)(2,1)}, u32[]{:S(2)}) copy-start(bf16[128,512]{1,0:T(8,128)(2,1)} %gate_ref.5) | copy-start | bytes 393220
  2.0 10.7 %copy-start.1 = (bf16[128,512]{1,0:T(8,128)(2,1)S(1)}, bf16[128,512]{1,0:T(8,128)(2,1)}, u32[]{:S(2)}) copy-start(bf16[128,512]{1,0:T(8,128)(2,1)} %up_ref.5) | copy-start | bytes 393220
  2.0 18.9 %all-to-all-start = ((bf16[32,16,128]{2,1,0:T(8,128)(2,1)}), bf16[32,16,128]{2,1,0:T(8,128)(2,1)S(1)}, u32[]{:S(2)}, u32[]{:S(2)}) async-start(bf16[32,16,128]{2,1,0:T(8,128)(2,1)} %shard_map.137), calls=%async_computation | async-start | bytes 262144 | tf_op jit(solution)/shard_map/all_to_all | solution.py:23
  12.6 0.7 copy-start.5
  12.6 0.7 copy-start.6
  13.3 3.4 %collective-permute-start = (bf16[208,512]{1,0:T(8,128)(2,1)S(1)}, bf16[208,512]{1,0:T(8,128)(2,1)S(1)}, u32[]{:S(2)}, u32[]{:S(2)}) collective-permute-start(bf16[208,512]{1,0:T(8,128)(2,1)S(1)} %shard_map.138), channel_id=1, source_target_pairs={{0,32},{32,0},{1,33},{33,1},{2,34},{34,2},{3,35},{35,3},{4,36},{36... | collective-permute-start | bytes 638984 | tf_op jit(solution)/shard_map/ppermute | solution.py:27
  21.3 76.2 %copy-start.10 = (bf16[1,1024,256]{2,1,0:T(8,128)(2,1)S(1)}, bf16[1,1024,256]{2,1,0:T(8,128)(2,1)}, u32[]{:S(2)}) copy-start(bf16[1,1024,256]{2,1,0:T(8,128)(2,1)} %param.19) | copy-start | bytes 1572868
  40.5 57.0 %copy-start.8 = (bf16[1,2048,256]{2,1,0:T(8,128)(2,1)S(1)}, bf16[1,2048,256]{2,1,0:T(8,128)(2,1)}, u32[]{:S(2)}) copy-start(bf16[1,2048,256]{2,1,0:T(8,128)(2,1)} %param.17) | copy-start | bytes 3145732
  52.2 15.1 %copy-start.4 = (bf16[16,128]{1,0:T(8,128)(2,1)S(1)}, bf16[16,128]{1,0:T(8,128)(2,1)}, u32[]{:S(2)}) copy-start(bf16[16,128]{1,0:T(8,128)(2,1)} %x_ref.3) | copy-start | bytes 12292
  52.2 45.4 %copy-start.7 = (bf16[1,2048,256]{2,1,0:T(8,128)(2,1)S(1)}, bf16[1,2048,256]{2,1,0:T(8,128)(2,1)}, u32[]{:S(2)}) copy-start(bf16[1,2048,256]{2,1,0:T(8,128)(2,1)} %param.16) | copy-start | bytes 3145732
  67.3 30.2 %copy-start.9 = (bf16[1,1024,256]{2,1,0:T(8,128)(2,1)S(1)}, bf16[1,1024,256]{2,1,0:T(8,128)(2,1)}, u32[]{:S(2)}) copy-start(bf16[1,1024,256]{2,1,0:T(8,128)(2,1)} %param.18) | copy-start | bytes 1572868
  92.1 5.4 %collective-permute-start.1 = (bf16[8,256,128]{2,1,0:T(8,128)(2,1)S(1)}, bf16[8,256,128]{2,1,0:T(8,128)(2,1)S(1)}, u32[]{:S(2)}, u32[]{:S(2)}) collective-permute-start(bf16[8,256,128]{2,1,0:T(8,128)(2,1)S(1)} %bitcast.18), channel_id=1, source_target_pairs={{0,32},{32,0},{1,33},{33,1},{2,34},{34,2},{3,35},{35,3},{4,36},{36... | collective-permute-start | bytes 1572872 | tf_op jit(solution)/shard_map/ppermute | solution.py:27
  100.8 3.8 %collective-permute-start.2 = (bf16[8,256,128]{2,1,0:T(8,128)(2,1)S(1)}, bf16[8,256,128]{2,1,0:T(8,128)(2,1)S(1)}, u32[]{:S(2)}, u32[]{:S(2)}) collective-permute-start(bf16[8,256,128]{2,1,0:T(8,128)(2,1)S(1)} %get-tuple-element.27), channel_id=1, source_target_pairs={{0,32},{32,0},{1,33},{33,1},{2,34},{34,2},{3,35},{35,3},{4,36},{36... | collective-permute-start | bytes 1572872 | tf_op jit(solution)/shard_map/ppermute | solution.py:27
  166.6 16.4 %all-to-all-start.9 = ((bf16[32,16,128]{2,1,0:T(8,128)(2,1)}), bf16[32,16,128]{2,1,0:T(8,128)(2,1)S(1)}, u32[]{:S(2)}, u32[]{:S(2)}) async-start(bf16[32,16,128]{2,1,0:T(8,128)(2,1)} %bitcast.13), calls=%async_computation.9 | async-start | bytes 262144 | tf_op jit(solution)/shard_map/all_to_all | solution.py:23
  174.8 8.4 %collective-permute-start.3 = (bf16[8,144,128]{2,1,0:T(8,128)(2,1)S(1)}, bf16[8,144,128]{2,1,0:T(8,128)(2,1)S(1)}, u32[]{:S(2)}, u32[]{:S(2)}) collective-permute-start(bf16[8,144,128]{2,1,0:T(8,128)(2,1)S(1)} %all_to_all.57.here_ref.grads_ref), channel_id=1, source_target_pairs={{0,32},{32,0},{1,33},{33,1},{2,34},{34,2},{3,35},{35,3},{4,36},{36... | collective-permute-start | bytes 884744 | tf_op jit(solution)/shard_map/ppermute | solution.py:27
  176.9 3.2 %collective-permute-start.4 = (bf16[8,32,256]{2,1,0:T(8,128)(2,1)S(1)}, bf16[8,32,256]{2,1,0:T(8,128)(2,1)S(1)}, u32[]{:S(2)}, u32[]{:S(2)}) collective-permute-start(bf16[8,32,256]{2,1,0:T(8,128)(2,1)S(1)} %all_to_all.51.act_ref.here_ref), channel_id=1, source_target_pairs={{0,32},{32,0},{1,33},{33,1},{2,34},{34,2},{3,35},{35,3},{4,36},{36... | collective-permute-start | bytes 393224 | tf_op jit(solution)/shard_map/ppermute | solution.py:27

commit v5 on v4

--- a/solution.py
+++ b/solution.py
@@ -101,16 +101,16 @@
     scaled_ref[...] = scaled
     mlp_there, final_there = got_gains(got_ref, feats + half // 4)
     scaled_there = (x_there * mlp_there).astype(BF)
-    gate = dot(scaled, gate_ref[:, here]) + dot(scaled_there, got_ref[:feats, :half])
-    up = dot(scaled, up_ref[:, here]) + dot(scaled_there, got_ref[:feats, half:])
+    both = jnp.concatenate([scaled, scaled_there], axis=1)
+    weights = jnp.concatenate([gate_ref[:, here], up_ref[:, here]], axis=1)
+    weights = jnp.concatenate([weights, got_ref[:feats, :]], axis=0)
+    gate_and_up = dot(both, weights).astype(BF)
     pieces = pieces_ref.shape[0]
     tokens = scaled.shape[0]
     share = tokens // pieces
-    for at, value in ((0, gate), (half, up)):
-        for lanes in range(0, half, LANES):
-            rows = (at + lanes) // LANES * share
-            part = value[:, lanes : lanes + LANES].astype(BF).reshape(pieces, share, LANES)
-            pieces_ref[:, rows : rows + share, :] = part
+    for i in range(2 * half // LANES):
+        part = gate_and_up[:, i * LANES : (i + 1) * LANES].reshape(pieces, share, LANES)
+        pieces_ref[:, i * share : (i + 1) * share, :] = part
     squares = x_here * x_here + x_there * x_there
     line = lax.dot_general(
         jnp.ones((8, LANES), F32),
@@ -168,16 +168,22 @@
     return jnp.concatenate([rows[:, i * LANES : (i + 1) * LANES] for i in range(4)], axis=0)
 
 
+def both_downs(core, down_ref, got_ref):
+    feats = down_ref.shape[1]
+    half = down_ref.shape[0] // 2
+    here = down_ref[half_of(core, half), :]
+    return jnp.concatenate([here, down_half(got_ref, feats, half)], axis=1)
+
+
 def mix(place_ref, act_ref, down_ref, got_ref, pieces_ref):
     core = lax.rem(place_ref[0], 2)
     pieces, share, half = act_ref.shape
     feats = down_ref.shape[1]
     act = act_ref[...].reshape(pieces * share, half)
     shape = pieces_ref.shape[1:]
-    here = dot(act, down_ref[half_of(core, half), :])
-    pieces_ref[core] = here.astype(BF).reshape(shape)
-    there = dot(act, down_half(got_ref, feats, half))
-    pieces_ref[1 - core] = there.astype(BF).reshape(shape)
+    mixed = dot(act, both_downs(core, down_ref, got_ref)).astype(BF)
+    pieces_ref[core] = mixed[:, :feats].reshape(shape)
+    pieces_ref[1 - core] = mixed[:, feats:].reshape(shape)
 
 
 def finish_outer(arrived_ref, x_ref, final_ref, copies_ref):
@@ -189,41 +195,81 @@
         copies_ref[i] = scaled
 
 
-def attend(place_ref, mine_ref, other_ref, wk_ref, wv_ref, recip_ref, q_ref, g_ref, qg_ref, keep_ref, send_ref):
-    core = lax.rem(place_ref[0], 2)
-    pairs = mine_ref.shape[0]
-    rows = mine_ref.shape[1]
+def two_blocks(ref, z, side):
+    return jnp.concatenate([ref[z, side], ref[z + 1, side]], axis=0)
+
+
+def add_features(block_ref, side, wk_ref, wv_ref, recip_ref, keys, values, square):
+    for z in range(0, block_ref.shape[0], 2):
+        block = jnp.concatenate([block_ref[z], block_ref[z + 1]], axis=1)
+        keys += dot(block, two_blocks(wk_ref, z, side))
+        values += dot(block, two_blocks(wv_ref, z, side))
+        for i in range(2):
+            wide = block_ref[z + i].astype(F32) * recip_ref[z + i, side]
+            square += wide * wide
+    return keys, values, square
+
+
+def project(place_ref, mine_ref, wk_ref, wv_ref, recip_ref, keys_ref, values_ref, square_ref):
+    core = lax.rem(place_ref[0], 2)
+    keys_ref[...], values_ref[...], square_ref[...] = add_features(
+        mine_ref,
+        core,
+        wk_ref,
+        wv_ref,
+        recip_ref,
+        jnp.zeros(keys_ref.shape, F32),
+        jnp.zeros(values_ref.shape, F32),
+        jnp.zeros(square_ref.shape, F32),
+    )
+
+
+def back_to_features(block_ref, side, wk_ref, wv_ref, recip_ref, grads, scales, out_ref):
+    key_grad, value_grad = grads
+    inv_out, along = scales
+    for z in range(0, block_ref.shape[0], 2):
+        total = dot(key_grad, two_blocks(wk_ref, z, side), COLS)
+        total += dot(value_grad, two_blocks(wv_ref, z, side), COLS)
+        for i in range(2):
+            recip = recip_ref[z + i, side]
+            term = block_ref[z + i].astype(F32) * (recip * recip) * along
+            part = total[:, i * LANES : (i + 1) * LANES] * inv_out - term
+            out_ref[z + i] = part.astype(out_ref.dtype)
+
+
+def attend(place_ref, other_ref, wk_ref, wv_ref, recip_ref, keys_ref, values_ref, square_ref, q_ref, g_ref, *outs):
+    qg_ref, send_ref, grads_ref, scales_ref = outs
+    core = lax.rem(place_ref[0], 2)
+    rows = other_ref.shape[1]
     scale = HEAD ** (-0.5)
-    keys_raw = jnp.zeros((rows, HEAD), F32)
-    values_raw = jnp.zeros((rows, HEAD), F32)
-    square = jnp.zeros((rows, LANES), F32)
-
-    def both_sides(ref, z):
-        return jnp.concatenate([ref[z, core], ref[z, 1 - core]], axis=0)
-
-    for z in range(pairs):
-        block = jnp.concatenate([mine_ref[z], other_ref[z]], axis=1)
-        keys_raw += dot(block, both_sides(wk_ref, z))
-        values_raw += dot(block, both_sides(wv_ref, z))
-        for block_ref, side in ((mine_ref, core), (other_ref, 1 - core)):
-            wide = block_ref[z].astype(F32) * recip_ref[z, side]
-            square += wide * wide
+    keys_raw, values_raw, square = add_features(
+        other_ref,
+        1 - core,
+        wk_ref,
+        wv_ref,
+        recip_ref,
+        keys_ref[...],
+        values_ref[...],
+        square_ref[...],
+    )
     inv_out = lax.rsqrt(jnp.sum(square, axis=1, keepdims=True) / D + EPSILON)
     keys = (keys_raw * inv_out).astype(BF)
     values = (values_raw * inv_out).astype(BF)
+    scaled_keys = (keys.astype(F32) * scale).astype(BF)
+    scaled_values = (values.astype(F32) * scale).astype(BF)
     key_grad = jnp.zeros((rows, HEAD), F32)
     value_grad = jnp.zeros((rows, HEAD), F32)
     step = 256
     for at in range(0, q_ref.shape[0], step):
         query = q_ref[at : at + step, :]
         grad = g_ref[at : at + step, :]
-        scores = dot(keys, query, COLS) * scale
+        scores = dot(scaled_keys, query, COLS)
         raised = jnp.exp(scores - jnp.max(scores, axis=0, keepdims=True))
-        probs = raised / jnp.sum(raised, axis=0, keepdims=True)
+        probs = raised * (1.0 / jnp.sum(raised, axis=0, keepdims=True))
         probs_bf = probs.astype(BF)
-        dprob = dot(values, grad, COLS)
+        dprob = dot(scaled_values, grad, COLS)
         delta = jnp.sum(probs_bf.astype(F32) * dprob, axis=0, keepdims=True)
-        dscore = (probs * (dprob - delta) * scale).astype(BF)
+        dscore = (probs * (dprob - delta)).astype(BF)
         qg_ref[at : at + step, :] = dot(dscore, keys, ROWS).astype(BF)
         key_grad += dot(dscore, query)
         value_grad += dot(probs_bf, grad)
@@ -233,15 +279,20 @@
         key_grad.astype(F32) * keys_raw + value_grad.astype(F32) * values_raw, axis=1, keepdims=True
     )
     along = inv_out * inv_out * inv_out * inner * (1.0 / D)
-    for z in range(pairs):
-        total = dot(key_grad, both_sides(wk_ref, z), COLS)
-        total += dot(value_grad, both_sides(wv_ref, z), COLS)
-        total *= inv_out
-        sides = ((mine_ref, keep_ref, core), (other_ref, send_ref, 1 - core))
-        for i, (block_ref, out_ref, side) in enumerate(sides):
-            recip = recip_ref[z, side]
-            term = block_ref[z].astype(F32) * (recip * recip) * along
-            out_ref[z] = (total[:, i * LANES : (i + 1) * LANES] - term).astype(out_ref.dtype)
+    grads_ref[0] = key_grad
+    grads_ref[1] = value_grad
+    scales_ref[0] = jnp.broadcast_to(inv_out, (rows, LANES))
+    scales_ref[1] = jnp.broadcast_to(along, (rows, LANES))
+    grads = (key_grad, value_grad)
+    scales = (inv_out, along)
+    back_to_features(other_ref, 1 - core, wk_ref, wv_ref, recip_ref, grads, scales, send_ref)
+
+
+def keep_own(place_ref, mine_ref, wk_ref, wv_ref, recip_ref, grads_ref, scales_ref, keep_ref):
+    core = lax.rem(place_ref[0], 2)
+    grads = (grads_ref[0], grads_ref[1])
+    scales = (scales_ref[0], scales_ref[1])
+    back_to_features(mine_ref, core, wk_ref, wv_ref, recip_ref, grads, scales, keep_ref)
 
 
 def outer_gradient(arrived_ref, final_ref, grad_ref, copies_ref):
@@ -257,10 +308,8 @@
 
 def through_down(place_ref, outer_ref, down_ref, got_ref, pieces_ref):
     core = lax.rem(place_ref[0], 2)
-    feats = down_ref.shape[1]
-    half = down_ref.shape[0] // 2
-    part = dot(outer_ref[core], down_ref[half_of(core, half), :], COLS)
-    part += dot(outer_ref[1 - core], down_half(got_ref, feats, half), COLS)
+    outer = jnp.concatenate([outer_ref[core], outer_ref[1 - core]], axis=1)
+    part = dot(outer, both_downs(core, down_ref, got_ref), COLS)
     pieces_ref[...] = part.astype(BF).reshape(pieces_ref.shape)
 
 
@@ -282,9 +331,9 @@
         copies_ref[i, 2 * rows :] = tile
 
 
-def columns_of(grads_ref, at, half):
-    share = (grads_ref.shape[1] - 16) * LANES // (2 * half)
-    blocks = range(at // LANES, (at + half) // LANES)
+def columns_of(grads_ref, at, width, whole):
+    share = (grads_ref.shape[1] - 16) * LANES // whole
+    blocks = range(at // LANES, (at + width) // LANES)
     tokens = grads_ref.shape[0] * share
     parts = [grads_ref[:, i * share : (i + 1) * share].reshape(tokens, LANES) for i in blocks]
     return jnp.concatenate(parts, axis=1)
@@ -297,28 +346,29 @@
     here = half_of(core, half)
     tokens = x_ref.shape[1]
     shape = pieces_ref.shape[1:]
-    gate = columns_of(grads_ref, 0, half)
-    up = columns_of(grads_ref, half, half)
+    weights = jnp.concatenate([gate_ref[:, here], up_ref[:, here]], axis=1)
+    weights = jnp.concatenate([weights, got_ref[:feats, :]], axis=0)
+    total = dot(columns_of(grads_ref, 0, 2 * half, 2 * half), weights, COLS)
     share = tokens // grads_ref.shape[0]
     lines = [grads_ref[i, grads_ref.shape[1] - 16 :].astype(F32) for i in range(grads_ref.shape[0])]
     inner = jnp.concatenate([as_column(v[0:1] + v[1:2], share) for v in lines], axis=0)
-    part = dot(gate, gate_ref[:, here], COLS) + dot(up, up_ref[:, here], COLS)
-    part = part * mlp_ref[...] - x_ref[core].astype(F32) * inner
+    part = total[:, :feats] * mlp_ref[...] - x_ref[core].astype(F32) * inner
     pieces_ref[core] = part.astype(BF).reshape(shape)
     mlp_there, _ = got_gains(got_ref, feats + half // 4)
-    part = dot(gate, got_ref[:feats, :half], COLS) + dot(up, got_ref[:feats, half:], COLS)
-    part = part * mlp_there - x_ref[1 - core].astype(F32) * inner
+    part = total[:, feats:] * mlp_there - x_ref[1 - core].astype(F32) * inner
     pieces_ref[1 - core] = part.astype(BF).reshape(shape)
 
 
-def gate_up_weights(place_ref, scaled_ref, here_ref, there_ref, gate_ref, up_ref):
+def finish(place_ref, scaled_ref, here_ref, there_ref, normed_ref, outer_ref, gate_ref, up_ref, grad_ref):
     core = lax.rem(place_ref[0], 2)
     half = gate_ref.shape[1] // 2
     scaled = scaled_ref[...]
     for grads_ref, place in ((here_ref, core), (there_ref, 1 - core)):
         at = half_of(place, half)
-        gate_ref[:, at] = dot(scaled, columns_of(grads_ref, 0, half), ROWS).astype(BF)
-        up_ref[:, at] = dot(scaled, columns_of(grads_ref, half, half), ROWS).astype(BF)
+        both = dot(scaled, columns_of(grads_ref, 0, 2 * half, 2 * half), ROWS).astype(BF)
+        gate_ref[:, at] = both[:, :half]
+        up_ref[:, at] = both[:, half:]
+    grad_ref[...] = outer_ref[...] + normed_ref[...]
 
 
 def down_weights(place_ref, outer_ref, here_ref, there_ref, down_ref):
@@ -406,12 +456,26 @@
     mine = exchange(copies, ("z", "tensor")).reshape(chips, tokens, feats)
     other = other_core(mine)
     by_block = (chips, 2, LANES, HEAD)
-    query_grad, keep, send = call(
+    weights = (key_weight.reshape(by_block), value_weight.reshape(by_block), recip)
+    projected = call(
+        project,
+        [((tokens, HEAD), F32)] * 2 + [((tokens, LANES), F32)],
+        place, mine, *weights,
+        flops=270_000_000,
+    )
+    query_grad, send, layer_grads, scales = call(
         attend,
-        [(queries.shape[1:], BF), (mine.shape, F32), (mine.shape, BF)],
-        place, mine, other, key_weight.reshape(by_block), value_weight.reshape(by_block), recip,
-        queries[0], context_grad[0],
-        flops=3_500_000_000,
+        [
+            (queries.shape[1:], BF),
+            (mine.shape, BF),
+            ((2, tokens, HEAD), BF),
+            ((2, tokens, LANES), F32),
+        ],
+        place, other, *weights, *projected, queries[0], context_grad[0],
+        flops=1_200_000_000,
+    )
+    (keep,) = call(
+        keep_own, [(mine.shape, F32)], place, mine, *weights, layer_grads, scales, flops=270_000_000
     )
     both = (keep + other_core(send).astype(F32)).astype(BF)
     arrived = exchange(both.reshape(-1, block, feats), ("z", "tensor"))
@@ -435,15 +499,11 @@
         place, grads, hidden, mlp_gain, w_gate, w_up, got,
     )
     arrived = exchange(pieces.reshape(-1, block, feats), WIDE)
-    gate_weight_grad, up_weight_grad = call(
-        gate_up_weights,
-        [(w_gate.shape, BF), (w_up.shape, BF)],
-        place, scaled, grads, grads_there,
-    )
-    outer_grad, gate_weight_grad, up_weight_grad = lax.optimization_barrier(
-        (outer_grad, gate_weight_grad, up_weight_grad)
-    )
-    hidden_grad = outer_grad + arrived.astype(F32).sum(axis=0)
+    gate_weight_grad, up_weight_grad, hidden_grad = call(
+        finish,
+        [(w_gate.shape, BF), (w_up.shape, BF), ((block, feats), F32)],
+        place, scaled, grads, grads_there, arrived.astype(F32).sum(axis=0), outer_grad,
+    )
     return (query_grad[None], hidden_grad, gate_weight_grad, up_weight_grad, down_weight_grad)
 
 

time: 185 us -> 184 us (level)
    pallas_call x13 -> x15, Pallas kernels: 8.06 us -> 8.73 us  [call(): pl.pallas_call(body, out_shape=shapes, in_specs=in_specs, out_specs=(vmem...]
where the time goes in v5:
time: 184 us; the launch traced here: 183 us
  blocking collectives  130 us (71%)
  starting transfers between devices  31.4 us (17%)
  waiting for transfers between devices  10.5 us (6%)
  Pallas kernels  8.73 us (5%)
    all_to_all x8, blocking collectives, exchange(): return lax.all_to_all(pieces, axis, split_axis=0, concat_axis=0, tiled=True)  130 us
    all_to_all x2, starting transfers between devices, exchange(): return lax.all_to_all(pieces, axis, split_axis=0, concat_axis=0, tiled=True)  18.7 us
    ppermute x5, starting transfers between devices, other_core(): return lax.ppermute(value, 'core', [(0, 1), (1, 0)])  12.7 us
    pallas_call x15, Pallas kernels, call(): pl.pallas_call(body, out_shape=shapes, in_specs=in_specs, out_specs=(vmem...  8.73 us
    all_to_all x2, waiting for transfers between devices, exchange(): return lax.all_to_all(pieces, axis, split_axis=0, concat_axis=0, tiled=True)  6.25 us
    ppermute x5, waiting for transfers between devices, other_core(): return lax.ppermute(value, 'core', [(0, 1), (1, 0)])  4.29 us
  transfers between devices with their start and end apart: 7, of which 6 were waited for; matrix products, arithmetic and copies ran while one was open for 0% of the time, Pallas kernels for 1%

profile of v5, /device:TPU:1, one launch (start us, length us, event | category | flops | bytes accessed | tf_op | source)
XLA Modules:
  0.0 183.4 jit_solution(679718903478922584)
XLA Ops:
  0.6 0.0 copy-start.5
  0.6 0.7 copy-done.5
  1.3 0.7 shard_map.137
  2.0 10.6 %all-to-all-start = ((bf16[32,16,128]{2,1,0:T(8,128)(2,1)}), bf16[32,16,128]{2,1,0:T(8,128)(2,1)S(1)}, u32[]{:S(2)}, u32[]{:S(2)}) async-start(bf16[32,16,128]{2,1,0:T(8,128)(2,1)} %shard_map.137), calls=%async_computation | async-start | bytes 262144 | tf_op jit(solution)/shard_map/all_to_all | solution.py:23
  12.6 0.0 copy-start.7
  12.6 0.0 copy-start.8
  12.7 0.6 copy-done.7
  13.3 0.0 copy-done.8
  13.3 2.2 %collective-permute-start = (bf16[208,512]{1,0:T(8,128)(2,1)S(1)}, bf16[208,512]{1,0:T(8,128)(2,1)S(1)}, u32[]{:S(2)}, u32[]{:S(2)}) collective-permute-start(bf16[208,512]{1,0:T(8,128)(2,1)S(1)} %shard_map.138), channel_id=1, source_target_pairs={{0,32},{32,0},{1,33},{33,1},{2,34},{34,2},{3,35},{35,3},{4,36},{36... | collective-permute-start | bytes 638984 | tf_op jit(solution)/shard_map/ppermute | solution.py:27
  15.5 1.2 collective-permute-done.got_ref
  16.7 4.2 %all-to-all-done = bf16[32,16,128]{2,1,0:T(8,128)(2,1)S(1)} async-done(((bf16[32,16,128]{2,1,0:T(8,128)(2,1)}), bf16[32,16,128]{2,1,0:T(8,128)(2,1)S(1)}, u32[]{:S(2)}, u32[]{:S(2)}) %all-to-all-start) | async-done | bytes 131104 | tf_op jit(solution)/shard_map/all_to_all | solution.py:23
  20.9 0.3 shard_map.139
  21.3 18.9 %all_to_all.50.arrived_ref = bf16[8,144,128]{2,1,0:T(8,128)(2,1)S(1)} all-to-all(bf16[8,144,128]{2,1,0:T(8,128)(2,1)S(1)} %get-tuple-element.24), channel_id=1, replica_groups=mesh['z'=8,'core'=2,'tensor'=16,'dp'=2] {'z'}, dimensions={0} | all-to-all | bytes 589824 | tf_op jit(solution)/shard_map/all_to_all | solution.py:23
  40.2 0.1 shard_map.140
  40.3 0.0 copy-start.6
  40.3 11.3 %all_to_all.51.act_ref.here_ref = bf16[8,32,256]{2,1,0:T(8,128)(2,1)S(1)} all-to-all(bf16[8,32,256]{2,1,0:T(8,128)(2,1)S(1)} %get-tuple-element.25), channel_id=1, replica_groups=mesh['z'=8,'core'=2,'tensor'=16,'dp'=2] {'z'}, dimensions={0} | all-to-all | bytes 262144 | tf_op jit(solution)/shard_map/all_to_all | solution.py:23
  51.6 0.2 shard_map.141
  51.8 0.0 copy-start
  51.8 15.1 %all_to_all.52.arrived_ref = bf16[32,16,128]{2,1,0:T(8,128)(2,1)S(1)} all-to-all(bf16[32,16,128]{2,1,0:T(8,128)(2,1)S(1)} %bitcast.27), channel_id=1, replica_groups=mesh['z'=8,'core'=2,'tensor'=16,'dp'=2] {'core','tensor'}, dimensions={0} | all-to-all | bytes 262144 | tf_op jit(solution)/shard_map/all_to_all | solution.py:23
  66.9 0.1 shard_map.142
  67.0 24.6 %all_to_all.53 = bf16[128,16,128]{2,1,0:T(8,128)(2,1)S(1)} all-to-all(bf16[128,16,128]{2,1,0:T(8,128)(2,1)S(1)} %shard_map.142), channel_id=1, replica_groups=mesh['z'=8,'core'=2,'tensor'=16,'dp'=2] {'z','tensor'}, dimensions={0} | all-to-all | bytes 1048576 | tf_op jit(solution)/shard_map/all_to_all | solution.py:23
  91.6 3.9 %collective-permute-start.1 = (bf16[8,256,128]{2,1,0:T(8,128)(2,1)S(1)}, bf16[8,256,128]{2,1,0:T(8,128)(2,1)S(1)}, u32[]{:S(2)}, u32[]{:S(2)}) collective-permute-start(bf16[8,256,128]{2,1,0:T(8,128)(2,1)S(1)} %bitcast.14), channel_id=1, source_target_pairs={{0,32},{32,0},{1,33},{33,1},{2,34},{34,2},{3,35},{35,3},{4,36},{36... | collective-permute-start | bytes 1572872 | tf_op jit(solution)/shard_map/ppermute | solution.py:27
  95.5 0.0 copy-start.9
  95.5 0.0 copy-start.10
  95.5 0.4 shard_map.143
  96.0 1.0 collective-permute-done.1.other_ref
  97.0 0.0 copy-done.9
  97.0 3.2 %shard_map.144 = (bf16[1024,256]{1,0:T(8,128)(2,1)}, bf16[8,256,128]{2,1,0:T(8,128)(2,1)S(1)}, bf16[2,256,256]{2,1,0:T(8,128)(2,1)S(1)}, f32[2,256,128]{2,1,0:T(8,128)S(1)}) custom-call(s32[1]{0:T(128)} %bitcast.place_ref, bf16[8,256,128]{2,1,0:T(8,128)(2,1)S(1)} %collective-permute-done.1.other_ref, bf16[8,2,128,256]{3,2,1,0:T(8,128)(2,1)S(1)} %bitcast.18, ...), custom_call_target="tpu_custom_call" | custom-call | flops 1200000000 | bytes 5906436 | tf_op jit(solution)/shard_map/pallas_call | solution.py:391
  100.2 2.3 %collective-permute-start.2 = (bf16[8,256,128]{2,1,0:T(8,128)(2,1)S(1)}, bf16[8,256,128]{2,1,0:T(8,128)(2,1)S(1)}, u32[]{:S(2)}, u32[]{:S(2)}) collective-permute-start(bf16[8,256,128]{2,1,0:T(8,128)(2,1)S(1)} %get-tuple-element.34), channel_id=1, source_target_pairs={{0,32},{32,0},{1,33},{33,1},{2,34},{34,2},{3,35},{35,3},{4,36},{36... | collective-permute-start | bytes 1572872 | tf_op jit(solution)/shard_map/ppermute | solution.py:27
  102.5 0.5 shard_map.145
  102.9 1.0 collective-permute-done.2
  104.0 0.1 add_convert_fusion
  104.1 24.9 %all_to_all.54.arrived_ref = bf16[128,16,128]{2,1,0:T(8,128)(2,1)S(1)} all-to-all(bf16[128,16,128]{2,1,0:T(8,128)(2,1)S(1)} %bitcast.37), channel_id=1, replica_groups=mesh['z'=8,'core'=2,'tensor'=16,'dp'=2] {'z','tensor'}, dimensions={0} | all-to-all | bytes 1048576 | tf_op jit(solution)/shard_map/all_to_all | solution.py:23
  129.0 0.1 shard_map.146
  129.1 13.4 %all_to_all.55 = bf16[32,16,128]{2,1,0:T(8,128)(2,1)S(1)} all-to-all(bf16[32,16,128]{2,1,0:T(8,128)(2,1)S(1)} %get-tuple-element.35), channel_id=1, replica_groups=mesh['z'=8,'core'=2,'tensor'=16,'dp'=2] {'core','tensor'}, dimensions={0} | all-to-all | bytes 262144 | tf_op jit(solution)/shard_map/all_to_all | solution.py:23
  142.5 0.2 shard_map.147
  142.7 10.1 %all_to_all.56.arrived_ref = bf16[8,32,256]{2,1,0:T(8,128)(2,1)S(1)} all-to-all(bf16[8,32,256]{2,1,0:T(8,128)(2,1)S(1)} %shard_map.147), channel_id=1, replica_groups=mesh['z'=8,'core'=2,'tensor'=16,'dp'=2] {'z'}, dimensions={0} | all-to-all | bytes 262144 | tf_op jit(solution)/shard_map/all_to_all | solution.py:23
  152.8 0.1 shard_map.148
  153.0 12.1 %all_to_all.57.grads_ref.here_ref = bf16[8,144,128]{2,1,0:T(8,128)(2,1)S(1)} all-to-all(bf16[8,144,128]{2,1,0:T(8,128)(2,1)S(1)} %shard_map.148), channel_id=1, replica_groups=mesh['z'=8,'core'=2,'tensor'=16,'dp'=2] {'z'}, dimensions={0} | all-to-all | bytes 589824 | tf_op jit(solution)/shard_map/all_to_all | solution.py:23
  165.0 0.9 shard_map.149
  166.0 8.1 %all-to-all-start.9 = ((bf16[32,16,128]{2,1,0:T(8,128)(2,1)}), bf16[32,16,128]{2,1,0:T(8,128)(2,1)S(1)}, u32[]{:S(2)}, u32[]{:S(2)}) async-start(bf16[32,16,128]{2,1,0:T(8,128)(2,1)} %bitcast.13), calls=%async_computation.9 | async-start | bytes 262144 | tf_op jit(solution)/shard_map/all_to_all | solution.py:23
  174.1 2.1 %collective-permute-start.3 = (bf16[8,144,128]{2,1,0:T(8,128)(2,1)S(1)}, bf16[8,144,128]{2,1,0:T(8,128)(2,1)S(1)}, u32[]{:S(2)}, u32[]{:S(2)}) collective-permute-start(bf16[8,144,128]{2,1,0:T(8,128)(2,1)S(1)} %all_to_all.57.grads_ref.here_ref), channel_id=1, source_target_pairs={{0,32},{32,0},{1,33},{33,1},{2,34},{34,2},{3,35},{35,3},{4,36},{36... | collective-permute-start | bytes 884744 | tf_op jit(solution)/shard_map/ppermute | solution.py:27
  176.2 2.2 %collective-permute-start.4 = (bf16[8,32,256]{2,1,0:T(8,128)(2,1)S(1)}, bf16[8,32,256]{2,1,0:T(8,128)(2,1)S(1)}, u32[]{:S(2)}, u32[]{:S(2)}) collective-permute-start(bf16[8,32,256]{2,1,0:T(8,128)(2,1)S(1)} %all_to_all.51.act_ref.here_ref), channel_id=1, source_target_pairs={{0,32},{32,0},{1,33},{33,1},{2,34},{34,2},{3,35},{35,3},{4,36},{36... | collective-permute-start | bytes 393224 | tf_op jit(solution)/shard_map/ppermute | solution.py:27
  178.4 1.0 collective-permute-done.4.there_ref
  179.5 0.9 shard_map.151
  180.4 2.0 %all-to-all-done.9 = bf16[32,16,128]{2,1,0:T(8,128)(2,1)S(1)} async-done(((bf16[32,16,128]{2,1,0:T(8,128)(2,1)}), bf16[32,16,128]{2,1,0:T(8,128)(2,1)S(1)}, u32[]{:S(2)}, u32[]{:S(2)}) %all-to-all-start.9) | async-done | bytes 131104 | tf_op jit(solution)/shard_map/all_to_all | solution.py:23
  182.4 0.0 collective-permute-done.3.there_ref
  182.5 1.0 shard_map.150
  (13 shorter events, 0.1 us)
Async XLA Ops:
  0.6 0.7 copy-start.5
  1.3 11.3 %copy-start.4 = (bf16[512,128]{1,0:T(8,128)(2,1)S(1)}, bf16[512,128]{1,0:T(8,128)(2,1)}, u32[]{:S(2)}) copy-start(bf16[512,128]{1,0:T(8,128)(2,1)} %down_ref.5) | copy-start | bytes 393220
  2.0 10.7 %copy-start.2 = (bf16[128,512]{1,0:T(8,128)(2,1)S(1)}, bf16[128,512]{1,0:T(8,128)(2,1)}, u32[]{:S(2)}) copy-start(bf16[128,512]{1,0:T(8,128)(2,1)} %gate_ref.5) | copy-start | bytes 393220
  2.0 10.7 %copy-start.3 = (bf16[128,512]{1,0:T(8,128)(2,1)S(1)}, bf16[128,512]{1,0:T(8,128)(2,1)}, u32[]{:S(2)}) copy-start(bf16[128,512]{1,0:T(8,128)(2,1)} %up_ref.5) | copy-start | bytes 393220
  2.0 18.9 %all-to-all-start = ((bf16[32,16,128]{2,1,0:T(8,128)(2,1)}), bf16[32,16,128]{2,1,0:T(8,128)(2,1)S(1)}, u32[]{:S(2)}, u32[]{:S(2)}) async-start(bf16[32,16,128]{2,1,0:T(8,128)(2,1)} %shard_map.137), calls=%async_computation | async-start | bytes 262144 | tf_op jit(solution)/shard_map/all_to_all | solution.py:23
  12.6 0.7 copy-start.7
  12.6 0.7 copy-start.8
  13.3 3.4 %collective-permute-start = (bf16[208,512]{1,0:T(8,128)(2,1)S(1)}, bf16[208,512]{1,0:T(8,128)(2,1)S(1)}, u32[]{:S(2)}, u32[]{:S(2)}) collective-permute-start(bf16[208,512]{1,0:T(8,128)(2,1)S(1)} %shard_map.138), channel_id=1, source_target_pairs={{0,32},{32,0},{1,33},{33,1},{2,34},{34,2},{3,35},{35,3},{4,36},{36... | collective-permute-start | bytes 638984 | tf_op jit(solution)/shard_map/ppermute | solution.py:27
  40.3 26.6 %copy-start.6 = (bf16[16,128]{1,0:T(8,128)(2,1)S(1)}, bf16[16,128]{1,0:T(8,128)(2,1)}, u32[]{:S(2)}) copy-start(bf16[16,128]{1,0:T(8,128)(2,1)} %x_ref.3) | copy-start | bytes 12292
  51.6 43.9 %copy-start.1 = (bf16[1,2048,256]{2,1,0:T(8,128)(2,1)S(1)}, bf16[1,2048,256]{2,1,0:T(8,128)(2,1)}, u32[]{:S(2)}) copy-start(bf16[1,2048,256]{2,1,0:T(8,128)(2,1)} %param.17) | copy-start | bytes 3145732
  51.8 43.7 %copy-start = (bf16[1,2048,256]{2,1,0:T(8,128)(2,1)S(1)}, bf16[1,2048,256]{2,1,0:T(8,128)(2,1)}, u32[]{:S(2)}) copy-start(bf16[1,2048,256]{2,1,0:T(8,128)(2,1)} %param.16) | copy-start | bytes 3145732
  91.6 5.4 %collective-permute-start.1 = (bf16[8,256,128]{2,1,0:T(8,128)(2,1)S(1)}, bf16[8,256,128]{2,1,0:T(8,128)(2,1)S(1)}, u32[]{:S(2)}, u32[]{:S(2)}) collective-permute-start(bf16[8,256,128]{2,1,0:T(8,128)(2,1)S(1)} %bitcast.14), channel_id=1, source_target_pairs={{0,32},{32,0},{1,33},{33,1},{2,34},{34,2},{3,35},{35,3},{4,36},{36... | collective-permute-start | bytes 1572872 | tf_op jit(solution)/shard_map/ppermute | solution.py:27
  95.5 1.5 copy-start.9
  95.5 1.5 copy-start.10
  100.2 3.8 %collective-permute-start.2 = (bf16[8,256,128]{2,1,0:T(8,128)(2,1)S(1)}, bf16[8,256,128]{2,1,0:T(8,128)(2,1)S(1)}, u32[]{:S(2)}, u32[]{:S(2)}) collective-permute-start(bf16[8,256,128]{2,1,0:T(8,128)(2,1)S(1)} %get-tuple-element.34), channel_id=1, source_target_pairs={{0,32},{32,0},{1,33},{33,1},{2,34},{34,2},{3,35},{35,3},{4,36},{36... | collective-permute-start | bytes 1572872 | tf_op jit(solution)/shard_map/ppermute | solution.py:27
  166.0 16.4 %all-to-all-start.9 = ((bf16[32,16,128]{2,1,0:T(8,128)(2,1)}), bf16[32,16,128]{2,1,0:T(8,128)(2,1)S(1)}, u32[]{:S(2)}, u32[]{:S(2)}) async-start(bf16[32,16,128]{2,1,0:T(8,128)(2,1)} %bitcast.13), calls=%async_computation.9 | async-start | bytes 262144 | tf_op jit(solution)/shard_map/all_to_all | solution.py:23
  174.1 8.4 %collective-permute-start.3 = (bf16[8,144,128]{2,1,0:T(8,128)(2,1)S(1)}, bf16[8,144,128]{2,1,0:T(8,128)(2,1)S(1)}, u32[]{:S(2)}, u32[]{:S(2)}) collective-permute-start(bf16[8,144,128]{2,1,0:T(8,128)(2,1)S(1)} %all_to_all.57.grads_ref.here_ref), channel_id=1, source_target_pairs={{0,32},{32,0},{1,33},{33,1},{2,34},{34,2},{3,35},{35,3},{4,36},{36... | collective-permute-start | bytes 884744 | tf_op jit(solution)/shard_map/ppermute | solution.py:27
  176.2 3.2 %collective-permute-start.4 = (bf16[8,32,256]{2,1,0:T(8,128)(2,1)S(1)}, bf16[8,32,256]{2,1,0:T(8,128)(2,1)S(1)}, u32[]{:S(2)}, u32[]{:S(2)}) collective-permute-start(bf16[8,32,256]{2,1,0:T(8,128)(2,1)S(1)} %all_to_all.51.act_ref.here_ref), channel_id=1, source_target_pairs={{0,32},{32,0},{1,33},{33,1},{2,34},{34,2},{3,35},{35,3},{4,36},{36... | collective-permute-start | bytes 393224 | tf_op jit(solution)/shard_map/ppermute | solution.py:27

commit v6 on v5

--- a/solution.py
+++ b/solution.py
@@ -238,7 +238,7 @@
 
 
 def attend(place_ref, other_ref, wk_ref, wv_ref, recip_ref, keys_ref, values_ref, square_ref, q_ref, g_ref, *outs):
-    qg_ref, send_ref, grads_ref, scales_ref = outs
+    qg_ref, send_ref, grads_ref, scales_ref, held_ref, sems = outs
     core = lax.rem(place_ref[0], 2)
     rows = other_ref.shape[1]
     scale = HEAD ** (-0.5)
@@ -260,6 +260,7 @@
     key_grad = jnp.zeros((rows, HEAD), F32)
     value_grad = jnp.zeros((rows, HEAD), F32)
     step = 256
+    leaving = []
     for at in range(0, q_ref.shape[0], step):
         query = q_ref[at : at + step, :]
         grad = g_ref[at : at + step, :]
@@ -270,7 +271,12 @@
         dprob = dot(scaled_values, grad, COLS)
         delta = jnp.sum(probs_bf.astype(F32) * dprob, axis=0, keepdims=True)
         dscore = (probs * (dprob - delta)).astype(BF)
-        qg_ref[at : at + step, :] = dot(dscore, keys, ROWS).astype(BF)
+        part = pl.ds(at, step)
+        held_ref[part, :] = dot(dscore, keys, ROWS).astype(BF)
+        leaving.append(
+            pltpu.make_async_copy(held_ref.at[part, :], qg_ref.at[part, :], sems.at[at // step])
+        )
+        leaving[-1].start()
         key_grad += dot(dscore, query)
         value_grad += dot(probs_bf, grad)
     key_grad = key_grad.astype(BF)
@@ -286,6 +292,8 @@
     grads = (key_grad, value_grad)
     scales = (inv_out, along)
     back_to_features(other_ref, 1 - core, wk_ref, wv_ref, recip_ref, grads, scales, send_ref)
+    for copy in leaving:
+        copy.wait()
 
 
 def keep_own(place_ref, mine_ref, wk_ref, wv_ref, recip_ref, grads_ref, scales_ref, keep_ref):
@@ -381,7 +389,7 @@
         down_ref[half_of(place, half), :] = dot(act, outer, ROWS).astype(BF)
 
 
-def call(body, outs, *args, flops=0):
+def call(body, outs, *args, flops=0, first_out=None, scratch=()):
     vmem = pl.BlockSpec(memory_space=pltpu.VMEM)
     in_specs = [vmem] * len(args)
     if args[0].dtype == jnp.int32:
@@ -392,7 +400,8 @@
         body,
         out_shape=shapes,
         in_specs=in_specs,
-        out_specs=(vmem,) * len(shapes),
+        out_specs=(first_out or vmem,) + (vmem,) * (len(shapes) - 1),
+        scratch_shapes=scratch,
         compiler_params=pltpu.CompilerParams(vmem_limit_bytes=40 * 1024 * 1024),
         cost_estimate=pl.CostEstimate(flops=flops, bytes_accessed=moved, transcendentals=0),
     )(*args)
@@ -473,6 +482,8 @@
         ],
         place, other, *weights, *projected, queries[0], context_grad[0],
         flops=1_200_000_000,
+        first_out=pl.BlockSpec(memory_space=pl.ANY),
+        scratch=[pltpu.VMEM(queries.shape[1:], BF), pltpu.SemaphoreType.DMA((4,))],
     )
     (keep,) = call(
         keep_own, [(mine.shape, F32)], place, mine, *weights, layer_grads, scales, flops=270_000_000

time: 184 us -> 184 us (level)
  no operation moved by 1% of the time
where the time goes in v6:
time: 184 us; the launch traced here: 183 us
  blocking collectives  130 us (71%)
  starting transfers between devices  31.4 us (17%)
  waiting for transfers between devices  10.5 us (6%)
  Pallas kernels  8.46 us (5%)
    all_to_all x8, blocking collectives, exchange(): return lax.all_to_all(pieces, axis, split_axis=0, concat_axis=0, tiled=True)  130 us
    all_to_all x2, starting transfers between devices, exchange(): return lax.all_to_all(pieces, axis, split_axis=0, concat_axis=0, tiled=True)  18.7 us
    ppermute x5, starting transfers between devices, other_core(): return lax.ppermute(value, 'core', [(0, 1), (1, 0)])  12.7 us
    pallas_call x15, Pallas kernels, call(): pl.pallas_call(body, out_shape=shapes, in_specs=in_specs, out_specs=(firs...  8.46 us
    all_to_all x2, waiting for transfers between devices, exchange(): return lax.all_to_all(pieces, axis, split_axis=0, concat_axis=0, tiled=True)  6.25 us
    ppermute x5, waiting for transfers between devices, other_core(): return lax.ppermute(value, 'core', [(0, 1), (1, 0)])  4.28 us
  transfers between devices with their start and end apart: 7, of which 6 were waited for; matrix products, arithmetic and copies ran while one was open for 0% of the time, Pallas kernels for 1%

profile of v6, /device:TPU:1, one launch (start us, length us, event | category | flops | bytes accessed | tf_op | source)
XLA Modules:
  0.0 183.2 jit_solution(7962645751112579991)
XLA Ops:
  0.6 0.0 copy-start.5
  0.6 0.7 copy-done.5
  1.3 0.7 shard_map.137
  2.0 10.6 %all-to-all-start = ((bf16[32,16,128]{2,1,0:T(8,128)(2,1)}), bf16[32,16,128]{2,1,0:T(8,128)(2,1)S(1)}, u32[]{:S(2)}, u32[]{:S(2)}) async-start(bf16[32,16,128]{2,1,0:T(8,128)(2,1)} %shard_map.137), calls=%async_computation | async-start | bytes 262144 | tf_op jit(solution)/shard_map/all_to_all | solution.py:23
  12.6 0.0 copy-start.7
  12.6 0.0 copy-start.8
  12.7 0.6 copy-done.7
  13.3 0.0 copy-done.8
  13.3 2.2 %collective-permute-start = (bf16[208,512]{1,0:T(8,128)(2,1)S(1)}, bf16[208,512]{1,0:T(8,128)(2,1)S(1)}, u32[]{:S(2)}, u32[]{:S(2)}) collective-permute-start(bf16[208,512]{1,0:T(8,128)(2,1)S(1)} %shard_map.138), channel_id=1, source_target_pairs={{0,32},{32,0},{1,33},{33,1},{2,34},{34,2},{3,35},{35,3},{4,36},{36... | collective-permute-start | bytes 638984 | tf_op jit(solution)/shard_map/ppermute | solution.py:27
  15.5 1.2 collective-permute-done.got_ref
  16.7 4.2 %all-to-all-done = bf16[32,16,128]{2,1,0:T(8,128)(2,1)S(1)} async-done(((bf16[32,16,128]{2,1,0:T(8,128)(2,1)}), bf16[32,16,128]{2,1,0:T(8,128)(2,1)S(1)}, u32[]{:S(2)}, u32[]{:S(2)}) %all-to-all-start) | async-done | bytes 131104 | tf_op jit(solution)/shard_map/all_to_all | solution.py:23
  20.9 0.3 shard_map.139
  21.3 18.9 %all_to_all.50.arrived_ref = bf16[8,144,128]{2,1,0:T(8,128)(2,1)S(1)} all-to-all(bf16[8,144,128]{2,1,0:T(8,128)(2,1)S(1)} %get-tuple-element.24), channel_id=1, replica_groups=mesh['z'=8,'core'=2,'tensor'=16,'dp'=2] {'z'}, dimensions={0} | all-to-all | bytes 589824 | tf_op jit(solution)/shard_map/all_to_all | solution.py:23
  40.2 0.1 shard_map.140
  40.3 0.0 copy-start.6
  40.3 11.3 %all_to_all.51.act_ref.here_ref = bf16[8,32,256]{2,1,0:T(8,128)(2,1)S(1)} all-to-all(bf16[8,32,256]{2,1,0:T(8,128)(2,1)S(1)} %get-tuple-element.25), channel_id=1, replica_groups=mesh['z'=8,'core'=2,'tensor'=16,'dp'=2] {'z'}, dimensions={0} | all-to-all | bytes 262144 | tf_op jit(solution)/shard_map/all_to_all | solution.py:23
  51.6 0.2 shard_map.141
  51.8 0.0 copy-start
  51.8 15.1 %all_to_all.52.arrived_ref = bf16[32,16,128]{2,1,0:T(8,128)(2,1)S(1)} all-to-all(bf16[32,16,128]{2,1,0:T(8,128)(2,1)S(1)} %bitcast.27), channel_id=1, replica_groups=mesh['z'=8,'core'=2,'tensor'=16,'dp'=2] {'core','tensor'}, dimensions={0} | all-to-all | bytes 262144 | tf_op jit(solution)/shard_map/all_to_all | solution.py:23
  66.9 0.1 shard_map.142
  67.0 24.6 %all_to_all.53 = bf16[128,16,128]{2,1,0:T(8,128)(2,1)S(1)} all-to-all(bf16[128,16,128]{2,1,0:T(8,128)(2,1)S(1)} %shard_map.142), channel_id=1, replica_groups=mesh['z'=8,'core'=2,'tensor'=16,'dp'=2] {'z','tensor'}, dimensions={0} | all-to-all | bytes 1048576 | tf_op jit(solution)/shard_map/all_to_all | solution.py:23
  91.6 3.9 %collective-permute-start.1 = (bf16[8,256,128]{2,1,0:T(8,128)(2,1)S(1)}, bf16[8,256,128]{2,1,0:T(8,128)(2,1)S(1)}, u32[]{:S(2)}, u32[]{:S(2)}) collective-permute-start(bf16[8,256,128]{2,1,0:T(8,128)(2,1)S(1)} %bitcast.14), channel_id=1, source_target_pairs={{0,32},{32,0},{1,33},{33,1},{2,34},{34,2},{3,35},{35,3},{4,36},{36... | collective-permute-start | bytes 1572872 | tf_op jit(solution)/shard_map/ppermute | solution.py:27
  95.5 0.0 copy-start.9
  95.5 0.0 copy-start.10
  95.5 0.4 shard_map.143
  96.0 1.0 collective-permute-done.1.other_ref
  97.0 0.0 copy-done.9
  97.0 2.9 %shard_map.144 = (bf16[1024,256]{1,0:T(8,128)(2,1)}, bf16[8,256,128]{2,1,0:T(8,128)(2,1)S(1)}, bf16[2,256,256]{2,1,0:T(8,128)(2,1)S(1)}, f32[2,256,128]{2,1,0:T(8,128)S(1)}) custom-call(s32[1]{0:T(128)} %bitcast.place_ref, bf16[8,256,128]{2,1,0:T(8,128)(2,1)S(1)} %collective-permute-done.1.other_ref, bf16[8,2,128,256]{3,2,1,0:T(8,128)(2,1)S(1)} %bitcast.18, ...), custom_call_target="tpu_custom_call" | custom-call | flops 1200000000 | bytes 5906436 | tf_op jit(solution)/shard_map/pallas_call | solution.py:399
  99.9 2.3 %collective-permute-start.2 = (bf16[8,256,128]{2,1,0:T(8,128)(2,1)S(1)}, bf16[8,256,128]{2,1,0:T(8,128)(2,1)S(1)}, u32[]{:S(2)}, u32[]{:S(2)}) collective-permute-start(bf16[8,256,128]{2,1,0:T(8,128)(2,1)S(1)} %get-tuple-element.34), channel_id=1, source_target_pairs={{0,32},{32,0},{1,33},{33,1},{2,34},{34,2},{3,35},{35,3},{4,36},{36... | collective-permute-start | bytes 1572872 | tf_op jit(solution)/shard_map/ppermute | solution.py:27
  102.2 0.5 shard_map.145
  102.7 1.0 collective-permute-done.2
  103.7 0.1 add_convert_fusion
  103.9 24.9 %all_to_all.54.arrived_ref = bf16[128,16,128]{2,1,0:T(8,128)(2,1)S(1)} all-to-all(bf16[128,16,128]{2,1,0:T(8,128)(2,1)S(1)} %bitcast.37), channel_id=1, replica_groups=mesh['z'=8,'core'=2,'tensor'=16,'dp'=2] {'z','tensor'}, dimensions={0} | all-to-all | bytes 1048576 | tf_op jit(solution)/shard_map/all_to_all | solution.py:23
  128.7 0.1 shard_map.146
  128.8 13.4 %all_to_all.55 = bf16[32,16,128]{2,1,0:T(8,128)(2,1)S(1)} all-to-all(bf16[32,16,128]{2,1,0:T(8,128)(2,1)S(1)} %get-tuple-element.35), channel_id=1, replica_groups=mesh['z'=8,'core'=2,'tensor'=16,'dp'=2] {'core','tensor'}, dimensions={0} | all-to-all | bytes 262144 | tf_op jit(solution)/shard_map/all_to_all | solution.py:23
  142.2 0.2 shard_map.147
  142.4 10.1 %all_to_all.56.arrived_ref = bf16[8,32,256]{2,1,0:T(8,128)(2,1)S(1)} all-to-all(bf16[8,32,256]{2,1,0:T(8,128)(2,1)S(1)} %shard_map.147), channel_id=1, replica_groups=mesh['z'=8,'core'=2,'tensor'=16,'dp'=2] {'z'}, dimensions={0} | all-to-all | bytes 262144 | tf_op jit(solution)/shard_map/all_to_all | solution.py:23
  152.6 0.1 shard_map.148
  152.7 12.1 %all_to_all.57.grads_ref.here_ref = bf16[8,144,128]{2,1,0:T(8,128)(2,1)S(1)} all-to-all(bf16[8,144,128]{2,1,0:T(8,128)(2,1)S(1)} %shard_map.148), channel_id=1, replica_groups=mesh['z'=8,'core'=2,'tensor'=16,'dp'=2] {'z'}, dimensions={0} | all-to-all | bytes 589824 | tf_op jit(solution)/shard_map/all_to_all | solution.py:23
  164.8 0.9 shard_map.149
  165.7 8.1 %all-to-all-start.9 = ((bf16[32,16,128]{2,1,0:T(8,128)(2,1)}), bf16[32,16,128]{2,1,0:T(8,128)(2,1)S(1)}, u32[]{:S(2)}, u32[]{:S(2)}) async-start(bf16[32,16,128]{2,1,0:T(8,128)(2,1)} %bitcast.13), calls=%async_computation.9 | async-start | bytes 262144 | tf_op jit(solution)/shard_map/all_to_all | solution.py:23
  173.8 2.1 %collective-permute-start.3 = (bf16[8,144,128]{2,1,0:T(8,128)(2,1)S(1)}, bf16[8,144,128]{2,1,0:T(8,128)(2,1)S(1)}, u32[]{:S(2)}, u32[]{:S(2)}) collective-permute-start(bf16[8,144,128]{2,1,0:T(8,128)(2,1)S(1)} %all_to_all.57.grads_ref.here_ref), channel_id=1, source_target_pairs={{0,32},{32,0},{1,33},{33,1},{2,34},{34,2},{3,35},{35,3},{4,36},{36... | collective-permute-start | bytes 884744 | tf_op jit(solution)/shard_map/ppermute | solution.py:27
  176.0 2.2 %collective-permute-start.4 = (bf16[8,32,256]{2,1,0:T(8,128)(2,1)S(1)}, bf16[8,32,256]{2,1,0:T(8,128)(2,1)S(1)}, u32[]{:S(2)}, u32[]{:S(2)}) collective-permute-start(bf16[8,32,256]{2,1,0:T(8,128)(2,1)S(1)} %all_to_all.51.act_ref.here_ref), channel_id=1, source_target_pairs={{0,32},{32,0},{1,33},{33,1},{2,34},{34,2},{3,35},{35,3},{4,36},{36... | collective-permute-start | bytes 393224 | tf_op jit(solution)/shard_map/ppermute | solution.py:27
  178.2 1.0 collective-permute-done.4.there_ref
  179.2 0.9 shard_map.151
  180.2 2.0 %all-to-all-done.9 = bf16[32,16,128]{2,1,0:T(8,128)(2,1)S(1)} async-done(((bf16[32,16,128]{2,1,0:T(8,128)(2,1)}), bf16[32,16,128]{2,1,0:T(8,128)(2,1)S(1)}, u32[]{:S(2)}, u32[]{:S(2)}) %all-to-all-start.9) | async-done | bytes 131104 | tf_op jit(solution)/shard_map/all_to_all | solution.py:23
  182.2 0.0 collective-permute-done.3.there_ref
  182.2 1.0 shard_map.150
  (13 shorter events, 0.1 us)
Async XLA Ops:
  0.6 0.7 copy-start.5
  1.3 11.3 %copy-start.4 = (bf16[512,128]{1,0:T(8,128)(2,1)S(1)}, bf16[512,128]{1,0:T(8,128)(2,1)}, u32[]{:S(2)}) copy-start(bf16[512,128]{1,0:T(8,128)(2,1)} %down_ref.5) | copy-start | bytes 393220
  2.0 10.7 %copy-start.2 = (bf16[128,512]{1,0:T(8,128)(2,1)S(1)}, bf16[128,512]{1,0:T(8,128)(2,1)}, u32[]{:S(2)}) copy-start(bf16[128,512]{1,0:T(8,128)(2,1)} %gate_ref.5) | copy-start | bytes 393220
  2.0 10.7 %copy-start.3 = (bf16[128,512]{1,0:T(8,128)(2,1)S(1)}, bf16[128,512]{1,0:T(8,128)(2,1)}, u32[]{:S(2)}) copy-start(bf16[128,512]{1,0:T(8,128)(2,1)} %up_ref.5) | copy-start | bytes 393220
  2.0 18.9 %all-to-all-start = ((bf16[32,16,128]{2,1,0:T(8,128)(2,1)}), bf16[32,16,128]{2,1,0:T(8,128)(2,1)S(1)}, u32[]{:S(2)}, u32[]{:S(2)}) async-start(bf16[32,16,128]{2,1,0:T(8,128)(2,1)} %shard_map.137), calls=%async_computation | async-start | bytes 262144 | tf_op jit(solution)/shard_map/all_to_all | solution.py:23
  12.6 0.7 copy-start.7
  12.6 0.7 copy-start.8
  13.3 3.4 %collective-permute-start = (bf16[208,512]{1,0:T(8,128)(2,1)S(1)}, bf16[208,512]{1,0:T(8,128)(2,1)S(1)}, u32[]{:S(2)}, u32[]{:S(2)}) collective-permute-start(bf16[208,512]{1,0:T(8,128)(2,1)S(1)} %shard_map.138), channel_id=1, source_target_pairs={{0,32},{32,0},{1,33},{33,1},{2,34},{34,2},{3,35},{35,3},{4,36},{36... | collective-permute-start | bytes 638984 | tf_op jit(solution)/shard_map/ppermute | solution.py:27
  40.3 26.6 %copy-start.6 = (bf16[16,128]{1,0:T(8,128)(2,1)S(1)}, bf16[16,128]{1,0:T(8,128)(2,1)}, u32[]{:S(2)}) copy-start(bf16[16,128]{1,0:T(8,128)(2,1)} %x_ref.3) | copy-start | bytes 12292
  51.6 43.9 %copy-start.1 = (bf16[1,2048,256]{2,1,0:T(8,128)(2,1)S(1)}, bf16[1,2048,256]{2,1,0:T(8,128)(2,1)}, u32[]{:S(2)}) copy-start(bf16[1,2048,256]{2,1,0:T(8,128)(2,1)} %param.17) | copy-start | bytes 3145732
  51.8 43.7 %copy-start = (bf16[1,2048,256]{2,1,0:T(8,128)(2,1)S(1)}, bf16[1,2048,256]{2,1,0:T(8,128)(2,1)}, u32[]{:S(2)}) copy-start(bf16[1,2048,256]{2,1,0:T(8,128)(2,1)} %param.16) | copy-start | bytes 3145732
  91.6 5.4 %collective-permute-start.1 = (bf16[8,256,128]{2,1,0:T(8,128)(2,1)S(1)}, bf16[8,256,128]{2,1,0:T(8,128)(2,1)S(1)}, u32[]{:S(2)}, u32[]{:S(2)}) collective-permute-start(bf16[8,256,128]{2,1,0:T(8,128)(2,1)S(1)} %bitcast.14), channel_id=1, source_target_pairs={{0,32},{32,0},{1,33},{33,1},{2,34},{34,2},{3,35},{35,3},{4,36},{36... | collective-permute-start | bytes 1572872 | tf_op jit(solution)/shard_map/ppermute | solution.py:27
  95.5 1.5 copy-start.9
  95.5 1.5 copy-start.10
  99.9 3.8 %collective-permute-start.2 = (bf16[8,256,128]{2,1,0:T(8,128)(2,1)S(1)}, bf16[8,256,128]{2,1,0:T(8,128)(2,1)S(1)}, u32[]{:S(2)}, u32[]{:S(2)}) collective-permute-start(bf16[8,256,128]{2,1,0:T(8,128)(2,1)S(1)} %get-tuple-element.34), channel_id=1, source_target_pairs={{0,32},{32,0},{1,33},{33,1},{2,34},{34,2},{3,35},{35,3},{4,36},{36... | collective-permute-start | bytes 1572872 | tf_op jit(solution)/shard_map/ppermute | solution.py:27
  165.7 16.5 %all-to-all-start.9 = ((bf16[32,16,128]{2,1,0:T(8,128)(2,1)}), bf16[32,16,128]{2,1,0:T(8,128)(2,1)S(1)}, u32[]{:S(2)}, u32[]{:S(2)}) async-start(bf16[32,16,128]{2,1,0:T(8,128)(2,1)} %bitcast.13), calls=%async_computation.9 | async-start | bytes 262144 | tf_op jit(solution)/shard_map/all_to_all | solution.py:23
  173.8 8.4 %collective-permute-start.3 = (bf16[8,144,128]{2,1,0:T(8,128)(2,1)S(1)}, bf16[8,144,128]{2,1,0:T(8,128)(2,1)S(1)}, u32[]{:S(2)}, u32[]{:S(2)}) collective-permute-start(bf16[8,144,128]{2,1,0:T(8,128)(2,1)S(1)} %all_to_all.57.grads_ref.here_ref), channel_id=1, source_target_pairs={{0,32},{32,0},{1,33},{33,1},{2,34},{34,2},{3,35},{35,3},{4,36},{36... | collective-permute-start | bytes 884744 | tf_op jit(solution)/shard_map/ppermute | solution.py:27
  176.0 3.2 %collective-permute-start.4 = (bf16[8,32,256]{2,1,0:T(8,128)(2,1)S(1)}, bf16[8,32,256]{2,1,0:T(8,128)(2,1)S(1)}, u32[]{:S(2)}, u32[]{:S(2)}) collective-permute-start(bf16[8,32,256]{2,1,0:T(8,128)(2,1)S(1)} %all_to_all.51.act_ref.here_ref), channel_id=1, source_target_pairs={{0,32},{32,0},{1,33},{33,1},{2,34},{34,2},{3,35},{35,3},{4,36},{36... | collective-permute-start | bytes 393224 | tf_op jit(solution)/shard_map/ppermute | solution.py:27

commit v7 on v6

--- a/solution.py
+++ b/solution.py
@@ -371,11 +371,12 @@
     core = lax.rem(place_ref[0], 2)
     half = gate_ref.shape[1] // 2
     scaled = scaled_ref[...]
-    for grads_ref, place in ((here_ref, core), (there_ref, 1 - core)):
+    columns = [columns_of(ref, 0, 2 * half, 2 * half) for ref in (here_ref, there_ref)]
+    both = dot(scaled, jnp.concatenate(columns, axis=1), ROWS).astype(BF)
+    for i, place in enumerate((core, 1 - core)):
         at = half_of(place, half)
-        both = dot(scaled, columns_of(grads_ref, 0, 2 * half, 2 * half), ROWS).astype(BF)
-        gate_ref[:, at] = both[:, :half]
-        up_ref[:, at] = both[:, half:]
+        gate_ref[:, at] = both[:, 2 * i * half : (2 * i + 1) * half]
+        up_ref[:, at] = both[:, (2 * i + 1) * half : (2 * i + 2) * half]
     grad_ref[...] = outer_ref[...] + normed_ref[...]
 
 

time: 184 us -> 184 us (level)
  no operation moved by 1% of the time
where the time goes in v7:
time: 184 us; the launch traced here: 183 us
  blocking collectives  130 us (71%)
  starting transfers between devices  31.4 us (17%)
  waiting for transfers between devices  10.5 us (6%)
  Pallas kernels  8.46 us (5%)
    all_to_all x8, blocking collectives, exchange(): return lax.all_to_all(pieces, axis, split_axis=0, concat_axis=0, tiled=True)  130 us
    all_to_all x2, starting transfers between devices, exchange(): return lax.all_to_all(pieces, axis, split_axis=0, concat_axis=0, tiled=True)  18.7 us
    ppermute x5, starting transfers between devices, other_core(): return lax.ppermute(value, 'core', [(0, 1), (1, 0)])  12.7 us
    pallas_call x15, Pallas kernels, call(): pl.pallas_call(body, out_shape=shapes, in_specs=in_specs, out_specs=(firs...  8.46 us
    all_to_all x2, waiting for transfers between devices, exchange(): return lax.all_to_all(pieces, axis, split_axis=0, concat_axis=0, tiled=True)  6.25 us
    ppermute x5, waiting for transfers between devices, other_core(): return lax.ppermute(value, 'core', [(0, 1), (1, 0)])  4.28 us
  transfers between devices with their start and end apart: 7, of which 6 were waited for; matrix products, arithmetic and copies ran while one was open for 0% of the time, Pallas kernels for 1%

profile of v7, /device:TPU:1, one launch (start us, length us, event | category | flops | bytes accessed | tf_op | source)
XLA Modules:
  0.0 183.2 jit_solution(7962645751112579991)
XLA Ops:
  0.6 0.0 copy-start.5
  0.6 0.7 copy-done.5
  1.3 0.7 shard_map.137
  2.0 10.6 %all-to-all-start = ((bf16[32,16,128]{2,1,0:T(8,128)(2,1)}), bf16[32,16,128]{2,1,0:T(8,128)(2,1)S(1)}, u32[]{:S(2)}, u32[]{:S(2)}) async-start(bf16[32,16,128]{2,1,0:T(8,128)(2,1)} %shard_map.137), calls=%async_computation | async-start | bytes 262144 | tf_op jit(solution)/shard_map/all_to_all | solution.py:23
  12.6 0.0 copy-start.7
  12.6 0.0 copy-start.8
  12.7 0.6 copy-done.7
  13.3 0.0 copy-done.8
  13.3 2.2 %collective-permute-start = (bf16[208,512]{1,0:T(8,128)(2,1)S(1)}, bf16[208,512]{1,0:T(8,128)(2,1)S(1)}, u32[]{:S(2)}, u32[]{:S(2)}) collective-permute-start(bf16[208,512]{1,0:T(8,128)(2,1)S(1)} %shard_map.138), channel_id=1, source_target_pairs={{0,32},{32,0},{1,33},{33,1},{2,34},{34,2},{3,35},{35,3},{4,36},{36... | collective-permute-start | bytes 638984 | tf_op jit(solution)/shard_map/ppermute | solution.py:27
  15.5 1.2 collective-permute-done.got_ref
  16.7 4.2 %all-to-all-done = bf16[32,16,128]{2,1,0:T(8,128)(2,1)S(1)} async-done(((bf16[32,16,128]{2,1,0:T(8,128)(2,1)}), bf16[32,16,128]{2,1,0:T(8,128)(2,1)S(1)}, u32[]{:S(2)}, u32[]{:S(2)}) %all-to-all-start) | async-done | bytes 131104 | tf_op jit(solution)/shard_map/all_to_all | solution.py:23
  20.9 0.3 shard_map.139
  21.3 18.9 %all_to_all.50.arrived_ref = bf16[8,144,128]{2,1,0:T(8,128)(2,1)S(1)} all-to-all(bf16[8,144,128]{2,1,0:T(8,128)(2,1)S(1)} %get-tuple-element.24), channel_id=1, replica_groups=mesh['z'=8,'core'=2,'tensor'=16,'dp'=2] {'z'}, dimensions={0} | all-to-all | bytes 589824 | tf_op jit(solution)/shard_map/all_to_all | solution.py:23
  40.2 0.1 shard_map.140
  40.3 0.0 copy-start.6
  40.3 11.3 %all_to_all.51.act_ref.here_ref = bf16[8,32,256]{2,1,0:T(8,128)(2,1)S(1)} all-to-all(bf16[8,32,256]{2,1,0:T(8,128)(2,1)S(1)} %get-tuple-element.25), channel_id=1, replica_groups=mesh['z'=8,'core'=2,'tensor'=16,'dp'=2] {'z'}, dimensions={0} | all-to-all | bytes 262144 | tf_op jit(solution)/shard_map/all_to_all | solution.py:23
  51.6 0.2 shard_map.141
  51.8 0.0 copy-start
  51.8 15.1 %all_to_all.52.arrived_ref = bf16[32,16,128]{2,1,0:T(8,128)(2,1)S(1)} all-to-all(bf16[32,16,128]{2,1,0:T(8,128)(2,1)S(1)} %bitcast.27), channel_id=1, replica_groups=mesh['z'=8,'core'=2,'tensor'=16,'dp'=2] {'core','tensor'}, dimensions={0} | all-to-all | bytes 262144 | tf_op jit(solution)/shard_map/all_to_all | solution.py:23
  66.9 0.1 shard_map.142
  67.0 24.6 %all_to_all.53 = bf16[128,16,128]{2,1,0:T(8,128)(2,1)S(1)} all-to-all(bf16[128,16,128]{2,1,0:T(8,128)(2,1)S(1)} %shard_map.142), channel_id=1, replica_groups=mesh['z'=8,'core'=2,'tensor'=16,'dp'=2] {'z','tensor'}, dimensions={0} | all-to-all | bytes 1048576 | tf_op jit(solution)/shard_map/all_to_all | solution.py:23
  91.6 3.9 %collective-permute-start.1 = (bf16[8,256,128]{2,1,0:T(8,128)(2,1)S(1)}, bf16[8,256,128]{2,1,0:T(8,128)(2,1)S(1)}, u32[]{:S(2)}, u32[]{:S(2)}) collective-permute-start(bf16[8,256,128]{2,1,0:T(8,128)(2,1)S(1)} %bitcast.14), channel_id=1, source_target_pairs={{0,32},{32,0},{1,33},{33,1},{2,34},{34,2},{3,35},{35,3},{4,36},{36... | collective-permute-start | bytes 1572872 | tf_op jit(solution)/shard_map/ppermute | solution.py:27
  95.5 0.0 copy-start.9
  95.5 0.0 copy-start.10
  95.5 0.4 shard_map.143
  96.0 1.0 collective-permute-done.1.other_ref
  97.0 0.0 copy-done.9
  97.0 2.9 %shard_map.144 = (bf16[1024,256]{1,0:T(8,128)(2,1)}, bf16[8,256,128]{2,1,0:T(8,128)(2,1)S(1)}, bf16[2,256,256]{2,1,0:T(8,128)(2,1)S(1)}, f32[2,256,128]{2,1,0:T(8,128)S(1)}) custom-call(s32[1]{0:T(128)} %bitcast.place_ref, bf16[8,256,128]{2,1,0:T(8,128)(2,1)S(1)} %collective-permute-done.1.other_ref, bf16[8,2,128,256]{3,2,1,0:T(8,128)(2,1)S(1)} %bitcast.18, ...), custom_call_target="tpu_custom_call" | custom-call | flops 1200000000 | bytes 5906436 | tf_op jit(solution)/shard_map/pallas_call | solution.py:400
  99.9 2.3 %collective-permute-start.2 = (bf16[8,256,128]{2,1,0:T(8,128)(2,1)S(1)}, bf16[8,256,128]{2,1,0:T(8,128)(2,1)S(1)}, u32[]{:S(2)}, u32[]{:S(2)}) collective-permute-start(bf16[8,256,128]{2,1,0:T(8,128)(2,1)S(1)} %get-tuple-element.34), channel_id=1, source_target_pairs={{0,32},{32,0},{1,33},{33,1},{2,34},{34,2},{3,35},{35,3},{4,36},{36... | collective-permute-start | bytes 1572872 | tf_op jit(solution)/shard_map/ppermute | solution.py:27
  102.2 0.5 shard_map.145
  102.7 1.0 collective-permute-done.2
  103.7 0.1 add_convert_fusion
  103.9 24.9 %all_to_all.54.arrived_ref = bf16[128,16,128]{2,1,0:T(8,128)(2,1)S(1)} all-to-all(bf16[128,16,128]{2,1,0:T(8,128)(2,1)S(1)} %bitcast.37), channel_id=1, replica_groups=mesh['z'=8,'core'=2,'tensor'=16,'dp'=2] {'z','tensor'}, dimensions={0} | all-to-all | bytes 1048576 | tf_op jit(solution)/shard_map/all_to_all | solution.py:23
  128.7 0.1 shard_map.146
  128.8 13.4 %all_to_all.55 = bf16[32,16,128]{2,1,0:T(8,128)(2,1)S(1)} all-to-all(bf16[32,16,128]{2,1,0:T(8,128)(2,1)S(1)} %get-tuple-element.35), channel_id=1, replica_groups=mesh['z'=8,'core'=2,'tensor'=16,'dp'=2] {'core','tensor'}, dimensions={0} | all-to-all | bytes 262144 | tf_op jit(solution)/shard_map/all_to_all | solution.py:23
  142.2 0.2 shard_map.147
  142.4 10.1 %all_to_all.56.arrived_ref = bf16[8,32,256]{2,1,0:T(8,128)(2,1)S(1)} all-to-all(bf16[8,32,256]{2,1,0:T(8,128)(2,1)S(1)} %shard_map.147), channel_id=1, replica_groups=mesh['z'=8,'core'=2,'tensor'=16,'dp'=2] {'z'}, dimensions={0} | all-to-all | bytes 262144 | tf_op jit(solution)/shard_map/all_to_all | solution.py:23
  152.6 0.1 shard_map.148
  152.7 12.1 %all_to_all.57.grads_ref.here_ref = bf16[8,144,128]{2,1,0:T(8,128)(2,1)S(1)} all-to-all(bf16[8,144,128]{2,1,0:T(8,128)(2,1)S(1)} %shard_map.148), channel_id=1, replica_groups=mesh['z'=8,'core'=2,'tensor'=16,'dp'=2] {'z'}, dimensions={0} | all-to-all | bytes 589824 | tf_op jit(solution)/shard_map/all_to_all | solution.py:23
  164.8 0.9 shard_map.149
  165.7 8.1 %all-to-all-start.9 = ((bf16[32,16,128]{2,1,0:T(8,128)(2,1)}), bf16[32,16,128]{2,1,0:T(8,128)(2,1)S(1)}, u32[]{:S(2)}, u32[]{:S(2)}) async-start(bf16[32,16,128]{2,1,0:T(8,128)(2,1)} %bitcast.13), calls=%async_computation.9 | async-start | bytes 262144 | tf_op jit(solution)/shard_map/all_to_all | solution.py:23
  173.8 2.1 %collective-permute-start.3 = (bf16[8,144,128]{2,1,0:T(8,128)(2,1)S(1)}, bf16[8,144,128]{2,1,0:T(8,128)(2,1)S(1)}, u32[]{:S(2)}, u32[]{:S(2)}) collective-permute-start(bf16[8,144,128]{2,1,0:T(8,128)(2,1)S(1)} %all_to_all.57.grads_ref.here_ref), channel_id=1, source_target_pairs={{0,32},{32,0},{1,33},{33,1},{2,34},{34,2},{3,35},{35,3},{4,36},{36... | collective-permute-start | bytes 884744 | tf_op jit(solution)/shard_map/ppermute | solution.py:27
  176.0 2.2 %collective-permute-start.4 = (bf16[8,32,256]{2,1,0:T(8,128)(2,1)S(1)}, bf16[8,32,256]{2,1,0:T(8,128)(2,1)S(1)}, u32[]{:S(2)}, u32[]{:S(2)}) collective-permute-start(bf16[8,32,256]{2,1,0:T(8,128)(2,1)S(1)} %all_to_all.51.act_ref.here_ref), channel_id=1, source_target_pairs={{0,32},{32,0},{1,33},{33,1},{2,34},{34,2},{3,35},{35,3},{4,36},{36... | collective-permute-start | bytes 393224 | tf_op jit(solution)/shard_map/ppermute | solution.py:27
  178.2 1.0 collective-permute-done.4.there_ref
  179.2 0.9 shard_map.151
  180.2 2.0 %all-to-all-done.9 = bf16[32,16,128]{2,1,0:T(8,128)(2,1)S(1)} async-done(((bf16[32,16,128]{2,1,0:T(8,128)(2,1)}), bf16[32,16,128]{2,1,0:T(8,128)(2,1)S(1)}, u32[]{:S(2)}, u32[]{:S(2)}) %all-to-all-start.9) | async-done | bytes 131104 | tf_op jit(solution)/shard_map/all_to_all | solution.py:23
  182.2 0.0 collective-permute-done.3.there_ref
  182.2 1.0 shard_map.150
  (13 shorter events, 0.1 us)
Async XLA Ops:
  0.6 0.7 copy-start.5
  1.3 11.3 %copy-start.4 = (bf16[512,128]{1,0:T(8,128)(2,1)S(1)}, bf16[512,128]{1,0:T(8,128)(2,1)}, u32[]{:S(2)}) copy-start(bf16[512,128]{1,0:T(8,128)(2,1)} %down_ref.5) | copy-start | bytes 393220
  2.0 10.7 %copy-start.2 = (bf16[128,512]{1,0:T(8,128)(2,1)S(1)}, bf16[128,512]{1,0:T(8,128)(2,1)}, u32[]{:S(2)}) copy-start(bf16[128,512]{1,0:T(8,128)(2,1)} %gate_ref.5) | copy-start | bytes 393220
  2.0 10.7 %copy-start.3 = (bf16[128,512]{1,0:T(8,128)(2,1)S(1)}, bf16[128,512]{1,0:T(8,128)(2,1)}, u32[]{:S(2)}) copy-start(bf16[128,512]{1,0:T(8,128)(2,1)} %up_ref.5) | copy-start | bytes 393220
  2.0 18.9 %all-to-all-start = ((bf16[32,16,128]{2,1,0:T(8,128)(2,1)}), bf16[32,16,128]{2,1,0:T(8,128)(2,1)S(1)}, u32[]{:S(2)}, u32[]{:S(2)}) async-start(bf16[32,16,128]{2,1,0:T(8,128)(2,1)} %shard_map.137), calls=%async_computation | async-start | bytes 262144 | tf_op jit(solution)/shard_map/all_to_all | solution.py:23
  12.6 0.7 copy-start.7
  12.6 0.7 copy-start.8
  13.3 3.4 %collective-permute-start = (bf16[208,512]{1,0:T(8,128)(2,1)S(1)}, bf16[208,512]{1,0:T(8,128)(2,1)S(1)}, u32[]{:S(2)}, u32[]{:S(2)}) collective-permute-start(bf16[208,512]{1,0:T(8,128)(2,1)S(1)} %shard_map.138), channel_id=1, source_target_pairs={{0,32},{32,0},{1,33},{33,1},{2,34},{34,2},{3,35},{35,3},{4,36},{36... | collective-permute-start | bytes 638984 | tf_op jit(solution)/shard_map/ppermute | solution.py:27
  40.3 26.6 %copy-start.6 = (bf16[16,128]{1,0:T(8,128)(2,1)S(1)}, bf16[16,128]{1,0:T(8,128)(2,1)}, u32[]{:S(2)}) copy-start(bf16[16,128]{1,0:T(8,128)(2,1)} %x_ref.3) | copy-start | bytes 12292
  51.6 43.9 %copy-start.1 = (bf16[1,2048,256]{2,1,0:T(8,128)(2,1)S(1)}, bf16[1,2048,256]{2,1,0:T(8,128)(2,1)}, u32[]{:S(2)}) copy-start(bf16[1,2048,256]{2,1,0:T(8,128)(2,1)} %param.17) | copy-start | bytes 3145732
  51.8 43.7 %copy-start = (bf16[1,2048,256]{2,1,0:T(8,128)(2,1)S(1)}, bf16[1,2048,256]{2,1,0:T(8,128)(2,1)}, u32[]{:S(2)}) copy-start(bf16[1,2048,256]{2,1,0:T(8,128)(2,1)} %param.16) | copy-start | bytes 3145732
  91.6 5.4 %collective-permute-start.1 = (bf16[8,256,128]{2,1,0:T(8,128)(2,1)S(1)}, bf16[8,256,128]{2,1,0:T(8,128)(2,1)S(1)}, u32[]{:S(2)}, u32[]{:S(2)}) collective-permute-start(bf16[8,256,128]{2,1,0:T(8,128)(2,1)S(1)} %bitcast.14), channel_id=1, source_target_pairs={{0,32},{32,0},{1,33},{33,1},{2,34},{34,2},{3,35},{35,3},{4,36},{36... | collective-permute-start | bytes 1572872 | tf_op jit(solution)/shard_map/ppermute | solution.py:27
  95.5 1.5 copy-start.9
  95.5 1.5 copy-start.10
  99.9 3.8 %collective-permute-start.2 = (bf16[8,256,128]{2,1,0:T(8,128)(2,1)S(1)}, bf16[8,256,128]{2,1,0:T(8,128)(2,1)S(1)}, u32[]{:S(2)}, u32[]{:S(2)}) collective-permute-start(bf16[8,256,128]{2,1,0:T(8,128)(2,1)S(1)} %get-tuple-element.34), channel_id=1, source_target_pairs={{0,32},{32,0},{1,33},{33,1},{2,34},{34,2},{3,35},{35,3},{4,36},{36... | collective-permute-start | bytes 1572872 | tf_op jit(solution)/shard_map/ppermute | solution.py:27
  165.7 16.5 %all-to-all-start.9 = ((bf16[32,16,128]{2,1,0:T(8,128)(2,1)}), bf16[32,16,128]{2,1,0:T(8,128)(2,1)S(1)}, u32[]{:S(2)}, u32[]{:S(2)}) async-start(bf16[32,16,128]{2,1,0:T(8,128)(2,1)} %bitcast.13), calls=%async_computation.9 | async-start | bytes 262144 | tf_op jit(solution)/shard_map/all_to_all | solution.py:23
  173.8 8.4 %collective-permute-start.3 = (bf16[8,144,128]{2,1,0:T(8,128)(2,1)S(1)}, bf16[8,144,128]{2,1,0:T(8,128)(2,1)S(1)}, u32[]{:S(2)}, u32[]{:S(2)}) collective-permute-start(bf16[8,144,128]{2,1,0:T(8,128)(2,1)S(1)} %all_to_all.57.grads_ref.here_ref), channel_id=1, source_target_pairs={{0,32},{32,0},{1,33},{33,1},{2,34},{34,2},{3,35},{35,3},{4,36},{36... | collective-permute-start | bytes 884744 | tf_op jit(solution)/shard_map/ppermute | solution.py:27
  176.0 3.2 %collective-permute-start.4 = (bf16[8,32,256]{2,1,0:T(8,128)(2,1)S(1)}, bf16[8,32,256]{2,1,0:T(8,128)(2,1)S(1)}, u32[]{:S(2)}, u32[]{:S(2)}) collective-permute-start(bf16[8,32,256]{2,1,0:T(8,128)(2,1)S(1)} %all_to_all.51.act_ref.here_ref), channel_id=1, source_target_pairs={{0,32},{32,0},{1,33},{33,1},{2,34},{34,2},{3,35},{35,3},{4,36},{36... | collective-permute-start | bytes 393224 | tf_op jit(solution)/shard_map/ppermute | solution.py:27
